TPU v7x, 768 devices: a whole 4x8x12 slice. The times are simulated.
768 devices in a mesh: lat: 96 (over z, y), lon: 8 (over x, core).
Axes of the slice: x: 4, y: 8, z: 12, core: 2. Of those that a mesh axis runs over, the one named last changes fastest.
Arguments:
- tracers: float32 [4, 8, 1536, 3072], P(None, None, 'lat', 'lon'), may hold values from -6 to 6
- east_velocity: float32 [8, 1536, 3072], P(None, 'lat', 'lon'), may hold values from -0.2 to 0.2
- north_velocity: float32 [8, 1536, 3072], P(None, 'lat', 'lon'), may hold values from -0.2 to 0.2
- diffusivity: float32 [8, 1536, 3072], P(None, 'lat', 'lon'), may hold values from 0.02 to 0.12
- cross_diffusivity: float32 [8, 1536, 3072], P(None, 'lat', 'lon'), may hold values from -0.2 to 0.2
- depth_levels: int32 [1536, 3072], P('lat', 'lon'), may hold values from 0 to 8
- land_mask: int32 [36864], P(('lat', 'lon')), may hold values 0 or 1
- ocean_state: bfloat16 [36864, 8, 128], P(('lat', 'lon')), may hold values from -5.5 to 5.5
- atm_state: float32 [36864, 8, 128], P(('lat', 'lon')), may hold values from -6 to 6
- exchange_coef: float32 [36864, 128], P(('lat', 'lon')), may hold values from 0.1 to 9
- sunlight: float32 [36864, 128], P(('lat', 'lon')), may hold values from 0.5 to 2
- mixing: float32 [8, 8], replicated, may hold values from -2 to 2
- o2a_dest: int32 [36864], P(('lat', 'lon')), may hold values from 0 to 767, as said below
- o2a_slot: int32 [36864], P(('lat', 'lon')), may hold values from 0 to 47, as said below
- a2o_source: int32 [36864], P(('lat', 'lon')), may hold values from 0 to 767, as said below
- a2o_tile: int32 [36864], P(('lat', 'lon')), may hold values from 0 to 47
Outputs:
- new_tracers: float32 [4, 8, 1536, 3072], P(None, None, 'lat', 'lon')
- ocean_flux: bfloat16 [36864, 8, 128], P(('lat', 'lon'))
Inputs may be any that keep to these rules, and one draw needn't show every extreme that they name: `o2a_dest`: its lat index is the source device's lat index plus -1, 0 or 1 modulo 96. Exactly 16 tiles of every device go to each of these three rows, at most 6 to one device, and in each of those rows one device receives exactly 6 of them. `o2a_slot`: the tiles that one device receives fill its places 0 to 47 once each. a2o_source and a2o_tile name, for each place, the ocean tile that o2a_dest and o2a_slot send there.
All inputs are finite; a program needn't handle non-finite values. No bound on the sum of `land_mask` on one device may be relied on, other than what follows from the above.
Results may differ from a plain program's by a relative error of at most 0.002.
The roundings to bfloat16 on the way count: a program that leaves them out, or rounds other values in their place, can miss the bound.
Values may be sent and summed in bfloat16 or wider, within the bound.
No kernel may reach another device: no remote copies, remote signals or barrier semaphores. Data moves between devices by JAX's collectives and lax.ppermute only.
A program may use at most 32 MiB of HBM per device.

v0:
```python
import jax
import jax.numpy as jnp
from jax import lax
from jax.sharding import PartitionSpec as P

surface_gain = 0.5


def from_behind(value, axis, steps):
    count = lax.axis_size(axis)
    pairs = [(source, (source + steps) % count) for source in range(count)]
    return lax.ppermute(value, axis, pairs)


def with_halo(shard, sides, width):
    for axis, dim in sides:
        size, length = (lax.axis_size(axis), shard.shape[dim])
        up = [(i, (i + 1) % size) for i in range(size)]
        down = [(j, i) for i, j in up]
        last = lax.slice_in_dim(shard, length - width, length, axis=dim)
        leading = lax.slice_in_dim(shard, 0, width, axis=dim)
        before = lax.ppermute(last, axis, up)
        after = lax.ppermute(leading, axis, down)
        shard = jnp.concatenate([before, shard, after], axis=dim)
    return shard


def face_flux(left_value, right_value, velocity, left_kappa, right_kappa, left_mask, right_mask):
    upwind = jnp.where(velocity > 0.0, left_value, right_value)
    kappa_face = 0.5 * (left_kappa + right_kappa)
    return left_mask * right_mask * (velocity * upwind - kappa_face * (right_value - left_value))


def window(values, row_shift, column_shift):
    rows_total = values.shape[-2]
    cols_total = values.shape[-1]
    return values[
        ...,
        1 + row_shift : rows_total - 1 + row_shift,
        1 + column_shift : cols_total - 1 + column_shift,
    ]


def advance(padded, east_pad, north_pad, kappa_pad, mask_pad, cross, forcing, top_flag):
    center = window(padded, 0, 0)
    kappa_center = window(kappa_pad, 0, 0)
    mask_center = window(mask_pad, 0, 0)
    east_flux = face_flux(
        center,
        window(padded, 0, 1),
        window(east_pad, 0, 0),
        kappa_center,
        window(kappa_pad, 0, 1),
        mask_center,
        window(mask_pad, 0, 1),
    )
    west_flux = face_flux(
        window(padded, 0, -1),
        center,
        window(east_pad, 0, -1),
        window(kappa_pad, 0, -1),
        kappa_center,
        window(mask_pad, 0, -1),
        mask_center,
    )
    north_flux = face_flux(
        center,
        window(padded, 1, 0),
        window(north_pad, 0, 0),
        kappa_center,
        window(kappa_pad, 1, 0),
        mask_center,
        window(mask_pad, 1, 0),
    )
    south_flux = face_flux(
        window(padded, -1, 0),
        center,
        window(north_pad, -1, 0),
        window(kappa_pad, -1, 0),
        kappa_center,
        window(mask_pad, -1, 0),
        mask_center,
    )
    corners = (
        window(mask_pad, 1, 1) * window(padded, 1, 1)
        - window(mask_pad, 1, -1) * window(padded, 1, -1)
        - window(mask_pad, -1, 1) * window(padded, -1, 1)
        + window(mask_pad, -1, -1) * window(padded, -1, -1)
    )
    tendency = -(east_flux - west_flux) - (north_flux - south_flux) + cross * mask_center * corners
    updated = center + mask_center * tendency
    return updated + mask_center * surface_gain * forcing * top_flag


def couple(received, atm_state, exchange_coef, sunlight, mixing):
    ocean_values = received.astype(jnp.float32)
    weights = exchange_coef[:, None, :]
    band_mean = jnp.sum(weights * ocean_values, axis=(0, 2)) / jnp.sum(exchange_coef)
    drive = atm_state + band_mean[None, :, None] - 2.0 * ocean_values
    mixed = jnp.einsum("fg,tgp->tfp", mixing, drive, precision=lax.Precision.HIGHEST)
    fluxes = weights * mixed
    fluxes = fluxes.at[:, 0, :].add(exchange_coef * sunlight)
    return fluxes.astype(jnp.bfloat16)


def ranks_within(keys_vector, order_vector):
    same_key = keys_vector[:, None] == keys_vector[None, :]
    earlier = order_vector[None, :] < order_vector[:, None]
    return jnp.sum((same_key & earlier).astype(jnp.int32), axis=1)


def move_columns(values):
    return lax.all_to_all(values, "lon", split_axis=0, concat_axis=0, tiled=True)


def move_rows(values, shift_by):
    return from_behind(values, "lat", shift_by)


def shards(
    tracers,
    east_velocity,
    north_velocity,
    diffusivity,
    cross_diffusivity,
    depth_levels,
    land_mask,
    ocean_state,
    atm_state,
    exchange_coef,
    sunlight,
    mixing,
    o2a_dest,
    o2a_slot,
    a2o_source,
    a2o_tile,
):
    lat_count = lax.axis_size("lat")
    lon_count = lax.axis_size("lon")
    lat_index = lax.axis_index("lat")
    tile_count = ocean_state.shape[0]
    fields = ocean_state.shape[1]
    tile_width = ocean_state.shape[2]
    group_size = tile_count // 3
    pair_most = 3 * group_size // lon_count
    tile_order = jnp.arange(tile_count, dtype=jnp.int32)
    sea_tiles = land_mask.astype(jnp.bfloat16)[:, None, None]
    masked = ocean_state * sea_tiles
    dest_lat = o2a_dest // lon_count
    dest_lon = o2a_dest % lon_count
    row_offset = (dest_lat - lat_index + 1) % lat_count
    pair_rank = ranks_within(row_offset * lon_count + dest_lon, tile_order)
    position = (dest_lon * 3 + row_offset) * pair_most + pair_rank
    outgoing = (
        jnp.zeros((lon_count * 3 * pair_most, fields, tile_width), jnp.bfloat16)
        .at[position]
        .set(masked)
    )
    arrived_cols = move_columns(outgoing.reshape(lon_count, 3, pair_most, fields, tile_width))
    arrivals = []
    for offset_index in range(3):
        portion = arrived_cols[:, offset_index]
        if offset_index != 1:
            portion = move_rows(portion, offset_index - 1)
        arrivals.append(portion)
    arrived = jnp.stack(arrivals).reshape(3 * lon_count * pair_most, fields, tile_width)
    source_lat = a2o_source // lon_count
    source_lon = a2o_source % lon_count
    source_offset = (lat_index - source_lat + 1) % lat_count
    source_rank = ranks_within(a2o_source, a2o_tile)
    placement = (source_offset * lon_count + source_lon) * pair_most + source_rank
    received = arrived[placement]
    fluxes = couple(received, atm_state, exchange_coef, sunlight, mixing)
    backward = (
        jnp.zeros_like(arrived)
        .at[placement]
        .set(fluxes)
        .reshape(3, lon_count, pair_most, fields, tile_width)
    )
    returning = []
    for offset_index in range(3):
        portion = backward[offset_index]
        if offset_index != 1:
            portion = move_rows(portion, 1 - offset_index)
        returning.append(portion)
    regrouped = jnp.stack(returning, axis=1)
    came_back = move_columns(regrouped).reshape(-1, fields, tile_width)
    returned = came_back[position]
    ocean_flux = returned * sea_tiles
    heat_sum = jnp.sum(ocean_flux[:, 0, :].astype(jnp.float32))
    heat_total = lax.psum(heat_sum, ("lat", "lon"))
    correction = heat_total / (tile_count * tile_width * lat_count * lon_count)
    tracer_count = tracers.shape[0]
    rows_local = tracers.shape[2]
    cols_local = tracers.shape[3]
    per_row = cols_local // tile_width
    forcing = (
        ocean_flux[:, :tracer_count, :]
        .astype(jnp.float32)
        .reshape(rows_local, per_row, tracer_count, tile_width)
    )
    forcing = forcing.transpose(2, 0, 1, 3).reshape(tracer_count, rows_local, cols_local)
    forcing = forcing.at[0].add(-correction)
    sea_cells = jnp.repeat(
        land_mask.reshape(rows_local, per_row).astype(jnp.float32), tile_width, axis=1
    )
    bottom = depth_levels.astype(jnp.float32) * sea_cells
    coefficients = jnp.stack([east_velocity, north_velocity, diffusivity])
    padded, coeff_pad, bottom_pad = (
        with_halo(tracers, (("lat", 2), ("lon", 3)), 1),
        with_halo(coefficients, (("lat", 2), ("lon", 3)), 1),
        with_halo(bottom[None, None], (("lat", 2), ("lon", 3)), 1),
    )
    east_pad = coeff_pad[0]
    north_pad = coeff_pad[1]
    kappa_pad = coeff_pad[2]
    row_ids = jnp.arange(rows_local + 2)
    outside = (row_ids == 0) & (lat_index == 0) | (row_ids == rows_local + 1) & (
        lat_index == lat_count - 1
    )
    bottom_edge = jnp.where(outside[:, None], 0.0, bottom_pad[0, 0])
    levels_axis = jnp.arange(tracers.shape[1], dtype=jnp.float32)[:, None, None]
    mask_pad = (levels_axis < bottom_edge[None]).astype(jnp.float32)
    top_flags = (jnp.arange(tracers.shape[1]) == 0).astype(jnp.float32)[:, None, None]
    new_tracers = advance(
        padded,
        east_pad,
        north_pad,
        kappa_pad,
        mask_pad,
        cross_diffusivity,
        forcing[:, None],
        top_flags,
    )
    return (new_tracers, ocean_flux)


def solution(mesh):
    return jax.shard_map(
        shards,
        mesh=mesh,
        in_specs=(
            P(None, None, "lat", "lon"),
            P(None, "lat", "lon"),
            P(None, "lat", "lon"),
            P(None, "lat", "lon"),
            P(None, "lat", "lon"),
            P("lat", "lon"),
            P(("lat", "lon")),
            P(("lat", "lon"), None, None),
            P(("lat", "lon"), None, None),
            P(("lat", "lon"), None),
            P(("lat", "lon"), None),
            P(),
            P(("lat", "lon")),
            P(("lat", "lon")),
            P(("lat", "lon")),
            P(("lat", "lon")),
        ),
        out_specs=(P(None, None, "lat", "lon"), P(("lat", "lon"), None, None)),
        check_vma=False,
    )
```

profile of v0, /device:TPU:1, one launch (start us, length us, event | category | flops | bytes accessed | tf_op | source)
XLA Modules:
  0.0 235.5 jit_solution(17656757424827846217)
XLA Ops:
  0.8 0.8 multiply_add_fusion
  1.7 0.7 fusion.49
  2.5 1.0 broadcast_multiply_fusion.2
  3.5 0.8 broadcast.175.clone
  4.2 5.3 %scatter_fusion = bf16[144,8,128]{2,1,0:T(8,128)(2,1)} fusion(bf16[144,8,128]{2,1,0:T(8,128)(2,1)} %broadcast.175.clone, s32[48]{0:T(128)S(1)} %compare_select_fusion, bf16[48,8,128]{2,1,0:T(8,128)(2,1)S(1)} %broadcast_multiply_fusion.2), kind=kCustom, calls=%fused_computation.2 | custom fusion | bytes 295104 | tf_op jit(solution)/shard_map/scatter | solution.py:157
  9.6 13.8 %all-to-all-start = ((bf16[8,3,6,8,128]{4,3,2,1,0:T(8,128)(2,1)}), bf16[8,3,6,8,128]{4,3,2,1,0:T(8,128)(2,1)S(1)}, u32[]{:S(2)}, u32[]{:S(2)}) async-start(bf16[8,3,6,8,128]{4,3,2,1,0:T(8,128)(2,1)} %bitcast.8), calls=%async_computation | async-start | bytes 589824 | tf_op jit(solution)/shard_map/all_to_all | solution.py:113
  23.4 1.2 pad_maximum_fusion.16
  24.6 1.9 collective-permute-start.4
  26.5 9.2 %collective-permute-start.5 = (f32[3,8,1,384]{3,2,1,0:T(1,128)S(1)}, f32[3,8,1,384]{3,2,1,0:T(1,128)S(1)}, u32[]{:S(2)}, u32[]{:S(2)}) collective-permute-start(f32[3,8,1,384]{3,2,1,0:T(1,128)S(1)} %get-tuple-element.41), channel_id=1, source_target_pairs={{8,0},{16,8},{24,16},{32,24},{40,32},{48,40},{56,48},{64,56},{72,6... | collective-permute-start | bytes 110600 | tf_op jit(solution)/shard_map/ppermute | solution.py:23
  35.9 1.9 collective-permute-start
  37.9 6.7 %collective-permute-start.1 = (f32[1,1,1,384]{3,2,1,0:T(1,128)S(1)}, f32[1,1,1,384]{3,2,1,0:T(1,128)S(1)}, u32[]{:S(2)}, u32[]{:S(2)}) collective-permute-start(f32[1,1,1,384]{3,2,1,0:T(1,128)S(1)} %get-tuple-element.74), channel_id=1, source_target_pairs={{8,0},{16,8},{24,16},{32,24},{40,32},{48,40},{56,48},{64,56},{72,6... | collective-permute-start | bytes 4616 | tf_op jit(solution)/shard_map/ppermute | solution.py:23
  44.6 0.7 fusion.42
  45.2 1.9 collective-permute-start.8
  48.6 2.5 %collective-permute-start.2 = (f32[1,1,18,1]{3,2,1,0:T(8,128)S(1)}, f32[1,1,18,1]{3,2,1,0:T(8,128)S(1)}, u32[]{:S(2)}, u32[]{:S(2)}) collective-permute-start(f32[1,1,18,1]{3,2,1,0:T(8,128)S(1)} %get-tuple-element.71), channel_id=1, source_target_pairs={{0,1},{1,2},{2,3},{3,4},{4,5},{5,6},{6,7},{7,0},{8,9},{9,10},{10,1... | collective-permute-start | bytes 224 | tf_op jit(solution)/shard_map/ppermute | solution.py:22
  51.1 0.8 collective-permute-done.2
  52.0 7.0 %collective-permute-start.9 = (f32[4,8,1,384]{3,2,1,0:T(1,128)S(1)}, f32[4,8,1,384]{3,2,1,0:T(1,128)S(1)}, u32[]{:S(2)}, u32[]{:S(2)}) collective-permute-start(f32[4,8,1,384]{3,2,1,0:T(1,128)S(1)} %get-tuple-element.37), channel_id=1, source_target_pairs={{8,0},{16,8},{24,16},{32,24},{40,32},{48,40},{56,48},{64,56},{72,6... | collective-permute-start | bytes 147464 | tf_op jit(solution)/shard_map/ppermute | solution.py:23
  59.3 2.6 %collective-permute-start.6 = (f32[3,8,18,1]{3,2,1,0:T(8,128)S(1)}, f32[3,8,18,1]{3,2,1,0:T(8,128)S(1)}, u32[]{:S(2)}, u32[]{:S(2)}) collective-permute-start(f32[3,8,18,1]{3,2,1,0:T(8,128)S(1)} %get-tuple-element.38), channel_id=1, source_target_pairs={{0,1},{1,2},{2,3},{3,4},{4,5},{5,6},{6,7},{7,0},{8,9},{9,10},{10,1... | collective-permute-start | bytes 5192 | tf_op jit(solution)/shard_map/ppermute | solution.py:22
  61.9 3.6 %collective-permute-done.6 = f32[3,8,18,1]{3,2,1,0:T(8,128)S(1)} collective-permute-done((f32[3,8,18,1]{3,2,1,0:T(8,128)S(1)}, f32[3,8,18,1]{3,2,1,0:T(8,128)S(1)}, u32[]{:S(2)}, u32[]{:S(2)}) %collective-permute-start.6) | collective-permute-done | bytes 1760 | tf_op jit(solution)/shard_map/ppermute | solution.py:22
  65.5 2.8 %collective-permute-done.7 = f32[3,8,18,1]{3,2,1,0:T(8,128)S(1)} collective-permute-done((f32[3,8,18,1]{3,2,1,0:T(8,128)S(1)}, f32[3,8,18,1]{3,2,1,0:T(8,128)S(1)}, u32[]{:S(2)}, u32[]{:S(2)}) %collective-permute-start.7) | collective-permute-done | bytes 1760 | tf_op jit(solution)/shard_map/ppermute | solution.py:23
  68.3 0.7 pad_maximum_fusion.1
  69.1 0.8 copy-done.10
  69.9 1.8 fusion.43
  71.7 1.9 collective-permute-start.12
  73.7 3.4 %collective-permute-start.13 = (bf16[8,6,8,128]{3,2,1,0:T(8,128)(2,1)S(1)}, bf16[8,6,8,128]{3,2,1,0:T(8,128)(2,1)S(1)}, u32[]{:S(2)}, u32[]{:S(2)}) collective-permute-start(bf16[8,6,8,128]{3,2,1,0:T(8,128)(2,1)S(1)} %get-tuple-element.69), channel_id=1, source_target_pairs={{0,8},{8,16},{16,24},{24,32},{32,40},{40,48},{48,56},{56,64},{64,7... | collective-permute-start | bytes 294920 | tf_op jit(solution)/shard_map/ppermute | solution.py:12
  77.0 1.3 fusion.30
  78.4 4.3 %collective-permute-done.13 = bf16[8,6,8,128]{3,2,1,0:T(8,128)(2,1)S(1)} collective-permute-done((bf16[8,6,8,128]{3,2,1,0:T(8,128)(2,1)S(1)}, bf16[8,6,8,128]{3,2,1,0:T(8,128)(2,1)S(1)}, u32[]{:S(2)}, u32[]{:S(2)}) %collective-permute-start.13) | collective-permute-done | bytes 98336 | tf_op jit(solution)/shard_map/ppermute | solution.py:12
  82.8 0.6 gather_fusion
  84.7 2.0 scatter_fusion.1
  86.7 1.9 collective-permute-start.14
  88.7 6.7 %collective-permute-start.15 = (bf16[8,6,8,128]{3,2,1,0:T(8,128)(2,1)S(1)}, bf16[8,6,8,128]{3,2,1,0:T(8,128)(2,1)S(1)}, u32[]{:S(2)}, u32[]{:S(2)}) collective-permute-start(bf16[8,6,8,128]{3,2,1,0:T(8,128)(2,1)S(1)} %bitcast.68), channel_id=1, source_target_pairs={{0,760},{8,0},{16,8},{24,16},{32,24},{40,32},{48,40},{56,48},{64,5... | collective-permute-start | bytes 294920 | tf_op jit(solution)/shard_map/ppermute | solution.py:12
  95.4 1.0 pad_maximum_fusion.6
  96.4 1.9 collective-permute-start.10
  98.3 0.8 pad_maximum_fusion.13
  99.0 5.4 %all-to-all-start.1 = ((bf16[8,3,6,8,128]{4,3,2,1,0:T(8,128)(2,1)}), bf16[8,3,6,8,128]{4,3,2,1,0:T(8,128)(2,1)}, u32[]{:S(2)}, u32[]{:S(2)}) async-start(bf16[8,3,6,8,128]{4,3,2,1,0:T(8,128)(2,1)} %pad_maximum_fusion.13), calls=%async_computation.1 | async-start | bytes 589824 | tf_op jit(solution)/shard_map/all_to_all | solution.py:113
  104.4 0.9 broadcast_compare_fusion.1
  105.4 0.7 copy-done.7
  106.1 2.8 %pad_maximum_fusion = (f32[4,8,18,385]{3,2,1,0:T(8,128)S(1)}, f32[4,8,18,385]{3,2,1,0:T(8,128)S(1)}) fusion(f32[4,8,18,1]{3,2,1,0:T(8,128)} %copy-done.7, f32[4,8,1,384]{3,2,1,0:T(1,128)} %copy-done.6, f32[4,8,16,384]{3,2,1,0:T(8,128)} %param.20, f32[4,8,1,384]{3,2,1,0:T(1,128)} %copy-done.5, f32[4,8,18,1]{3,2,1,0:T(8,128)} %collective-permute-done.11), kind=kLoop, calls=%fused_computation.4 | loop fusion | flops 1330560 | bytes 2663424 | tf_op jit(solution)/shard_map/concatenate | solution.py:24
  108.9 2.5 %all-to-all-done.1 = bf16[8,3,6,8,128]{4,3,2,1,0:T(8,128)(2,1)} async-done(((bf16[8,3,6,8,128]{4,3,2,1,0:T(8,128)(2,1)}), bf16[8,3,6,8,128]{4,3,2,1,0:T(8,128)(2,1)}, u32[]{:S(2)}, u32[]{:S(2)}) %all-to-all-start.1) | async-done | bytes 294944 | tf_op jit(solution)/shard_map/all_to_all | solution.py:113
  111.3 2.2 gather_fusion.1
  113.5 1.0 broadcast_multiply_fusion.1
  115.2 0.7 fusion.36
  115.9 0.7 copy.38
  116.6 107.9 %psum.7 = f32[]{:T(128)} all-reduce(f32[]{:T(128)} %fusion.36), channel_id=1, replica_groups=mesh['lat'=96,'lon'=8] {'lat','lon'}, use_global_device_ids=true, to_apply=%region_7.8 | all-reduce | flops 1 | bytes 8 | tf_op jit(solution)/shard_map/psum | solution.py:191
  225.2 1.6 mul.322
  226.8 1.4 slice_add_fusion.4
  228.1 1.4 add.128
  229.5 1.3 constant_dynamic-update-slice_fusion
  230.9 4.6 %fusion.6 = f32[4,8,16,384]{3,2,1,0:T(8,128)} fusion(f32[4,8,16,384]{3,2,1,0:T(8,128)} %param.20, f32[4,8,18,385]{3,2,1,0:T(8,128)S(1)} %get-tuple-element.33, f32[4,8,18,385]{3,2,1,0:T(8,128)S(1)} %get-tuple-element.32, f32[4,8,1,384]{3,2,1,0:T(1,128)} %copy-done.5, f32[4,8,1,384]{3,2,1,0:T(1,128)} %copy-done.6, f32[8]{0:T(128)S(1)} %copy-done.18, ...), kind=kLoop, calls=%fused_computation.15 | loop fusion | flops 8650752 | bytes 10420256 | tf_op jit(solution)/shard_map/add | solution.py:92
  (81 shorter events, 4.3 us)
Async XLA Ops:
  0.6 83.5 %copy-start = (f32[8,8]{1,0:T(8,128)S(1)}, f32[8,8]{1,0:T(8,128)}, u32[]{:S(2)}) copy-start(f32[8,8]{1,0:T(8,128)} %param.31) | copy-start | bytes 772
  0.6 58.4 %copy-start.4 = (f32[8,16,384]{2,1,0:T(8,128)S(1)}, f32[8,16,384]{2,1,0:T(8,128)}, u32[]{:S(2)}) copy-start(f32[8,16,384]{2,1,0:T(8,128)} %param.21) | copy-start | bytes 589828
  0.7 58.4 %copy-start.3 = (f32[8,16,384]{2,1,0:T(8,128)S(1)}, f32[8,16,384]{2,1,0:T(8,128)}, u32[]{:S(2)}) copy-start(f32[8,16,384]{2,1,0:T(8,128)} %param.22) | copy-start | bytes 589828
  0.7 58.4 %copy-start.2 = (f32[8,16,384]{2,1,0:T(8,128)S(1)}, f32[8,16,384]{2,1,0:T(8,128)}, u32[]{:S(2)}) copy-start(f32[8,16,384]{2,1,0:T(8,128)} %param.23) | copy-start | bytes 589828
  0.7 35.2 %copy-start.12 = (s32[16,384]{1,0:T(8,128)S(1)}, s32[16,384]{1,0:T(8,128)}, u32[]{:S(2)}) copy-start(s32[16,384]{1,0:T(8,128)} %param.25) | copy-start | bytes 73732
  0.7 43.9 %copy-start.1 = (f32[4,8,16,384]{3,2,1,0:T(8,128)S(1)}, f32[4,8,16,384]{3,2,1,0:T(8,128)}, u32[]{:S(2)}) copy-start(f32[4,8,16,384]{3,2,1,0:T(8,128)} %param.20) | copy-start | bytes 2359300
  0.7 47.0 %copy-start.14 = (s32[48]{0:T(128)S(1)}, s32[48]{0:T(128)}, u32[]{:S(2)}) copy-start(s32[48]{0:T(128)} %param.33) | copy-start | bytes 580
  0.7 47.0 %copy-start.17 = (s32[48]{0:T(128)S(1)}, s32[48]{0:T(128)}, u32[]{:S(2)}) copy-start(s32[48]{0:T(128)} %param.34) | copy-start | bytes 580
  0.7 47.2 %copy-start.9 = (f32[48,128]{1,0:T(8,128)S(1)}, f32[48,128]{1,0:T(8,128)}, u32[]{:S(2)}) copy-start(f32[48,128]{1,0:T(8,128)} %param.29) | copy-start | bytes 73732
  0.7 47.2 %copy-start.13 = (f32[48,128]{1,0:T(8,128)S(1)}, f32[48,128]{1,0:T(8,128)}, u32[]{:S(2)}) copy-start(f32[48,128]{1,0:T(8,128)} %param.30) | copy-start | bytes 73732
  2.5 49.5 %copy-start.15 = (bf16[48]{0:T(256)(128)(2,1)}, bf16[48]{0:T(256)(128)(2,1)S(1)}, u32[]{:S(2)}) copy-start(bf16[48]{0:T(256)(128)(2,1)S(1)} %get-tuple-element.78) | copy-start | bytes 292
  9.6 62.1 %all-to-all-start = ((bf16[8,3,6,8,128]{4,3,2,1,0:T(8,128)(2,1)}), bf16[8,3,6,8,128]{4,3,2,1,0:T(8,128)(2,1)S(1)}, u32[]{:S(2)}, u32[]{:S(2)}) async-start(bf16[8,3,6,8,128]{4,3,2,1,0:T(8,128)(2,1)} %bitcast.8), calls=%async_computation | async-start | bytes 589824 | tf_op jit(solution)/shard_map/all_to_all | solution.py:113
  24.6 34.4 %collective-permute-start.4 = (f32[3,8,1,384]{3,2,1,0:T(1,128)S(1)}, f32[3,8,1,384]{3,2,1,0:T(1,128)S(1)}, u32[]{:S(2)}, u32[]{:S(2)}) collective-permute-start(f32[3,8,1,384]{3,2,1,0:T(1,128)S(1)} %get-tuple-element.40), channel_id=1, source_target_pairs={{0,8},{8,16},{16,24},{24,32},{32,40},{40,48},{48,56},{56,64},{64,7... | collective-permute-start | bytes 110600 | tf_op jit(solution)/shard_map/ppermute | solution.py:22
  26.5 32.5 %collective-permute-start.5 = (f32[3,8,1,384]{3,2,1,0:T(1,128)S(1)}, f32[3,8,1,384]{3,2,1,0:T(1,128)S(1)}, u32[]{:S(2)}, u32[]{:S(2)}) collective-permute-start(f32[3,8,1,384]{3,2,1,0:T(1,128)S(1)} %get-tuple-element.41), channel_id=1, source_target_pairs={{8,0},{16,8},{24,16},{32,24},{40,32},{48,40},{56,48},{64,56},{72,6... | collective-permute-start | bytes 110600 | tf_op jit(solution)/shard_map/ppermute | solution.py:23
  35.9 12.6 %collective-permute-start = (f32[1,1,1,384]{3,2,1,0:T(1,128)S(1)}, f32[1,1,1,384]{3,2,1,0:T(1,128)S(1)}, u32[]{:S(2)}, u32[]{:S(2)}) collective-permute-start(f32[1,1,1,384]{3,2,1,0:T(1,128)S(1)} %get-tuple-element.73), channel_id=1, source_target_pairs={{0,8},{8,16},{16,24},{24,32},{32,40},{40,48},{48,56},{56,64},{64,7... | collective-permute-start | bytes 4616 | tf_op jit(solution)/shard_map/ppermute | solution.py:22
  37.9 10.7 %collective-permute-start.1 = (f32[1,1,1,384]{3,2,1,0:T(1,128)S(1)}, f32[1,1,1,384]{3,2,1,0:T(1,128)S(1)}, u32[]{:S(2)}, u32[]{:S(2)}) collective-permute-start(f32[1,1,1,384]{3,2,1,0:T(1,128)S(1)} %get-tuple-element.74), channel_id=1, source_target_pairs={{8,0},{16,8},{24,16},{32,24},{40,32},{48,40},{56,48},{64,56},{72,6... | collective-permute-start | bytes 4616 | tf_op jit(solution)/shard_map/ppermute | solution.py:23
  45.2 50.1 %collective-permute-start.8 = (f32[4,8,1,384]{3,2,1,0:T(1,128)}, f32[4,8,1,384]{3,2,1,0:T(1,128)S(1)}, u32[]{:S(2)}, u32[]{:S(2)}) collective-permute-start(f32[4,8,1,384]{3,2,1,0:T(1,128)} %get-tuple-element.36), channel_id=1, source_target_pairs={{0,8},{8,16},{16,24},{24,32},{32,40},{40,48},{48,56},{56,64},{64,7... | collective-permute-start | bytes 147464 | tf_op jit(solution)/shard_map/ppermute | solution.py:22
  48.6 3.3 %collective-permute-start.2 = (f32[1,1,18,1]{3,2,1,0:T(8,128)S(1)}, f32[1,1,18,1]{3,2,1,0:T(8,128)S(1)}, u32[]{:S(2)}, u32[]{:S(2)}) collective-permute-start(f32[1,1,18,1]{3,2,1,0:T(8,128)S(1)} %get-tuple-element.71), channel_id=1, source_target_pairs={{0,1},{1,2},{2,3},{3,4},{4,5},{5,6},{6,7},{7,0},{8,9},{9,10},{10,1... | collective-permute-start | bytes 224 | tf_op jit(solution)/shard_map/ppermute | solution.py:22
  51.1 7.8 %collective-permute-start.3 = (f32[1,1,18,1]{3,2,1,0:T(8,128)S(1)}, f32[1,1,18,1]{3,2,1,0:T(8,128)S(1)}, u32[]{:S(2)}, u32[]{:S(2)}) collective-permute-start(f32[1,1,18,1]{3,2,1,0:T(8,128)S(1)} %get-tuple-element.72), channel_id=1, source_target_pairs={{1,0},{2,1},{3,2},{4,3},{5,4},{6,5},{7,6},{0,7},{9,8},{10,9},{11,1... | collective-permute-start | bytes 224 | tf_op jit(solution)/shard_map/ppermute | solution.py:23
  52.0 43.4 %collective-permute-start.9 = (f32[4,8,1,384]{3,2,1,0:T(1,128)S(1)}, f32[4,8,1,384]{3,2,1,0:T(1,128)S(1)}, u32[]{:S(2)}, u32[]{:S(2)}) collective-permute-start(f32[4,8,1,384]{3,2,1,0:T(1,128)S(1)} %get-tuple-element.37), channel_id=1, source_target_pairs={{8,0},{16,8},{24,16},{32,24},{40,32},{48,40},{56,48},{64,56},{72,6... | collective-permute-start | bytes 147464 | tf_op jit(solution)/shard_map/ppermute | solution.py:23
  59.3 6.2 %collective-permute-start.6 = (f32[3,8,18,1]{3,2,1,0:T(8,128)S(1)}, f32[3,8,18,1]{3,2,1,0:T(8,128)S(1)}, u32[]{:S(2)}, u32[]{:S(2)}) collective-permute-start(f32[3,8,18,1]{3,2,1,0:T(8,128)S(1)} %get-tuple-element.38), channel_id=1, source_target_pairs={{0,1},{1,2},{2,3},{3,4},{4,5},{5,6},{6,7},{7,0},{8,9},{9,10},{10,1... | collective-permute-start | bytes 5192 | tf_op jit(solution)/shard_map/ppermute | solution.py:22
  61.9 6.4 %collective-permute-start.7 = (f32[3,8,18,1]{3,2,1,0:T(8,128)S(1)}, f32[3,8,18,1]{3,2,1,0:T(8,128)S(1)}, u32[]{:S(2)}, u32[]{:S(2)}) collective-permute-start(f32[3,8,18,1]{3,2,1,0:T(8,128)S(1)} %get-tuple-element.39), channel_id=1, source_target_pairs={{1,0},{2,1},{3,2},{4,3},{5,4},{6,5},{7,6},{0,7},{9,8},{10,9},{11,1... | collective-permute-start | bytes 5192 | tf_op jit(solution)/shard_map/ppermute | solution.py:23
  69.0 0.9 copy-start.10
  71.7 6.6 %collective-permute-start.12 = (bf16[8,6,8,128]{3,2,1,0:T(8,128)(2,1)S(1)}, bf16[8,6,8,128]{3,2,1,0:T(8,128)(2,1)S(1)}, u32[]{:S(2)}, u32[]{:S(2)}) collective-permute-start(bf16[8,6,8,128]{3,2,1,0:T(8,128)(2,1)S(1)} %get-tuple-element.68), channel_id=1, source_target_pairs={{0,760},{8,0},{16,8},{24,16},{32,24},{40,32},{48,40},{56,48},{64,5... | collective-permute-start | bytes 294920 | tf_op jit(solution)/shard_map/ppermute | solution.py:12
  73.7 9.1 %collective-permute-start.13 = (bf16[8,6,8,128]{3,2,1,0:T(8,128)(2,1)S(1)}, bf16[8,6,8,128]{3,2,1,0:T(8,128)(2,1)S(1)}, u32[]{:S(2)}, u32[]{:S(2)}) collective-permute-start(bf16[8,6,8,128]{3,2,1,0:T(8,128)(2,1)S(1)} %get-tuple-element.69), channel_id=1, source_target_pairs={{0,8},{8,16},{16,24},{24,32},{32,40},{40,48},{48,56},{56,64},{64,7... | collective-permute-start | bytes 294920 | tf_op jit(solution)/shard_map/ppermute | solution.py:12
  77.0 7.1 %copy-start.11 = (f32[48,8,128]{2,1,0:T(8,128)S(1)}, f32[48,8,128]{2,1,0:T(8,128)}, u32[]{:S(2)}) copy-start(f32[48,8,128]{2,1,0:T(8,128)} %param.28) | copy-start | bytes 589828
  86.7 11.6 %collective-permute-start.14 = (bf16[8,6,8,128]{3,2,1,0:T(8,128)(2,1)S(1)}, bf16[8,6,8,128]{3,2,1,0:T(8,128)(2,1)S(1)}, u32[]{:S(2)}, u32[]{:S(2)}) collective-permute-start(bf16[8,6,8,128]{3,2,1,0:T(8,128)(2,1)S(1)} %bitcast.70), channel_id=1, source_target_pairs={{0,8},{8,16},{16,24},{24,32},{32,40},{40,48},{48,56},{56,64},{64,7... | collective-permute-start | bytes 294920 | tf_op jit(solution)/shard_map/ppermute | solution.py:12
  88.7 9.6 %collective-permute-start.15 = (bf16[8,6,8,128]{3,2,1,0:T(8,128)(2,1)S(1)}, bf16[8,6,8,128]{3,2,1,0:T(8,128)(2,1)S(1)}, u32[]{:S(2)}, u32[]{:S(2)}) collective-permute-start(bf16[8,6,8,128]{3,2,1,0:T(8,128)(2,1)S(1)} %bitcast.68), channel_id=1, source_target_pairs={{0,760},{8,0},{16,8},{24,16},{32,24},{40,32},{48,40},{56,48},{64,5... | collective-permute-start | bytes 294920 | tf_op jit(solution)/shard_map/ppermute | solution.py:12
  95.4 10.0 %copy-start.5 = (f32[4,8,1,384]{3,2,1,0:T(1,128)}, f32[4,8,1,384]{3,2,1,0:T(1,128)S(1)}, u32[]{:S(2)}) copy-start(f32[4,8,1,384]{3,2,1,0:T(1,128)S(1)} %collective-permute-done.8) | copy-start | bytes 147460
  95.4 9.9 %copy-start.6 = (f32[4,8,1,384]{3,2,1,0:T(1,128)}, f32[4,8,1,384]{3,2,1,0:T(1,128)S(1)}, u32[]{:S(2)}) copy-start(f32[4,8,1,384]{3,2,1,0:T(1,128)S(1)} %collective-permute-done.9) | copy-start | bytes 147460
  96.4 9.0 %collective-permute-start.10 = (f32[4,8,18,1]{3,2,1,0:T(8,128)}, f32[4,8,18,1]{3,2,1,0:T(8,128)S(1)}, u32[]{:S(2)}, u32[]{:S(2)}) collective-permute-start(f32[4,8,18,1]{3,2,1,0:T(8,128)} %get-tuple-element.34), channel_id=1, source_target_pairs={{1,0},{2,1},{3,2},{4,3},{5,4},{6,5},{7,6},{0,7},{9,8},{10,9},{11,1... | collective-permute-start | bytes 6920 | tf_op jit(solution)/shard_map/ppermute | solution.py:23
  98.3 7.8 %collective-permute-start.11 = (f32[4,8,18,1]{3,2,1,0:T(8,128)S(1)}, f32[4,8,18,1]{3,2,1,0:T(8,128)}, u32[]{:S(2)}, u32[]{:S(2)}) collective-permute-start(f32[4,8,18,1]{3,2,1,0:T(8,128)S(1)} %get-tuple-element.35), channel_id=1, source_target_pairs={{0,1},{1,2},{2,3},{3,4},{4,5},{5,6},{6,7},{7,0},{8,9},{9,10},{10,1... | collective-permute-start | bytes 6920 | tf_op jit(solution)/shard_map/ppermute | solution.py:22
  99.0 12.3 %all-to-all-start.1 = ((bf16[8,3,6,8,128]{4,3,2,1,0:T(8,128)(2,1)}), bf16[8,3,6,8,128]{4,3,2,1,0:T(8,128)(2,1)}, u32[]{:S(2)}, u32[]{:S(2)}) async-start(bf16[8,3,6,8,128]{4,3,2,1,0:T(8,128)(2,1)} %pad_maximum_fusion.13), calls=%async_computation.1 | async-start | bytes 589824 | tf_op jit(solution)/shard_map/all_to_all | solution.py:113
  105.3 8.2 %copy-start.16 = (bf16[48]{0:T(256)(128)(2,1)S(1)}, bf16[48]{0:T(256)(128)(2,1)}, u32[]{:S(2)}) copy-start(bf16[48]{0:T(256)(128)(2,1)} %copy-done.15) | copy-start | bytes 292
  105.3 125.5 %copy-start.18 = (f32[8]{0:T(128)S(1)}, f32[8]{0:T(128)}, u32[]{:S(2)}) copy-start(f32[8]{0:T(128)} %compare_convert_fusion) | copy-start | bytes 100
  105.3 0.7 copy-start.7
  114.6 0.6 copy-start.8
where the time goes:
time: 237 us; the launch traced here: 235 us
  blocking collectives  108 us (46%)
  starting transfers between devices  68.6 us (29%)
  other arithmetic  23.4 us (10%)
  local copies, waits for them, and re-layouts  19.3 us (8%)
  waiting for transfers between devices  14.1 us (6%)
    psum x1, blocking collectives, shards(): heat_total = lax.psum(heat_sum, ('lat', 'lon'))  108 us
    ppermute x6, starting transfers between devices, with_halo(): after = lax.ppermute(leading, axis, down)  24.7 us
    all_to_all x2, starting transfers between devices, move_columns(): lax.all_to_all(values, 'lon', split_axis=0, concat_axis=0, tiled=True)  19.2 us
    ppermute x4, starting transfers between devices, from_behind(): return lax.ppermute(value, axis, pairs)  13.9 us
    ppermute x6, starting transfers between devices, with_halo(): before = lax.ppermute(last, axis, up)  10.8 us
    scatter x1, local copies, waits for them, and re-layouts, shards(): outgoing = jnp.zeros((lon_count * 3 * pair_most, fields, tile_width), jnp...  5.34 us
  transfers between devices with their start and end apart: 18, of which 5 were waited for; matrix products, arithmetic and copies ran while one was open for 7% of the time, Pallas kernels for 0%

commit v1 on v0

v1 whole, which is shorter than its diff:
```python
import functools

import jax
import jax.numpy as jnp
from jax import lax
from jax.experimental import pallas as pl
from jax.experimental.pallas import tpu as pltpu
from jax.sharding import PartitionSpec as P

F32 = jnp.float32
BF16 = jnp.bfloat16
PAIR = 6
SLOTS = 20
LAND = 2.0**100
LAND_TEST = 2.0**90
VMEM = pl.BlockSpec(memory_space=pltpu.VMEM)
SMEM = pl.BlockSpec(memory_space=pltpu.SMEM)


def iota(shape, dim):
    return lax.broadcasted_iota(jnp.int32, shape, dim)


def block_of(ref, block):
    return ref[..., 128 * block : 128 * block + 128]


def tile_column(land_ref, block):
    rows = iota((16, 128), 0)
    out = jnp.zeros((16, 128), F32)
    for r in range(16):
        out = jnp.where(rows == r, land_ref[3 * r + block].astype(F32), out)
    return out


def pack_kernel(lats, dest_ref, land_ref, state_ref, tracer_ref, east_ref, kappa_ref, depth_ref,
                out_ref, code_ref, count_ref):
    lat = lax.axis_index("lat")
    lon = lax.axis_index("lon")
    lons = 8
    for i in range(24):
        count_ref[i] = 0
    for t in range(48):
        dest = dest_ref[t]
        off = lax.shift_right_logical(dest, 3) - lat + 1
        off = jnp.where(off < 0, off + lats, jnp.where(off >= lats, off - lats, off))
        dlon = lax.bitwise_and(dest, 7)
        key = off * 8 + dlon
        rank = count_ref[key]
        count_ref[key] = rank + 1
        code_ref[t] = key * 8 + rank
        value = state_ref[t].astype(F32)
        value = jnp.where(land_ref[t] > 0, value, LAND)
        out_ref[dlon * SLOTS + off * PAIR + rank] = value.astype(BF16)
    lanes = iota((16, 128), 1)
    for block, lane, shift in ((2, 127, 1), (0, 0, lons - 1)):
        packed = jnp.zeros((16, 128), F32)
        for i in range(32):
            packed = jnp.where(lanes == i, block_of(tracer_ref, block)[i][:, lane : lane + 1], packed)
        for i in range(8):
            if block == 2:
                packed = jnp.where(lanes == 32 + i, block_of(east_ref, block)[i][:, lane : lane + 1], packed)
            packed = jnp.where(lanes == 40 + i, block_of(kappa_ref, block)[i][:, lane : lane + 1], packed)
        bottom = block_of(depth_ref, block)[...].astype(F32) * tile_column(land_ref, block)
        packed = jnp.where(lanes == 48, bottom[:, lane : lane + 1], packed)
        target = lax.rem(lon + shift, lons)
        out_ref[target * SLOTS + 18] = packed[:8].astype(BF16)
        out_ref[target * SLOTS + 19] = packed[8:].astype(BF16)


def rows_kernel(land_ref, came_ref, tracer_ref, north_ref, kappa_ref, depth_ref, up_ref, down_ref):
    lon = lax.axis_index("lon")
    west = lax.rem(lon + 7, 8)
    east = lax.rem(lon + 1, 8)
    subs = iota((8, 128), 0)
    for out_ref, first, row in ((up_ref, 12, 15), (down_ref, 0, 0)):
        for s in range(8):
            for k in range(PAIR):
                out_ref[s * PAIR + k] = came_ref[s * SLOTS + first + k]
        half, sub = (19, 7) if row else (18, 0)
        corners = (
            came_ref[west * SLOTS + half].astype(F32)[sub : sub + 1],
            None,
            came_ref[east * SLOTS + half].astype(F32)[sub : sub + 1],
        )
        for j in range(3):
            cols = slice(128 * j, 128 * j + 128)
            for k in range(4):
                out_ref[48 + 3 * k + j] = tracer_ref[8 * k : 8 * k + 8, row, cols].astype(BF16)
            if row:
                out_ref[48 + 12 + j] = north_ref[:, row, cols].astype(BF16)
            else:
                out_ref[48 + 12 + j] = jnp.zeros((8, 128), BF16)
            out_ref[48 + 15 + j] = kappa_ref[:, row, cols].astype(BF16)
            bottom = depth_ref[row : row + 1, cols].astype(F32) * land_ref[3 * row + j].astype(F32)
            last = jnp.where(subs == 0, bottom, 0.0)
            if j != 1:
                last = jnp.where(subs == 1, corners[j], last)
            out_ref[48 + 18 + j] = last.astype(BF16)


def couple_kernel(place_ref, came_ref, low_ref, high_ref, atm_ref, coef_ref, sun_ref, mixing_ref,
                  out_ref, got_ref):
    total = jnp.zeros((8, 128), F32)
    for q in range(48):
        code = place_ref[q]
        rank = lax.bitwise_and(code, 7)
        slon = lax.bitwise_and(lax.shift_right_logical(code, 3), 7)
        off = lax.shift_right_logical(code, 6)
        at = slon * PAIR + rank
        own = came_ref[slon * SLOTS + PAIR + rank].astype(F32)
        low = low_ref[at].astype(F32)
        high = high_ref[at].astype(F32)
        value = jnp.where(off == 1, own, jnp.where(off == 2, low, high))
        got_ref[q] = value
        total = total + coef_ref[q : q + 1, :] * jnp.where(value < LAND_TEST, value, 0.0)
    weight = jnp.sum(jnp.sum(coef_ref[...], axis=0, keepdims=True), axis=1, keepdims=True)
    band_mean = jnp.sum(total, axis=1, keepdims=True) / weight
    mixing = mixing_ref[...]
    columns = [jnp.broadcast_to(mixing[:, g : g + 1], (8, 128)) for g in range(8)]
    heat = jnp.zeros((8, 128), F32)
    first = iota((8, 128), 0) == 0
    for q in range(48):
        code = place_ref[q]
        rank = lax.bitwise_and(code, 7)
        slon = lax.bitwise_and(lax.shift_right_logical(code, 3), 7)
        off = lax.shift_right_logical(code, 6)
        value = got_ref[q]
        wet = value < LAND_TEST
        drive = atm_ref[q] + band_mean - 2.0 * jnp.where(wet, value, 0.0)
        mixed = columns[0] * drive[0:1]
        for g in range(1, 8):
            mixed = mixed + columns[g] * drive[g : g + 1]
        coef = coef_ref[q : q + 1, :]
        flux = coef * mixed
        flux = flux + jnp.where(first, coef * sun_ref[q : q + 1, :], 0.0)
        rounded = flux.astype(BF16)
        out_ref[slon * SLOTS + off * PAIR + rank] = rounded
        heat = heat + jnp.where(wet, rounded.astype(F32), 0.0)
    subs = iota((8, 128), 0)
    row = jnp.broadcast_to(heat[0:1], (8, 128))
    one = row.astype(BF16).astype(F32)
    two = (row - one).astype(BF16).astype(F32)
    three = row - one - two
    parts = jnp.where(subs == 0, one, jnp.where(subs == 1, two, jnp.where(subs == 2, three, 0.0)))
    for s in range(8):
        out_ref[s * SLOTS + 18] = parts.astype(BF16)


def split_kernel(lats, back_ref, to_south_ref, to_north_ref, heat_ref):
    heat = jnp.zeros((8, 128), F32)
    for s in range(8):
        heat = heat + back_ref[s * SLOTS + 18].astype(F32)
        for k in range(PAIR):
            to_south_ref[s * PAIR + k] = back_ref[s * SLOTS + 12 + k]
            to_north_ref[s * PAIR + k] = back_ref[s * SLOTS + k]
    row = jnp.sum(heat, axis=0, keepdims=True)
    heat_ref[...] = jnp.broadcast_to(row[None], (lats, 1, 128))


def stencil_kernel(lats, land_ref, came_ref, low_ref, high_ref, tracer_ref, east_ref, north_ref,
                   kappa_ref, cross_ref, depth_ref, out_ref, rows_ref, diag_ref, bottom_ref):
    lat = lax.axis_index("lat")
    lon = lax.axis_index("lon")
    west = lax.rem(lon + 7, 8)
    east = lax.rem(lon + 1, 8)
    full = (16, 384)
    lanes = iota(full, 1)
    subs = iota(full, 0)
    at_west, at_east = lanes == 0, lanes == 383
    at_south, at_north = subs == 0, subs == 15
    small = iota((8, 384), 1)
    lane8, sub8 = iota((8, 128), 1), iota((8, 128), 0)

    def columns_of(side):
        return jnp.concatenate(
            [came_ref[side * SLOTS + 18].astype(F32), came_ref[side * SLOTS + 19].astype(F32)], axis=0
        )

    def from_west(v, column):
        return jnp.where(at_west, column, pltpu.roll(v, 1, 1))

    def from_east(v, column):
        return jnp.where(at_east, column, pltpu.roll(v, 383, 1))

    def from_south(v, row):
        return jnp.where(at_south, row, pltpu.roll(v, 1, 0))

    def from_north(v, row):
        return jnp.where(at_north, row, pltpu.roll(v, 15, 0))

    col_west, col_east = columns_of(west), columns_of(east)
    for side, ref in enumerate((low_ref, high_ref)):
        inside = jnp.where(lat == (0, lats - 1)[side], 0.0, 1.0)
        for k in range(7):
            for j in range(3):
                tile = ref[48 + 3 * k + j].astype(F32)
                if k == 6:
                    tile = jnp.where(sub8 == 0, tile * inside, tile)
                rows_ref[side, 8 * k : 8 * k + 8, 128 * j : 128 * j + 128] = tile
    for j in range(3):
        cols = slice(128 * j, 128 * j + 128)
        bottom_ref[0, :, cols] = depth_ref[:, cols].astype(F32) * tile_column(land_ref, j)
    bottom = bottom_ref[0]
    bottom_ref[1] = from_east(bottom, col_east[:, 48:49])
    bottom_ref[2] = from_west(bottom, col_west[:, 48:49])
    bottom_ref[3] = from_north(bottom, rows_ref[1, 48:49, :])
    bottom_ref[4] = from_south(bottom, rows_ref[0, 48:49, :])

    level8 = iota((8, 384), 0).astype(F32)
    for side in range(2):
        inside = jnp.where(lat == (0, lats - 1)[side], 0.0, 1.0)
        corner_w = jnp.broadcast_to(rows_ref[side, 49:50, 0:128], (8, 128))
        corner_e = jnp.broadcast_to(rows_ref[side, 49:50, 256:384], (8, 128))
        edge = jnp.broadcast_to(rows_ref[side, 48:49, :], (8, 384))
        edge_e = jnp.where(small == 383, corner_e[:, 48:49] * inside, pltpu.roll(edge, 383, 1))
        edge_w = jnp.where(small == 0, corner_w[:, 48:49] * inside, pltpu.roll(edge, 1, 1))
        for k in range(4):
            value = rows_ref[side, 8 * k : 8 * k + 8, :]
            pick = lane8 == sub8 + 8 * k
            value_e = jnp.sum(jnp.where(pick, corner_e, 0.0), axis=1, keepdims=True)
            value_w = jnp.sum(jnp.where(pick, corner_w, 0.0), axis=1, keepdims=True)
            value_e = jnp.where(small == 383, value_e, pltpu.roll(value, 383, 1))
            value_w = jnp.where(small == 0, value_w, pltpu.roll(value, 1, 1))
            diag_ref[side, 8 * k : 8 * k + 8, :] = jnp.where(level8 < edge_e, value_e, 0.0) - jnp.where(
                level8 < edge_w, value_w, 0.0
            )

    def level_step(l, carry):
        lf = l.astype(F32)
        cw = pltpu.roll(col_west, lax.rem(128 - l, 128), 1)
        ce = pltpu.roll(col_east, lax.rem(128 - l, 128), 1)
        masks = [(lf < bottom_ref[i]).astype(F32) for i in range(5)]
        mask, mask_e, mask_w, mask_n, mask_s = masks
        kappa = kappa_ref[l]
        velocity = east_ref[l]
        kap = 0.5 * (kappa + from_east(kappa, ce[:, 40:41]))
        open_face = mask * mask_e
        out_e = open_face * (jnp.maximum(velocity, 0.0) + kap)
        in_e = open_face * (kap - jnp.minimum(velocity, 0.0))
        velocity = from_west(velocity, cw[:, 32:33])
        kap = 0.5 * (kappa + from_west(kappa, cw[:, 40:41]))
        open_face = mask * mask_w
        in_w = open_face * (jnp.maximum(velocity, 0.0) + kap)
        out_w = open_face * (kap - jnp.minimum(velocity, 0.0))
        velocity = north_ref[l]
        kap = 0.5 * (kappa + from_north(kappa, rows_ref[1, pl.ds(40 + l, 1), :]))
        open_face = mask * mask_n
        out_n = open_face * (jnp.maximum(velocity, 0.0) + kap)
        in_n = open_face * (kap - jnp.minimum(velocity, 0.0))
        velocity = from_south(velocity, rows_ref[0, pl.ds(32 + l, 1), :])
        kap = 0.5 * (kappa + from_south(kappa, rows_ref[0, pl.ds(40 + l, 1), :]))
        open_face = mask * mask_s
        in_s = open_face * (jnp.maximum(velocity, 0.0) + kap)
        out_s = open_face * (kap - jnp.minimum(velocity, 0.0))
        keep = 1.0 - (out_e + out_w + out_n + out_s)
        cross = cross_ref[l] * mask
        for t in range(4):
            i = 8 * t + l
            c = tracer_ref[i]
            c_e = from_east(c, ce[:, 8 * t : 8 * t + 1])
            c_w = from_west(c, cw[:, 8 * t : 8 * t + 1])
            c_n = from_north(c, rows_ref[1, pl.ds(i, 1), :])
            c_s = from_south(c, rows_ref[0, pl.ds(i, 1), :])
            diag = mask_e * c_e - mask_w * c_w
            diag_n = from_north(diag, diag_ref[1, pl.ds(i, 1), :])
            diag_s = from_south(diag, diag_ref[0, pl.ds(i, 1), :])
            out_ref[i] = (
                keep * c + in_e * c_e + in_w * c_w + in_n * c_n + in_s * c_s + cross * (diag_n - diag_s)
            )
        return carry

    lax.fori_loop(0, 8, level_step, 0)


def finish_kernel(points, code_ref, land_ref, back_ref, from_north_ref, from_south_ref, heat_ref, depth_ref,
                  step_ref, flux_ref, out_ref, wide_ref):
    for t in range(48):
        code = code_ref[t]
        rank = lax.bitwise_and(code, 7)
        dlon = lax.bitwise_and(lax.shift_right_logical(code, 3), 7)
        off = lax.shift_right_logical(code, 6)
        at = dlon * PAIR + rank
        own = back_ref[dlon * SLOTS + PAIR + rank].astype(F32)
        north = from_north_ref[at].astype(F32)
        south = from_south_ref[at].astype(F32)
        value = jnp.where(off == 1, own, jnp.where(off == 2, north, south))
        value = jnp.where(land_ref[t] > 0, value, 0.0)
        flux_ref[t] = value.astype(BF16)
        wide_ref[8 * t : 8 * t + 8, :] = value
    heat = jnp.sum(jnp.sum(heat_ref[...], axis=0), axis=1, keepdims=True)
    correction = heat / points
    for j in range(3):
        cols = slice(128 * j, 128 * j + 128)
        wet = depth_ref[:, cols].astype(F32) * tile_column(land_ref, j)
        gain = jnp.where(wet > 0.0, 0.5, 0.0)
        for t in range(4):
            force = wide_ref[pl.ds(8 * j + t, 16, stride=24), :]
            if t == 0:
                force = force - correction
            out_ref[t, 0, :, cols] = step_ref[t, 0, :, cols] + gain * force


def call(kernel, name, in_specs, out_shape, out_specs, scratch=(), **more):
    return pl.pallas_call(
        kernel,
        out_shape=out_shape,
        in_specs=in_specs,
        out_specs=out_specs,
        scratch_shapes=list(scratch),
        name=name,
        **more,
    )


def shape(dims, dtype):
    return jax.ShapeDtypeStruct(dims, dtype)


def shards(
    tracers,
    east_velocity,
    north_velocity,
    diffusivity,
    cross_diffusivity,
    depth_levels,
    land_mask,
    ocean_state,
    atm_state,
    exchange_coef,
    sunlight,
    mixing,
    o2a_dest,
    o2a_slot,
    a2o_source,
    a2o_tile,
):
    lats = lax.axis_size("lat")
    lons = lax.axis_size("lon")
    lat = lax.axis_index("lat")
    north_pairs = [(i, (i + 1) % lats) for i in range(lats)]
    south_pairs = [(j, i) for i, j in north_pairs]
    flat = (8 * SLOTS, 8, 128)

    def turn(values):
        values = values.reshape(8, SLOTS, 8, 128)
        return lax.all_to_all(values, "lon", 0, 0, tiled=True).reshape(flat)

    tracers_l = tracers.reshape(32, 16, 384)

    outgoing, code = call(
        functools.partial(pack_kernel, lats),
        "pack",
        [SMEM, SMEM, VMEM, VMEM, VMEM, VMEM, VMEM],
        (shape(flat, BF16), shape((48,), jnp.int32)),
        (VMEM, SMEM),
        [pltpu.SMEM((24,), jnp.int32)],
    )(o2a_dest, land_mask, ocean_state, tracers_l, east_velocity, diffusivity, depth_levels)

    source_off = (lat - a2o_source // lons + 1) % lats
    same = a2o_source[:, None] == a2o_source[None, :]
    earlier = a2o_tile[None, :] < a2o_tile[:, None]
    source_rank = jnp.sum((same & earlier).astype(jnp.int32), axis=1)
    place = source_off * 64 + (a2o_source % lons) * 8 + source_rank

    came = turn(outgoing)
    row_shape = shape((69, 8, 128), BF16)
    up, down = call(
        rows_kernel,
        "rows",
        [SMEM, VMEM, VMEM, VMEM, VMEM, VMEM],
        (row_shape, row_shape),
        (VMEM, VMEM),
    )(
        land_mask,
        came,
        tracers_l,
        north_velocity,
        diffusivity,
        depth_levels,
    )
    low = lax.ppermute(up, "lat", north_pairs)
    high = lax.ppermute(down, "lat", south_pairs)

    backward = call(
        couple_kernel,
        "couple",
        [SMEM] + [VMEM] * 7,
        shape(flat, BF16),
        VMEM,
        [pltpu.VMEM((48, 8, 128), F32)],
    )(place, came, low, high, atm_state, exchange_coef, sunlight, mixing)
    back = turn(backward)

    step = call(
        functools.partial(stencil_kernel, lats),
        "stencil",
        [SMEM] + [VMEM] * 9,
        shape((32, 16, 384), F32),
        VMEM,
        [pltpu.VMEM((2, 56, 384), F32), pltpu.VMEM((2, 32, 384), F32), pltpu.VMEM((5, 16, 384), F32)],
        cost_estimate=pl.CostEstimate(flops=8000000, bytes_accessed=3000000, transcendentals=0),
    )(
        land_mask,
        came,
        low,
        high,
        tracers_l,
        east_velocity,
        north_velocity,
        diffusivity,
        cross_diffusivity,
        depth_levels,
    )

    to_south, to_north, heat = call(
        functools.partial(split_kernel, lats),
        "split",
        [VMEM],
        (shape((48, 8, 128), BF16), shape((48, 8, 128), BF16), shape((lats, 1, 128), F32)),
        (VMEM, VMEM, VMEM),
    )(back)
    heat = lax.all_to_all(heat, "lat", 0, 0, tiled=True)
    back_north = lax.ppermute(to_south, "lat", south_pairs)
    back_south = lax.ppermute(to_north, "lat", north_pairs)

    points = float(48 * 128 * lats * lons)
    top = pl.BlockSpec((4, 1, 16, 384), lambda i: (0, 0, 0, 0))
    ocean_flux, new_tracers = call(
        functools.partial(finish_kernel, points),
        "finish",
        [SMEM, SMEM, VMEM, VMEM, VMEM, VMEM, VMEM, top],
        (shape((48, 8, 128), BF16), shape((4, 8, 16, 384), F32)),
        (VMEM, top),
        [pltpu.VMEM((384, 128), F32)],
        grid=(1,),
        input_output_aliases={7: 1},
    )(code, land_mask, back, back_north, back_south, heat, depth_levels, step.reshape(4, 8, 16, 384))
    return (new_tracers, ocean_flux)


def solution(mesh):
    return jax.shard_map(
        shards,
        mesh=mesh,
        in_specs=(
            P(None, None, "lat", "lon"),
            P(None, "lat", "lon"),
            P(None, "lat", "lon"),
            P(None, "lat", "lon"),
            P(None, "lat", "lon"),
            P("lat", "lon"),
            P(("lat", "lon")),
            P(("lat", "lon"), None, None),
            P(("lat", "lon"), None, None),
            P(("lat", "lon"), None),
            P(("lat", "lon"), None),
            P(),
            P(("lat", "lon")),
            P(("lat", "lon")),
            P(("lat", "lon")),
            P(("lat", "lon")),
        ),
        out_specs=(P(None, None, "lat", "lon"), P(("lat", "lon"), None, None)),
        check_vma=False,
    )
```

time: 237 us -> 88.2 us (0.37)
  blocking collectives: 108 us -> 13.5 us
  starting transfers between devices: 68.6 us -> 43.8 us
  other arithmetic: 23.4 us -> 0.71 us
  local copies, waits for them, and re-layouts: 19.3 us -> 2.7 us
  Pallas kernels: 0 us -> 15.6 us
  waiting for transfers between devices: 14.1 us -> 10.2 us
    psum x1 -> x0, blocking collectives: 108 us -> none  [shards(): heat_total = lax.psum(heat_sum, ('lat', 'lon'))]
    ppermute x16 -> x4, starting transfers between devices: 49.4 us -> 19.5 us  [the longest x1 9.14 us: shards(): high = lax.ppermute(down, 'lat', south_pairs)]
    pallas_call x0 -> x6, Pallas kernels: none -> 15.6 us  [the longest x1 4.64 us: shards(): call(functools.partial(stencil_kernel, lats), 'stencil', [SMEM] + [VMEM]...]
    all_to_all x0 -> x1, blocking collectives: none -> 13.5 us  [turn(): return lax.all_to_all(values, 'lon', 0, 0, tiled=True).reshape(flat)]
    ppermute x16 -> x4, waiting for transfers between devices: 11.6 us -> 3.91 us  [the longest x1 2.11 us: shards(): back_south = lax.ppermute(to_north, 'lat', north_pairs)]
    scatter x2 -> x0, local copies, waits for them, and re-layouts: 7.3 us -> none  [the longest x1 5.34 us: shards(): outgoing = jnp.zeros((lon_count * 3 * pair_most, fields, tile_width), jnp...]
    add x4 -> x1, other arithmetic: 6.81 us -> 0.54 us  [shards(): place = source_off * 64 + a2o_source % lons * 8 + source_rank]
    all_to_all x2, starting transfers between devices: 19.2 us -> 24.2 us  [the longest x1 13.9 us: turn(): return lax.all_to_all(values, 'lon', 0, 0, tiled=True).reshape(flat)]
  transfers between devices with their start and end apart: 18 -> 6, of which waited for: 5 -> 4; matrix products, arithmetic and copies ran while one was open for 7% -> 1% of each run, Pallas kernels for 0% -> 5%
where the time goes in v1:
time: 88.2 us; the launch traced here: 87.2 us
  starting transfers between devices  43.8 us (50%)
  Pallas kernels  15.6 us (18%)
  blocking collectives  13.5 us (15%)
  waiting for transfers between devices  10.2 us (12%)
  local copies, waits for them, and re-layouts  2.7 us (3%)
    all_to_all x1, starting transfers between devices, turn(): return lax.all_to_all(values, 'lon', 0, 0, tiled=True).reshape(flat)  13.9 us
    all_to_all x1, blocking collectives, turn(): return lax.all_to_all(values, 'lon', 0, 0, tiled=True).reshape(flat)  13.5 us
    all_to_all x1, starting transfers between devices, shards(): heat = lax.all_to_all(heat, 'lat', 0, 0, tiled=True)  10.4 us
    ppermute x1, starting transfers between devices, shards(): high = lax.ppermute(down, 'lat', south_pairs)  9.14 us
    ppermute x1, starting transfers between devices, shards(): back_north = lax.ppermute(to_south, 'lat', south_pairs)  6.55 us
    all_to_all x1, waiting for transfers between devices, turn(): return lax.all_to_all(values, 'lon', 0, 0, tiled=True).reshape(flat)  6.29 us
    pallas_call x1, Pallas kernels, shards(): call(functools.partial(stencil_kernel, lats), 'stencil', [SMEM] + [VMEM]...  4.64 us
    unnamed x18, local copies, waits for them, and re-layouts  2.7 us
  transfers between devices with their start and end apart: 6, of which 4 were waited for; matrix products, arithmetic and copies ran while one was open for 1% of the time, Pallas kernels for 5%

profile of v1, /device:TPU:1, one launch (start us, length us, event | category | flops | bytes accessed | tf_op | source)
XLA Modules:
  0.0 87.2 jit_solution(5803967554640481307)
XLA Ops:
  0.6 2.4 %pack.1 = (bf16[160,8,128]{2,1,0:T(8,128)(2,1)}, s32[48]{0:T(128)}) custom-call(s32[48]{0:T(128)} %dest_ref.1, s32[48]{0:T(128)} %land_ref.7, bf16[48,8,128]{2,1,0:T(8,128)(2,1)} %state_ref.1, f32[32,16,384]{2,1,0:T(8,128)} %bitcast.6, f32[8,16,384]{2,1,0:T(8,128)} %east_ref.3, f32[8,16,384]{2,1,0:T(8,128)} %kappa_ref.5, s32[16,384]{1,0:T(8,128)} %depth_ref.7), custom_call_target="tpu_custom_call" | custom-call | tf_op jit(solution)/shard_map/pack/pallas_call | solution.py:351
  3.0 13.9 %all-to-all-start = ((bf16[8,20,8,128]{3,2,1,0:T(8,128)(2,1)}), bf16[8,20,8,128]{3,2,1,0:T(8,128)(2,1)S(1)}, u32[]{:S(2)}, u32[]{:S(2)}) async-start(bf16[8,20,8,128]{3,2,1,0:T(8,128)(2,1)} %bitcast.16), calls=%async_computation | async-start | bytes 655360 | tf_op jit(solution)/shard_map/all_to_all | solution.py:347
  16.9 0.0 copy-start.6
  16.9 0.0 copy-start.7
  16.9 0.7 copy-done.6
  17.6 0.0 copy-done.7
  17.6 0.2 convert_reduce_fusion
  17.8 6.3 %all-to-all-done = bf16[8,20,8,128]{3,2,1,0:T(8,128)(2,1)S(1)} async-done(((bf16[8,20,8,128]{3,2,1,0:T(8,128)(2,1)}), bf16[8,20,8,128]{3,2,1,0:T(8,128)(2,1)S(1)}, u32[]{:S(2)}, u32[]{:S(2)}) %all-to-all-start) | async-done | bytes 327712 | tf_op jit(solution)/shard_map/all_to_all | solution.py:347
  24.0 0.0 copy-start
  24.1 0.7 copy-done
  24.8 2.1 %rows.1 = (bf16[69,8,128]{2,1,0:T(8,128)(2,1)}, bf16[69,8,128]{2,1,0:T(8,128)(2,1)}) custom-call(s32[48]{0:T(128)} %land_ref.7, bf16[160,8,128]{2,1,0:T(8,128)(2,1)} %bitcast.9, f32[32,16,384]{2,1,0:T(8,128)} %bitcast.7, f32[8,16,384]{2,1,0:T(8,128)} %north_ref.3, f32[8,16,384]{2,1,0:T(8,128)} %kappa_ref.5, s32[16,384]{1,0:T(8,128)} %depth_ref.7), custom_call_target="tpu_custom_call" | custom-call | tf_op jit(solution)/shard_map/rows/pallas_call | solution.py:368
  26.9 1.9 %collective-permute-start = (bf16[69,8,128]{2,1,0:T(8,128)(2,1)}, bf16[69,8,128]{2,1,0:T(8,128)(2,1)S(1)}, u32[]{:S(2)}, u32[]{:S(2)}) collective-permute-start(bf16[69,8,128]{2,1,0:T(8,128)(2,1)} %get-tuple-element.13), channel_id=1, source_target_pairs={{0,8},{8,16},{16,24},{24,32},{32,40},{40,48},{48,56},{56,64},{64,7... | collective-permute-start | bytes 423944 | tf_op jit(solution)/shard_map/ppermute | solution.py:382
  28.8 9.1 %collective-permute-start.1 = (bf16[69,8,128]{2,1,0:T(8,128)(2,1)}, bf16[69,8,128]{2,1,0:T(8,128)(2,1)S(1)}, u32[]{:S(2)}, u32[]{:S(2)}) collective-permute-start(bf16[69,8,128]{2,1,0:T(8,128)(2,1)} %get-tuple-element.14), channel_id=1, source_target_pairs={{8,0},{16,8},{24,16},{32,24},{40,32},{48,40},{56,48},{64,56},{72,6... | collective-permute-start | bytes 423944 | tf_op jit(solution)/shard_map/ppermute | solution.py:383
  38.0 0.5 fusion.2.place_ref
  38.5 0.7 collective-permute-done.low_ref
  39.1 0.0 copy-start.1
  39.2 1.1 %collective-permute-done.1.high_ref = bf16[69,8,128]{2,1,0:T(8,128)(2,1)S(1)} collective-permute-done((bf16[69,8,128]{2,1,0:T(8,128)(2,1)}, bf16[69,8,128]{2,1,0:T(8,128)(2,1)S(1)}, u32[]{:S(2)}, u32[]{:S(2)}) %collective-permute-start.1) | collective-permute-done | bytes 141344 | tf_op jit(solution)/shard_map/ppermute | solution.py:383
  40.3 0.0 copy-done.1
  40.3 0.0 copy-start.2
  40.3 0.7 copy-done.2
  41.0 2.6 %couple.1 = bf16[160,8,128]{2,1,0:T(8,128)(2,1)} custom-call(s32[48]{0:T(128)} %fusion.2.place_ref, bf16[160,8,128]{2,1,0:T(8,128)(2,1)} %bitcast.10, bf16[69,8,128]{2,1,0:T(8,128)(2,1)} %copy-done.1, bf16[69,8,128]{2,1,0:T(8,128)(2,1)} %copy-done.2, f32[48,8,128]{2,1,0:T(8,128)} %atm_ref.1, f32[48,128]{1,0:T(8,128)} %coef_ref.1, f32[48,128]{1,0:T(8,128)} %sun_ref.1, ...), custom_call_target="tpu_custom_call" | custom-call | tf_op jit(solution)/shard_map/couple/pallas_call | solution.py:385
  43.6 13.5 %all_to_all.15 = bf16[8,20,8,128]{3,2,1,0:T(8,128)(2,1)} all-to-all(bf16[8,20,8,128]{3,2,1,0:T(8,128)(2,1)} %bitcast.15), channel_id=1, replica_groups=mesh['lat'=96,'lon'=8] {'lon'}, dimensions={0} | all-to-all | bytes 655360 | tf_op jit(solution)/shard_map/all_to_all | solution.py:347
  57.1 1.7 %split.1 = (bf16[48,8,128]{2,1,0:T(8,128)(2,1)}, bf16[48,8,128]{2,1,0:T(8,128)(2,1)}, f32[96,1,128]{2,1,0:T(1,128)}) custom-call(bf16[160,8,128]{2,1,0:T(8,128)(2,1)} %bitcast.13), custom_call_target="tpu_custom_call" | custom-call | tf_op jit(solution)/shard_map/split/pallas_call | solution.py:416
  58.8 0.0 copy-start.8
  58.8 10.4 %all-to-all-start.2 = ((f32[96,1,128]{2,1,0:T(1,128)}), f32[96,1,128]{2,1,0:T(1,128)S(1)}, u32[]{:S(2)}, u32[]{:S(2)}) async-start(f32[96,1,128]{2,1,0:T(1,128)} %get-tuple-element.17), calls=%async_computation.2 | async-start | bytes 98304 | tf_op jit(solution)/shard_map/all_to_all | solution.py:423
  69.2 6.6 %collective-permute-start.2 = (bf16[48,8,128]{2,1,0:T(8,128)(2,1)}, bf16[48,8,128]{2,1,0:T(8,128)(2,1)S(1)}, u32[]{:S(2)}, u32[]{:S(2)}) collective-permute-start(bf16[48,8,128]{2,1,0:T(8,128)(2,1)} %get-tuple-element.15), channel_id=1, source_target_pairs={{8,0},{16,8},{24,16},{32,24},{40,32},{48,40},{56,48},{64,56},{72,6... | collective-permute-start | bytes 294920 | tf_op jit(solution)/shard_map/ppermute | solution.py:424
  75.7 0.0 copy-done.8
  75.7 1.9 %collective-permute-start.3 = (bf16[48,8,128]{2,1,0:T(8,128)(2,1)S(1)}, bf16[48,8,128]{2,1,0:T(8,128)(2,1)S(1)}, u32[]{:S(2)}, u32[]{:S(2)}) collective-permute-start(bf16[48,8,128]{2,1,0:T(8,128)(2,1)S(1)} %copy-done.8), channel_id=1, source_target_pairs={{0,8},{8,16},{16,24},{24,32},{32,40},{40,48},{48,56},{56,64},{64,7... | collective-permute-start | bytes 294920 | tf_op jit(solution)/shard_map/ppermute | solution.py:425
  77.7 4.6 %stencil.1 = f32[32,16,384]{2,1,0:T(8,128)} custom-call(s32[48]{0:T(128)} %land_ref.7, bf16[160,8,128]{2,1,0:T(8,128)(2,1)} %bitcast.11, bf16[69,8,128]{2,1,0:T(8,128)(2,1)} %copy-done.1, bf16[69,8,128]{2,1,0:T(8,128)(2,1)} %copy-done.2, f32[32,16,384]{2,1,0:T(8,128)} %bitcast.8, f32[8,16,384]{2,1,0:T(8,128)} %east_ref.3, f32[8,16,384]{2,1,0:T(8,128)} %north_ref.3, ...), custom_call_target="tpu_custom_call" | custom-call | flops 8000000 | bytes 3000000 | tf_op jit(solution)/shard_map/stencil/pallas_call | solution.py:395
  82.3 0.0 collective-permute-done.2.from_north_ref
  82.3 0.0 copy-start.4
  82.3 2.1 %collective-permute-done.3.from_south_ref = bf16[48,8,128]{2,1,0:T(8,128)(2,1)S(1)} collective-permute-done((bf16[48,8,128]{2,1,0:T(8,128)(2,1)S(1)}, bf16[48,8,128]{2,1,0:T(8,128)(2,1)S(1)}, u32[]{:S(2)}, u32[]{:S(2)}) %collective-permute-start.3) | collective-permute-done | bytes 98336 | tf_op jit(solution)/shard_map/ppermute | solution.py:425
  84.4 0.0 copy-start.5
  84.4 0.0 all-to-all-done.2.heat_ref
  84.4 0.0 copy-start.3
  84.4 0.0 copy-done.4
  84.4 0.6 copy-done.5
  85.1 0.0 copy-done.3
  85.1 2.2 %finish.1 = (bf16[48,8,128]{2,1,0:T(8,128)(2,1)}, f32[4,8,16,384]{3,2,1,0:T(8,128)}) custom-call(s32[48]{0:T(128)} %get-tuple-element.11.code_ref, s32[48]{0:T(128)} %land_ref.7, bf16[160,8,128]{2,1,0:T(8,128)(2,1)} %bitcast.14, bf16[48,8,128]{2,1,0:T(8,128)(2,1)} %copy-done.4, bf16[48,8,128]{2,1,0:T(8,128)(2,1)} %copy-done.5, ...), custom_call_target="tpu_custom_call", output_to_operand_aliasing={{1}: (7, {})} | custom-call | tf_op jit(solution)/shard_map/finish/pallas_call | solution.py:429
Async XLA Ops:
  3.0 21.0 %all-to-all-start = ((bf16[8,20,8,128]{3,2,1,0:T(8,128)(2,1)}), bf16[8,20,8,128]{3,2,1,0:T(8,128)(2,1)S(1)}, u32[]{:S(2)}, u32[]{:S(2)}) async-start(bf16[8,20,8,128]{3,2,1,0:T(8,128)(2,1)} %bitcast.16), calls=%async_computation | async-start | bytes 655360 | tf_op jit(solution)/shard_map/all_to_all | solution.py:347
  16.9 0.7 copy-start.6
  16.9 0.7 copy-start.7
  24.0 0.7 copy-start
  26.9 12.3 %collective-permute-start = (bf16[69,8,128]{2,1,0:T(8,128)(2,1)}, bf16[69,8,128]{2,1,0:T(8,128)(2,1)S(1)}, u32[]{:S(2)}, u32[]{:S(2)}) collective-permute-start(bf16[69,8,128]{2,1,0:T(8,128)(2,1)} %get-tuple-element.13), channel_id=1, source_target_pairs={{0,8},{8,16},{16,24},{24,32},{32,40},{40,48},{48,56},{56,64},{64,7... | collective-permute-start | bytes 423944 | tf_op jit(solution)/shard_map/ppermute | solution.py:382
  28.8 11.5 %collective-permute-start.1 = (bf16[69,8,128]{2,1,0:T(8,128)(2,1)}, bf16[69,8,128]{2,1,0:T(8,128)(2,1)S(1)}, u32[]{:S(2)}, u32[]{:S(2)}) collective-permute-start(bf16[69,8,128]{2,1,0:T(8,128)(2,1)} %get-tuple-element.14), channel_id=1, source_target_pairs={{8,0},{16,8},{24,16},{32,24},{40,32},{48,40},{56,48},{64,56},{72,6... | collective-permute-start | bytes 423944 | tf_op jit(solution)/shard_map/ppermute | solution.py:383
  39.1 1.1 %copy-start.1 = (bf16[69,8,128]{2,1,0:T(8,128)(2,1)}, bf16[69,8,128]{2,1,0:T(8,128)(2,1)S(1)}, u32[]{:S(2)}) copy-start(bf16[69,8,128]{2,1,0:T(8,128)(2,1)S(1)} %collective-permute-done.low_ref) | copy-start | bytes 423940
  40.3 0.7 copy-start.2
  58.8 17.0 %copy-start.8 = (bf16[48,8,128]{2,1,0:T(8,128)(2,1)S(1)}, bf16[48,8,128]{2,1,0:T(8,128)(2,1)}, u32[]{:S(2)}) copy-start(bf16[48,8,128]{2,1,0:T(8,128)(2,1)} %get-tuple-element.16) | copy-start | bytes 294916
  58.8 25.7 %all-to-all-start.2 = ((f32[96,1,128]{2,1,0:T(1,128)}), f32[96,1,128]{2,1,0:T(1,128)S(1)}, u32[]{:S(2)}, u32[]{:S(2)}) async-start(f32[96,1,128]{2,1,0:T(1,128)} %get-tuple-element.17), calls=%async_computation.2 | async-start | bytes 98304 | tf_op jit(solution)/shard_map/all_to_all | solution.py:423
  69.2 13.1 %collective-permute-start.2 = (bf16[48,8,128]{2,1,0:T(8,128)(2,1)}, bf16[48,8,128]{2,1,0:T(8,128)(2,1)S(1)}, u32[]{:S(2)}, u32[]{:S(2)}) collective-permute-start(bf16[48,8,128]{2,1,0:T(8,128)(2,1)} %get-tuple-element.15), channel_id=1, source_target_pairs={{8,0},{16,8},{24,16},{32,24},{40,32},{48,40},{56,48},{64,56},{72,6... | collective-permute-start | bytes 294920 | tf_op jit(solution)/shard_map/ppermute | solution.py:424
  75.7 8.7 %collective-permute-start.3 = (bf16[48,8,128]{2,1,0:T(8,128)(2,1)S(1)}, bf16[48,8,128]{2,1,0:T(8,128)(2,1)S(1)}, u32[]{:S(2)}, u32[]{:S(2)}) collective-permute-start(bf16[48,8,128]{2,1,0:T(8,128)(2,1)S(1)} %copy-done.8), channel_id=1, source_target_pairs={{0,8},{8,16},{16,24},{24,32},{32,40},{40,48},{48,56},{56,64},{64,7... | collective-permute-start | bytes 294920 | tf_op jit(solution)/shard_map/ppermute | solution.py:425
  82.3 2.1 %copy-start.4 = (bf16[48,8,128]{2,1,0:T(8,128)(2,1)}, bf16[48,8,128]{2,1,0:T(8,128)(2,1)S(1)}, u32[]{:S(2)}) copy-start(bf16[48,8,128]{2,1,0:T(8,128)(2,1)S(1)} %collective-permute-done.2.from_north_ref) | copy-start | bytes 294916
  84.4 0.6 copy-start.5
  84.4 0.6 copy-start.3

commit v2 on v1

--- a/solution.py
+++ b/solution.py
@@ -15,6 +15,8 @@
 LAND_TEST = 2.0**90
 VMEM = pl.BlockSpec(memory_space=pltpu.VMEM)
 SMEM = pl.BlockSpec(memory_space=pltpu.SMEM)
+ANY = pl.BlockSpec(memory_space=pl.ANY)
+SMALL = 16 * 1024 * 1024
 
 
 def iota(shape, dim):
@@ -147,7 +149,7 @@
         out_ref[s * SLOTS + 18] = parts.astype(BF16)
 
 
-def split_kernel(lats, back_ref, to_south_ref, to_north_ref, heat_ref):
+def split_kernel(lats, back_ref, done_ref, to_south_ref, to_north_ref, heat_ref):
     heat = jnp.zeros((8, 128), F32)
     for s in range(8):
         heat = heat + back_ref[s * SLOTS + 18].astype(F32)
@@ -159,7 +161,7 @@
 
 
 def stencil_kernel(lats, land_ref, came_ref, low_ref, high_ref, tracer_ref, east_ref, north_ref,
-                   kappa_ref, cross_ref, depth_ref, out_ref, rows_ref, diag_ref, bottom_ref):
+                   kappa_ref, cross_ref, depth_ref, after_ref, out_ref, done_ref, rows_ref, diag_ref, bottom_ref):
     lat = lax.axis_index("lat")
     lon = lax.axis_index("lon")
     west = lax.rem(lon + 7, 8)
@@ -271,6 +273,7 @@
         return carry
 
     lax.fori_loop(0, 8, level_step, 0)
+    done_ref[...] = jnp.zeros((8, 128), F32)
 
 
 def finish_kernel(points, code_ref, land_ref, back_ref, from_north_ref, from_south_ref, heat_ref, depth_ref,
@@ -301,7 +304,7 @@
             out_ref[t, 0, :, cols] = step_ref[t, 0, :, cols] + gain * force
 
 
-def call(kernel, name, in_specs, out_shape, out_specs, scratch=(), **more):
+def call(kernel, name, in_specs, out_shape, out_specs, scratch=(), limit=SMALL, **more):
     return pl.pallas_call(
         kernel,
         out_shape=out_shape,
@@ -309,6 +312,7 @@
         out_specs=out_specs,
         scratch_shapes=list(scratch),
         name=name,
+        compiler_params=pltpu.CompilerParams(vmem_limit_bytes=limit),
         **more,
     )
 
@@ -355,6 +359,7 @@
         (shape(flat, BF16), shape((48,), jnp.int32)),
         (VMEM, SMEM),
         [pltpu.SMEM((24,), jnp.int32)],
+        limit=60 * 1024 * 1024,
     )(o2a_dest, land_mask, ocean_state, tracers_l, east_velocity, diffusivity, depth_levels)
 
     source_off = (lat - a2o_source // lons + 1) % lats
@@ -392,12 +397,12 @@
     )(place, came, low, high, atm_state, exchange_coef, sunlight, mixing)
     back = turn(backward)
 
-    step = call(
+    step, done = call(
         functools.partial(stencil_kernel, lats),
         "stencil",
-        [SMEM] + [VMEM] * 9,
-        shape((32, 16, 384), F32),
-        VMEM,
+        [SMEM] + [VMEM] * 9 + [ANY],
+        (shape((32, 16, 384), F32), shape((8, 128), F32)),
+        (VMEM, VMEM),
         [pltpu.VMEM((2, 56, 384), F32), pltpu.VMEM((2, 32, 384), F32), pltpu.VMEM((5, 16, 384), F32)],
         cost_estimate=pl.CostEstimate(flops=8000000, bytes_accessed=3000000, transcendentals=0),
     )(
@@ -411,15 +416,16 @@
         diffusivity,
         cross_diffusivity,
         depth_levels,
+        backward,
     )
 
     to_south, to_north, heat = call(
         functools.partial(split_kernel, lats),
         "split",
-        [VMEM],
+        [VMEM, ANY],
         (shape((48, 8, 128), BF16), shape((48, 8, 128), BF16), shape((lats, 1, 128), F32)),
         (VMEM, VMEM, VMEM),
-    )(back)
+    )(back, done)
     heat = lax.all_to_all(heat, "lat", 0, 0, tiled=True)
     back_north = lax.ppermute(to_south, "lat", south_pairs)
     back_south = lax.ppermute(to_north, "lat", north_pairs)

time: 88.2 us -> 82.8 us (0.939)
  blocking collectives: 13.5 us -> 0 us
  waiting for transfers between devices: 10.2 us -> 18.5 us
  starting transfers between devices: 43.8 us -> 49.3 us
  Pallas kernels: 15.6 us -> 11.3 us
  local copies, waits for them, and re-layouts: 2.7 us -> 1.3 us
    all_to_all x1 -> x0, blocking collectives: 13.5 us -> none  [turn(): return lax.all_to_all(values, 'lon', 0, 0, tiled=True).reshape(flat)]
    all_to_all x1 -> x2, starting transfers between devices: 13.9 us -> 19.4 us  [turn(): return lax.all_to_all(values, 'lon', 0, 0, tiled=True).reshape(flat)]
    ppermute x1, waiting for transfers between devices: 2.11 us -> 6.75 us  [shards(): back_south = lax.ppermute(to_north, 'lat', north_pairs)]
    all_to_all x1 -> x2, waiting for transfers between devices: 6.29 us -> 9.79 us  [turn(): return lax.all_to_all(values, 'lon', 0, 0, tiled=True).reshape(flat)]
    pallas_call x1, Pallas kernels: 2.12 us -> 0.66 us  [shards(): call(rows_kernel, 'rows', [SMEM, VMEM, VMEM, VMEM, VMEM, VMEM], (row_shap...]
    unnamed x18 -> x28, local copies, waits for them, and re-layouts: 2.7 us -> 1.3 us
    pallas_call x1, Pallas kernels: 4.64 us -> 3.61 us  [shards(): call(functools.partial(stencil_kernel, lats), 'stencil', [SMEM] + [VMEM]...]
    pallas_call x1, Pallas kernels: 1.66 us -> 0.66 us  [shards(): call(functools.partial(split_kernel, lats), 'split', [VMEM, ANY], (shape(...]
  transfers between devices with their start and end apart: 6 -> 7, of which waited for: 4 -> 5; matrix products, arithmetic and copies ran while one was open for 1% -> 0% of each run, Pallas kernels for 5% -> 4%
where the time goes in v2:
time: 82.8 us; the launch traced here: 81.5 us
  starting transfers between devices  49.3 us (60%)
  waiting for transfers between devices  18.5 us (22%)
  Pallas kernels  11.3 us (14%)
  local copies, waits for them, and re-layouts  1.3 us (2%)
    all_to_all x2, starting transfers between devices, turn(): return lax.all_to_all(values, 'lon', 0, 0, tiled=True).reshape(flat)  19.4 us
    all_to_all x1, starting transfers between devices, shards(): heat = lax.all_to_all(heat, 'lat', 0, 0, tiled=True)  10.4 us
    all_to_all x2, waiting for transfers between devices, turn(): return lax.all_to_all(values, 'lon', 0, 0, tiled=True).reshape(flat)  9.79 us
    ppermute x1, starting transfers between devices, shards(): high = lax.ppermute(down, 'lat', south_pairs)  9.14 us
    ppermute x1, waiting for transfers between devices, shards(): back_south = lax.ppermute(to_north, 'lat', north_pairs)  6.75 us
    ppermute x1, starting transfers between devices, shards(): back_north = lax.ppermute(to_south, 'lat', south_pairs)  6.55 us
    pallas_call x1, Pallas kernels, shards(): call(functools.partial(stencil_kernel, lats), 'stencil', [SMEM] + [VMEM]...  3.61 us
    pallas_call x1, Pallas kernels, shards(): call(functools.partial(pack_kernel, lats), 'pack', [SMEM, SMEM, VMEM, VME...  2.48 us
  transfers between devices with their start and end apart: 7, of which 5 were waited for; matrix products, arithmetic and copies ran while one was open for 0% of the time, Pallas kernels for 4%

profile of v2, /device:TPU:1, one launch (start us, length us, event | category | flops | bytes accessed | tf_op | source)
XLA Modules:
  0.0 81.5 jit_solution(6734283418367282789)
XLA Ops:
  0.6 0.0 copy-start
  0.6 2.5 %pack.1 = (bf16[160,8,128]{2,1,0:T(8,128)(2,1)}, s32[48]{0:T(128)}) custom-call(s32[48]{0:T(128)} %dest_ref.1, s32[48]{0:T(128)} %land_ref.7, bf16[48,8,128]{2,1,0:T(8,128)(2,1)} %state_ref.1, f32[32,16,384]{2,1,0:T(8,128)} %bitcast.6, f32[8,16,384]{2,1,0:T(8,128)} %east_ref.3, f32[8,16,384]{2,1,0:T(8,128)} %kappa_ref.5, s32[16,384]{1,0:T(8,128)} %depth_ref.7), custom_call_target="tpu_custom_call" | custom-call | tf_op jit(solution)/shard_map/pack/pallas_call | solution.py:355
  3.1 0.0 copy-start.1
  3.1 0.0 copy-start.3
  3.2 0.0 copy-start.4
  3.2 14.0 %all-to-all-start = ((bf16[8,20,8,128]{3,2,1,0:T(8,128)(2,1)}), bf16[8,20,8,128]{3,2,1,0:T(8,128)(2,1)S(1)}, u32[]{:S(2)}, u32[]{:S(2)}) async-start(bf16[8,20,8,128]{3,2,1,0:T(8,128)(2,1)} %bitcast.15), calls=%async_computation | async-start | bytes 655360 | tf_op jit(solution)/shard_map/all_to_all | solution.py:351
  17.2 0.0 copy-start.12
  17.2 0.0 copy-start.13
  17.2 0.7 copy-done.12
  17.8 0.0 copy-done.13
  17.8 0.2 convert_reduce_fusion
  18.0 0.0 copy-start.9
  18.0 6.3 %all-to-all-done = bf16[8,20,8,128]{3,2,1,0:T(8,128)(2,1)S(1)} async-done(((bf16[8,20,8,128]{3,2,1,0:T(8,128)(2,1)}), bf16[8,20,8,128]{3,2,1,0:T(8,128)(2,1)S(1)}, u32[]{:S(2)}, u32[]{:S(2)}) %all-to-all-start) | async-done | bytes 327712 | tf_op jit(solution)/shard_map/all_to_all | solution.py:351
  24.3 0.0 copy-done
  24.3 0.0 copy-done.1
  24.3 0.0 copy-done.3
  24.3 0.0 copy-done.4
  24.3 0.0 copy-done.9
  24.3 0.0 copy-start.5
  24.3 0.0 copy-start.7
  24.4 0.0 copy-start.8
  24.4 0.7 rows.1
  25.0 0.0 copy-start.10
  25.0 1.9 %collective-permute-start = (bf16[69,8,128]{2,1,0:T(8,128)(2,1)S(1)}, bf16[69,8,128]{2,1,0:T(8,128)(2,1)S(1)}, u32[]{:S(2)}, u32[]{:S(2)}) collective-permute-start(bf16[69,8,128]{2,1,0:T(8,128)(2,1)S(1)} %get-tuple-element.15), channel_id=1, source_target_pairs={{0,8},{8,16},{16,24},{24,32},{32,40},{40,48},{48,56},{56,64},{64,7... | collective-permute-start | bytes 423944 | tf_op jit(solution)/shard_map/ppermute | solution.py:387
  27.0 9.1 %collective-permute-start.1 = (bf16[69,8,128]{2,1,0:T(8,128)(2,1)S(1)}, bf16[69,8,128]{2,1,0:T(8,128)(2,1)S(1)}, u32[]{:S(2)}, u32[]{:S(2)}) collective-permute-start(bf16[69,8,128]{2,1,0:T(8,128)(2,1)S(1)} %get-tuple-element.16), channel_id=1, source_target_pairs={{8,0},{16,8},{24,16},{32,24},{40,32},{48,40},{56,48},{64,56},{72,6... | collective-permute-start | bytes 423944 | tf_op jit(solution)/shard_map/ppermute | solution.py:388
  36.1 1.0 %collective-permute-done.low_ref = bf16[69,8,128]{2,1,0:T(8,128)(2,1)S(1)} collective-permute-done((bf16[69,8,128]{2,1,0:T(8,128)(2,1)S(1)}, bf16[69,8,128]{2,1,0:T(8,128)(2,1)S(1)}, u32[]{:S(2)}, u32[]{:S(2)}) %collective-permute-start) | collective-permute-done | bytes 141344 | tf_op jit(solution)/shard_map/ppermute | solution.py:387
  37.1 1.0 %collective-permute-done.1.high_ref = bf16[69,8,128]{2,1,0:T(8,128)(2,1)S(1)} collective-permute-done((bf16[69,8,128]{2,1,0:T(8,128)(2,1)S(1)}, bf16[69,8,128]{2,1,0:T(8,128)(2,1)S(1)}, u32[]{:S(2)}, u32[]{:S(2)}) %collective-permute-start.1) | collective-permute-done | bytes 141344 | tf_op jit(solution)/shard_map/ppermute | solution.py:388
  38.1 0.0 copy-done.5
  38.1 0.0 copy-done.7
  38.2 0.0 copy-done.8
  38.2 0.0 copy-done.10
  38.2 2.0 %couple.1.after_ref = bf16[160,8,128]{2,1,0:T(8,128)(2,1)} custom-call(s32[48]{0:T(128)S(1)} %fusion.2.place_ref, bf16[160,8,128]{2,1,0:T(8,128)(2,1)S(1)} %bitcast.10, bf16[69,8,128]{2,1,0:T(8,128)(2,1)S(1)} %collective-permute-done.low_ref, bf16[69,8,128]{2,1,0:T(8,128)(2,1)S(1)} %collective-permute-done.1.high_ref, f32[48,8,128]{2,1,0:T(8,128)S(1)} %copy-done.5, ...), custom_call_target="tpu_custom_call" | custom-call | tf_op jit(solution)/shard_map/couple/pallas_call | solution.py:390
  40.1 0.0 copy-start.2
  40.1 0.0 copy-start.6
  40.1 5.4 %all-to-all-start.1 = ((bf16[8,20,8,128]{3,2,1,0:T(8,128)(2,1)}), bf16[8,20,8,128]{3,2,1,0:T(8,128)(2,1)S(1)}, u32[]{:S(2)}, u32[]{:S(2)}) async-start(bf16[8,20,8,128]{3,2,1,0:T(8,128)(2,1)} %bitcast.3), calls=%async_computation.1 | async-start | bytes 655360 | tf_op jit(solution)/shard_map/all_to_all | solution.py:351
  45.6 0.0 copy-done.2
  45.6 0.0 copy-done.6
  45.6 3.6 %stencil.1 = (f32[32,16,384]{2,1,0:T(8,128)}, f32[8,128]{1,0:T(8,128)S(1)}) custom-call(s32[48]{0:T(128)S(1)} %copy-done.9, bf16[160,8,128]{2,1,0:T(8,128)(2,1)S(1)} %bitcast.11, bf16[69,8,128]{2,1,0:T(8,128)(2,1)S(1)} %collective-permute-done.low_ref, bf16[69,8,128]{2,1,0:T(8,128)(2,1)S(1)} %collective-permute-done.1.high_ref, f32[32,16,384]{2,1,0:T(8,128)S(1)} %bitcast.8, ...), custom_call_target="tpu_custom_call" | custom-call | flops 8000000 | bytes 3000000 | tf_op jit(solution)/shard_map/stencil/pallas_call | solution.py:400
  49.2 3.5 %all-to-all-done.1 = bf16[8,20,8,128]{3,2,1,0:T(8,128)(2,1)S(1)} async-done(((bf16[8,20,8,128]{3,2,1,0:T(8,128)(2,1)}), bf16[8,20,8,128]{3,2,1,0:T(8,128)(2,1)S(1)}, u32[]{:S(2)}, u32[]{:S(2)}) %all-to-all-start.1) | async-done | bytes 327712 | tf_op jit(solution)/shard_map/all_to_all | solution.py:351
  52.7 0.7 split.1
  53.4 10.4 %all-to-all-start.2 = ((f32[96,1,128]{2,1,0:T(1,128)}), f32[96,1,128]{2,1,0:T(1,128)S(1)}, u32[]{:S(2)}, u32[]{:S(2)}) async-start(f32[96,1,128]{2,1,0:T(1,128)} %get-tuple-element.20), calls=%async_computation.2 | async-start | bytes 98304 | tf_op jit(solution)/shard_map/all_to_all | solution.py:429
  63.8 6.6 %collective-permute-start.2 = (bf16[48,8,128]{2,1,0:T(8,128)(2,1)S(1)}, bf16[48,8,128]{2,1,0:T(8,128)(2,1)S(1)}, u32[]{:S(2)}, u32[]{:S(2)}) collective-permute-start(bf16[48,8,128]{2,1,0:T(8,128)(2,1)S(1)} %get-tuple-element.18), channel_id=1, source_target_pairs={{8,0},{16,8},{24,16},{32,24},{40,32},{48,40},{56,48},{64,56},{72,6... | collective-permute-start | bytes 294920 | tf_op jit(solution)/shard_map/ppermute | solution.py:430
  70.3 1.9 %collective-permute-start.3 = (bf16[48,8,128]{2,1,0:T(8,128)(2,1)S(1)}, bf16[48,8,128]{2,1,0:T(8,128)(2,1)S(1)}, u32[]{:S(2)}, u32[]{:S(2)}) collective-permute-start(bf16[48,8,128]{2,1,0:T(8,128)(2,1)S(1)} %get-tuple-element.19), channel_id=1, source_target_pairs={{0,8},{8,16},{16,24},{24,32},{32,40},{40,48},{48,56},{56,64},{64,7... | collective-permute-start | bytes 294920 | tf_op jit(solution)/shard_map/ppermute | solution.py:431
  72.3 0.0 collective-permute-done.2.from_north_ref
  72.3 6.8 %collective-permute-done.3.from_south_ref = bf16[48,8,128]{2,1,0:T(8,128)(2,1)S(1)} collective-permute-done((bf16[48,8,128]{2,1,0:T(8,128)(2,1)S(1)}, bf16[48,8,128]{2,1,0:T(8,128)(2,1)S(1)}, u32[]{:S(2)}, u32[]{:S(2)}) %collective-permute-start.3) | collective-permute-done | bytes 98336 | tf_op jit(solution)/shard_map/ppermute | solution.py:431
  79.0 0.0 all-to-all-done.2.heat_ref
  79.0 0.6 copy-done.11
  79.6 1.9 %finish.1 = (bf16[48,8,128]{2,1,0:T(8,128)(2,1)}, f32[4,8,16,384]{3,2,1,0:T(8,128)}) custom-call(s32[48]{0:T(128)S(1)} %copy-done.11, s32[48]{0:T(128)S(1)} %copy-done.9, bf16[160,8,128]{2,1,0:T(8,128)(2,1)S(1)} %bitcast.13, bf16[48,8,128]{2,1,0:T(8,128)(2,1)S(1)} %collective-permute-done.2.from_north_ref, ...), custom_call_target="tpu_custom_call", output_to_operand_aliasing={{1}: (7, {})} | custom-call | tf_op jit(solution)/shard_map/finish/pallas_call | solution.py:435
  (2 shorter events, 0.0 us)
Async XLA Ops:
  0.6 23.7 %copy-start = (f32[4,8,16,384]{3,2,1,0:T(8,128)S(1)}, f32[4,8,16,384]{3,2,1,0:T(8,128)}, u32[]{:S(2)}) copy-start(f32[4,8,16,384]{3,2,1,0:T(8,128)} %param.16) | copy-start | bytes 2359300
  3.1 21.2 %copy-start.1 = (f32[8,16,384]{2,1,0:T(8,128)S(1)}, f32[8,16,384]{2,1,0:T(8,128)}, u32[]{:S(2)}) copy-start(f32[8,16,384]{2,1,0:T(8,128)} %kappa_ref.5) | copy-start | bytes 589828
  3.1 21.2 %copy-start.3 = (f32[8,16,384]{2,1,0:T(8,128)S(1)}, f32[8,16,384]{2,1,0:T(8,128)}, u32[]{:S(2)}) copy-start(f32[8,16,384]{2,1,0:T(8,128)} %north_ref.3) | copy-start | bytes 589828
  3.2 21.2 %copy-start.4 = (s32[16,384]{1,0:T(8,128)S(1)}, s32[16,384]{1,0:T(8,128)}, u32[]{:S(2)}) copy-start(s32[16,384]{1,0:T(8,128)} %depth_ref.7) | copy-start | bytes 73732
  3.2 21.1 %all-to-all-start = ((bf16[8,20,8,128]{3,2,1,0:T(8,128)(2,1)}), bf16[8,20,8,128]{3,2,1,0:T(8,128)(2,1)S(1)}, u32[]{:S(2)}, u32[]{:S(2)}) async-start(bf16[8,20,8,128]{3,2,1,0:T(8,128)(2,1)} %bitcast.15), calls=%async_computation | async-start | bytes 655360 | tf_op jit(solution)/shard_map/all_to_all | solution.py:351
  17.2 0.7 copy-start.12
  17.2 0.7 copy-start.13
  18.0 6.3 %copy-start.9 = (s32[48]{0:T(128)S(1)}, s32[48]{0:T(128)}, u32[]{:S(2)}) copy-start(s32[48]{0:T(128)} %land_ref.7) | copy-start | bytes 580
  24.3 13.8 %copy-start.5 = (f32[48,8,128]{2,1,0:T(8,128)S(1)}, f32[48,8,128]{2,1,0:T(8,128)}, u32[]{:S(2)}) copy-start(f32[48,8,128]{2,1,0:T(8,128)} %atm_ref.1) | copy-start | bytes 589828
  24.3 13.8 %copy-start.7 = (f32[48,128]{1,0:T(8,128)S(1)}, f32[48,128]{1,0:T(8,128)}, u32[]{:S(2)}) copy-start(f32[48,128]{1,0:T(8,128)} %coef_ref.1) | copy-start | bytes 73732
  24.4 13.8 %copy-start.8 = (f32[48,128]{1,0:T(8,128)S(1)}, f32[48,128]{1,0:T(8,128)}, u32[]{:S(2)}) copy-start(f32[48,128]{1,0:T(8,128)} %sun_ref.1) | copy-start | bytes 73732
  25.0 13.1 %copy-start.10 = (f32[8,8]{1,0:T(8,128)S(1)}, f32[8,8]{1,0:T(8,128)}, u32[]{:S(2)}) copy-start(f32[8,8]{1,0:T(8,128)} %mixing_ref.1) | copy-start | bytes 772
  25.0 12.1 %collective-permute-start = (bf16[69,8,128]{2,1,0:T(8,128)(2,1)S(1)}, bf16[69,8,128]{2,1,0:T(8,128)(2,1)S(1)}, u32[]{:S(2)}, u32[]{:S(2)}) collective-permute-start(bf16[69,8,128]{2,1,0:T(8,128)(2,1)S(1)} %get-tuple-element.15), channel_id=1, source_target_pairs={{0,8},{8,16},{16,24},{24,32},{32,40},{40,48},{48,56},{56,64},{64,7... | collective-permute-start | bytes 423944 | tf_op jit(solution)/shard_map/ppermute | solution.py:387
  27.0 11.2 %collective-permute-start.1 = (bf16[69,8,128]{2,1,0:T(8,128)(2,1)S(1)}, bf16[69,8,128]{2,1,0:T(8,128)(2,1)S(1)}, u32[]{:S(2)}, u32[]{:S(2)}) collective-permute-start(bf16[69,8,128]{2,1,0:T(8,128)(2,1)S(1)} %get-tuple-element.16), channel_id=1, source_target_pairs={{8,0},{16,8},{24,16},{32,24},{40,32},{48,40},{56,48},{64,56},{72,6... | collective-permute-start | bytes 423944 | tf_op jit(solution)/shard_map/ppermute | solution.py:388
  40.1 5.5 %copy-start.2 = (f32[8,16,384]{2,1,0:T(8,128)S(1)}, f32[8,16,384]{2,1,0:T(8,128)}, u32[]{:S(2)}) copy-start(f32[8,16,384]{2,1,0:T(8,128)} %east_ref.3) | copy-start | bytes 589828
  40.1 5.5 %copy-start.6 = (f32[8,16,384]{2,1,0:T(8,128)S(1)}, f32[8,16,384]{2,1,0:T(8,128)}, u32[]{:S(2)}) copy-start(f32[8,16,384]{2,1,0:T(8,128)} %cross_ref.1) | copy-start | bytes 589828
  40.1 12.6 %all-to-all-start.1 = ((bf16[8,20,8,128]{3,2,1,0:T(8,128)(2,1)}), bf16[8,20,8,128]{3,2,1,0:T(8,128)(2,1)S(1)}, u32[]{:S(2)}, u32[]{:S(2)}) async-start(bf16[8,20,8,128]{3,2,1,0:T(8,128)(2,1)} %bitcast.3), calls=%async_computation.1 | async-start | bytes 655360 | tf_op jit(solution)/shard_map/all_to_all | solution.py:351
  53.4 25.6 %all-to-all-start.2 = ((f32[96,1,128]{2,1,0:T(1,128)}), f32[96,1,128]{2,1,0:T(1,128)S(1)}, u32[]{:S(2)}, u32[]{:S(2)}) async-start(f32[96,1,128]{2,1,0:T(1,128)} %get-tuple-element.20), calls=%async_computation.2 | async-start | bytes 98304 | tf_op jit(solution)/shard_map/all_to_all | solution.py:429
  63.8 8.5 %collective-permute-start.2 = (bf16[48,8,128]{2,1,0:T(8,128)(2,1)S(1)}, bf16[48,8,128]{2,1,0:T(8,128)(2,1)S(1)}, u32[]{:S(2)}, u32[]{:S(2)}) collective-permute-start(bf16[48,8,128]{2,1,0:T(8,128)(2,1)S(1)} %get-tuple-element.18), channel_id=1, source_target_pairs={{8,0},{16,8},{24,16},{32,24},{40,32},{48,40},{56,48},{64,56},{72,6... | collective-permute-start | bytes 294920 | tf_op jit(solution)/shard_map/ppermute | solution.py:430
  70.3 8.7 %collective-permute-start.3 = (bf16[48,8,128]{2,1,0:T(8,128)(2,1)S(1)}, bf16[48,8,128]{2,1,0:T(8,128)(2,1)S(1)}, u32[]{:S(2)}, u32[]{:S(2)}) collective-permute-start(bf16[48,8,128]{2,1,0:T(8,128)(2,1)S(1)} %get-tuple-element.19), channel_id=1, source_target_pairs={{0,8},{8,16},{16,24},{24,32},{32,40},{40,48},{48,56},{56,64},{64,7... | collective-permute-start | bytes 294920 | tf_op jit(solution)/shard_map/ppermute | solution.py:431
  79.0 0.6 copy-start.11

commit v3 on v2

--- a/solution.py
+++ b/solution.py
@@ -16,6 +16,7 @@
 VMEM = pl.BlockSpec(memory_space=pltpu.VMEM)
 SMEM = pl.BlockSpec(memory_space=pltpu.SMEM)
 ANY = pl.BlockSpec(memory_space=pl.ANY)
+HBM = pl.BlockSpec(memory_space=pltpu.HBM)
 SMALL = 16 * 1024 * 1024
 
 
@@ -35,13 +36,35 @@
     return out
 
 
-def pack_kernel(lats, dest_ref, land_ref, state_ref, tracer_ref, east_ref, kappa_ref, depth_ref,
-                out_ref, code_ref, count_ref):
+def pack_kernel(lats, dest_hbm, land_hbm, state_hbm, tracer_hbm, east_hbm, kappa_hbm, depth_hbm,
+                out_ref, code_ref, count_ref, dest_ref, land_ref, state_ref, tracer_ref, east_ref,
+                kappa_ref, depth_ref, sems):
+    first, last = pl.ds(0, 128), pl.ds(256, 128)
+    copies = [
+        pltpu.make_async_copy(source, target, sems.at[n])
+        for n, (source, target) in enumerate(
+            (
+                (dest_hbm, dest_ref),
+                (land_hbm, land_ref),
+                (state_hbm, state_ref),
+                (depth_hbm, depth_ref),
+                (tracer_hbm.at[:, :, last], tracer_ref.at[0]),
+                (tracer_hbm.at[:, :, first], tracer_ref.at[1]),
+                (kappa_hbm.at[:, :, last], kappa_ref.at[0]),
+                (kappa_hbm.at[:, :, first], kappa_ref.at[1]),
+                (east_hbm.at[:, :, last], east_ref),
+            )
+        )
+    ]
+    for copy in copies:
+        copy.start()
     lat = lax.axis_index("lat")
     lon = lax.axis_index("lon")
     lons = 8
     for i in range(24):
         count_ref[i] = 0
+    for copy in copies[:3]:
+        copy.wait()
     for t in range(48):
         dest = dest_ref[t]
         off = lax.shift_right_logical(dest, 3) - lat + 1
@@ -54,15 +77,17 @@
         value = state_ref[t].astype(F32)
         value = jnp.where(land_ref[t] > 0, value, LAND)
         out_ref[dlon * SLOTS + off * PAIR + rank] = value.astype(BF16)
+    for copy in copies[3:]:
+        copy.wait()
     lanes = iota((16, 128), 1)
-    for block, lane, shift in ((2, 127, 1), (0, 0, lons - 1)):
+    for side, block, lane, shift in ((0, 2, 127, 1), (1, 0, 0, lons - 1)):
         packed = jnp.zeros((16, 128), F32)
         for i in range(32):
-            packed = jnp.where(lanes == i, block_of(tracer_ref, block)[i][:, lane : lane + 1], packed)
+            packed = jnp.where(lanes == i, tracer_ref[side, i][:, lane : lane + 1], packed)
         for i in range(8):
-            if block == 2:
-                packed = jnp.where(lanes == 32 + i, block_of(east_ref, block)[i][:, lane : lane + 1], packed)
-            packed = jnp.where(lanes == 40 + i, block_of(kappa_ref, block)[i][:, lane : lane + 1], packed)
+            if side == 0:
+                packed = jnp.where(lanes == 32 + i, east_ref[i][:, lane : lane + 1], packed)
+            packed = jnp.where(lanes == 40 + i, kappa_ref[side, i][:, lane : lane + 1], packed)
         bottom = block_of(depth_ref, block)[...].astype(F32) * tile_column(land_ref, block)
         packed = jnp.where(lanes == 48, bottom[:, lane : lane + 1], packed)
         target = lax.rem(lon + shift, lons)
@@ -70,7 +95,24 @@
         out_ref[target * SLOTS + 19] = packed[8:].astype(BF16)
 
 
-def rows_kernel(land_ref, came_ref, tracer_ref, north_ref, kappa_ref, depth_ref, up_ref, down_ref):
+def by_parity(body, cross, inner):
+    odd = lax.rem(lax.axis_index("lat"), 2)
+
+    @pl.when(odd == 1)
+    def _():
+        body(cross, inner)
+
+    @pl.when(odd == 0)
+    def _():
+        body(inner, cross)
+
+
+def rows_kernel(land_ref, came_ref, tracer_ref, north_ref, kappa_ref, depth_ref, cross_ref, inner_ref):
+    inputs = (land_ref, came_ref, tracer_ref, north_ref, kappa_ref, depth_ref)
+    by_parity(functools.partial(fill_rows, *inputs), cross_ref, inner_ref)
+
+
+def fill_rows(land_ref, came_ref, tracer_ref, north_ref, kappa_ref, depth_ref, up_ref, down_ref):
     lon = lax.axis_index("lon")
     west = lax.rem(lon + 7, 8)
     east = lax.rem(lon + 1, 8)
@@ -101,8 +143,10 @@
             out_ref[48 + 18 + j] = last.astype(BF16)
 
 
-def couple_kernel(place_ref, came_ref, low_ref, high_ref, atm_ref, coef_ref, sun_ref, mixing_ref,
+def couple_kernel(place_ref, came_ref, cross_ref, inner_ref, atm_ref, coef_ref, sun_ref, mixing_ref,
                   out_ref, got_ref):
+    odd = lax.rem(lax.axis_index("lat"), 2)
+    cross_off = jnp.where(odd == 1, 0, 2)
     total = jnp.zeros((8, 128), F32)
     for q in range(48):
         code = place_ref[q]
@@ -111,9 +155,9 @@
         off = lax.shift_right_logical(code, 6)
         at = slon * PAIR + rank
         own = came_ref[slon * SLOTS + PAIR + rank].astype(F32)
-        low = low_ref[at].astype(F32)
-        high = high_ref[at].astype(F32)
-        value = jnp.where(off == 1, own, jnp.where(off == 2, low, high))
+        cross = cross_ref[at].astype(F32)
+        inner = inner_ref[at].astype(F32)
+        value = jnp.where(off == 1, own, jnp.where(off == cross_off, cross, inner))
         got_ref[q] = value
         total = total + coef_ref[q : q + 1, :] * jnp.where(value < LAND_TEST, value, 0.0)
     weight = jnp.sum(jnp.sum(coef_ref[...], axis=0, keepdims=True), axis=1, keepdims=True)
@@ -149,19 +193,23 @@
         out_ref[s * SLOTS + 18] = parts.astype(BF16)
 
 
-def split_kernel(lats, back_ref, done_ref, to_south_ref, to_north_ref, heat_ref):
+def split_kernel(lats, back_ref, done_ref, cross_ref, inner_ref, heat_ref):
+    odd = lax.rem(lax.axis_index("lat"), 2)
+    cross_at = jnp.where(odd == 1, 0, 12)
+    inner_at = 12 - cross_at
     heat = jnp.zeros((8, 128), F32)
     for s in range(8):
         heat = heat + back_ref[s * SLOTS + 18].astype(F32)
         for k in range(PAIR):
-            to_south_ref[s * PAIR + k] = back_ref[s * SLOTS + 12 + k]
-            to_north_ref[s * PAIR + k] = back_ref[s * SLOTS + k]
+            cross_ref[s * PAIR + k] = back_ref[s * SLOTS + cross_at + k]
+            inner_ref[s * PAIR + k] = back_ref[s * SLOTS + inner_at + k]
     row = jnp.sum(heat, axis=0, keepdims=True)
     heat_ref[...] = jnp.broadcast_to(row[None], (lats, 1, 128))
 
 
-def stencil_kernel(lats, land_ref, came_ref, low_ref, high_ref, tracer_ref, east_ref, north_ref,
-                   kappa_ref, cross_ref, depth_ref, after_ref, out_ref, done_ref, rows_ref, diag_ref, bottom_ref):
+def stencil_kernel(lats, land_ref, came_ref, cross_halo_ref, inner_halo_ref, tracer_ref, east_ref, north_ref,
+                   kappa_ref, cross_ref, depth_ref, code_ref, after_ref, out_ref, top_ref, done_ref, rows_ref,
+                   diag_ref, bottom_ref):
     lat = lax.axis_index("lat")
     lon = lax.axis_index("lon")
     west = lax.rem(lon + 7, 8)
@@ -192,14 +240,18 @@
         return jnp.where(at_north, row, pltpu.roll(v, 15, 0))
 
     col_west, col_east = columns_of(west), columns_of(east)
-    for side, ref in enumerate((low_ref, high_ref)):
-        inside = jnp.where(lat == (0, lats - 1)[side], 0.0, 1.0)
-        for k in range(7):
-            for j in range(3):
-                tile = ref[48 + 3 * k + j].astype(F32)
-                if k == 6:
-                    tile = jnp.where(sub8 == 0, tile * inside, tile)
-                rows_ref[side, 8 * k : 8 * k + 8, 128 * j : 128 * j + 128] = tile
+
+    def unpack_rows(high_ref, low_ref):
+        for side, ref in enumerate((low_ref, high_ref)):
+            inside = jnp.where(lat == (0, lats - 1)[side], 0.0, 1.0)
+            for k in range(7):
+                for j in range(3):
+                    tile = ref[48 + 3 * k + j].astype(F32)
+                    if k == 6:
+                        tile = jnp.where(sub8 == 0, tile * inside, tile)
+                    rows_ref[side, 8 * k : 8 * k + 8, 128 * j : 128 * j + 128] = tile
+
+    by_parity(unpack_rows, cross_halo_ref, inner_halo_ref)
     for j in range(3):
         cols = slice(128 * j, 128 * j + 128)
         bottom_ref[0, :, cols] = depth_ref[:, cols].astype(F32) * tile_column(land_ref, j)
@@ -273,11 +325,16 @@
         return carry
 
     lax.fori_loop(0, 8, level_step, 0)
-    done_ref[...] = jnp.zeros((8, 128), F32)
-
-
-def finish_kernel(points, code_ref, land_ref, back_ref, from_north_ref, from_south_ref, heat_ref, depth_ref,
-                  step_ref, flux_ref, out_ref, wide_ref):
+    for t in range(4):
+        top_ref[t] = out_ref[8 * t]
+    for t in range(48):
+        done_ref[t] = code_ref[t]
+
+
+def finish_kernel(points, code_ref, land_ref, back_ref, cross_ref, inner_ref, heat_ref, depth_ref,
+                  top_ref, step_hbm, flux_hbm, out_hbm, flux_ref, sum_ref, wide_ref, sems):
+    odd = lax.rem(lax.axis_index("lat"), 2)
+    cross_off = jnp.where(odd == 1, 2, 0)
     for t in range(48):
         code = code_ref[t]
         rank = lax.bitwise_and(code, 7)
@@ -285,12 +342,14 @@
         off = lax.shift_right_logical(code, 6)
         at = dlon * PAIR + rank
         own = back_ref[dlon * SLOTS + PAIR + rank].astype(F32)
-        north = from_north_ref[at].astype(F32)
-        south = from_south_ref[at].astype(F32)
-        value = jnp.where(off == 1, own, jnp.where(off == 2, north, south))
+        cross = cross_ref[at].astype(F32)
+        inner = inner_ref[at].astype(F32)
+        value = jnp.where(off == 1, own, jnp.where(off == cross_off, cross, inner))
         value = jnp.where(land_ref[t] > 0, value, 0.0)
         flux_ref[t] = value.astype(BF16)
         wide_ref[8 * t : 8 * t + 8, :] = value
+    flux_copy = pltpu.make_async_copy(flux_ref, flux_hbm, sems.at[0])
+    flux_copy.start()
     heat = jnp.sum(jnp.sum(heat_ref[...], axis=0), axis=1, keepdims=True)
     correction = heat / points
     for j in range(3):
@@ -301,7 +360,11 @@
             force = wide_ref[pl.ds(8 * j + t, 16, stride=24), :]
             if t == 0:
                 force = force - correction
-            out_ref[t, 0, :, cols] = step_ref[t, 0, :, cols] + gain * force
+            sum_ref[t, :, cols] = top_ref[t, :, cols] + gain * force
+    top_copy = pltpu.make_async_copy(sum_ref, out_hbm.at[:, 0], sems.at[1])
+    top_copy.start()
+    flux_copy.wait()
+    top_copy.wait()
 
 
 def call(kernel, name, in_specs, out_shape, out_specs, scratch=(), limit=SMALL, **more):
@@ -342,8 +405,11 @@
     lats = lax.axis_size("lat")
     lons = lax.axis_size("lon")
     lat = lax.axis_index("lat")
-    north_pairs = [(i, (i + 1) % lats) for i in range(lats)]
-    south_pairs = [(j, i) for i, j in north_pairs]
+    cross_pairs, inner_pairs = [], []
+    for i in range(0, lats, 2):
+        north, south = i + 1, (i + lats - 1) % lats
+        inner_pairs += [(i, north), (north, i)]
+        cross_pairs += [(i, south), (south, i)]
     flat = (8 * SLOTS, 8, 128)
 
     def turn(values):
@@ -355,10 +421,20 @@
     outgoing, code = call(
         functools.partial(pack_kernel, lats),
         "pack",
-        [SMEM, SMEM, VMEM, VMEM, VMEM, VMEM, VMEM],
+        [HBM] * 7,
         (shape(flat, BF16), shape((48,), jnp.int32)),
         (VMEM, SMEM),
-        [pltpu.SMEM((24,), jnp.int32)],
+        [
+            pltpu.SMEM((24,), jnp.int32),
+            pltpu.SMEM((48,), jnp.int32),
+            pltpu.SMEM((48,), jnp.int32),
+            pltpu.VMEM((48, 8, 128), BF16),
+            pltpu.VMEM((2, 32, 16, 128), F32),
+            pltpu.VMEM((8, 16, 128), F32),
+            pltpu.VMEM((2, 8, 16, 128), F32),
+            pltpu.VMEM((16, 384), jnp.int32),
+            pltpu.SemaphoreType.DMA((9,)),
+        ],
         limit=60 * 1024 * 1024,
     )(o2a_dest, land_mask, ocean_state, tracers_l, east_velocity, diffusivity, depth_levels)
 
@@ -370,7 +446,7 @@
 
     came = turn(outgoing)
     row_shape = shape((69, 8, 128), BF16)
-    up, down = call(
+    cross, inner = call(
         rows_kernel,
         "rows",
         [SMEM, VMEM, VMEM, VMEM, VMEM, VMEM],
@@ -384,8 +460,8 @@
         diffusivity,
         depth_levels,
     )
-    low = lax.ppermute(up, "lat", north_pairs)
-    high = lax.ppermute(down, "lat", south_pairs)
+    cross = lax.ppermute(cross, "lat", cross_pairs)
+    inner = lax.ppermute(inner, "lat", inner_pairs)
 
     backward = call(
         couple_kernel,
@@ -394,32 +470,33 @@
         shape(flat, BF16),
         VMEM,
         [pltpu.VMEM((48, 8, 128), F32)],
-    )(place, came, low, high, atm_state, exchange_coef, sunlight, mixing)
+    )(place, came, cross, inner, atm_state, exchange_coef, sunlight, mixing)
     back = turn(backward)
 
-    step, done = call(
+    step, top, done = call(
         functools.partial(stencil_kernel, lats),
         "stencil",
-        [SMEM] + [VMEM] * 9 + [ANY],
-        (shape((32, 16, 384), F32), shape((8, 128), F32)),
-        (VMEM, VMEM),
+        [SMEM] + [VMEM] * 9 + [SMEM, ANY],
+        (shape((32, 16, 384), F32), shape((4, 16, 384), F32), shape((48,), jnp.int32)),
+        (VMEM, VMEM, SMEM),
         [pltpu.VMEM((2, 56, 384), F32), pltpu.VMEM((2, 32, 384), F32), pltpu.VMEM((5, 16, 384), F32)],
         cost_estimate=pl.CostEstimate(flops=8000000, bytes_accessed=3000000, transcendentals=0),
     )(
         land_mask,
         came,
-        low,
-        high,
+        cross,
+        inner,
         tracers_l,
         east_velocity,
         north_velocity,
         diffusivity,
         cross_diffusivity,
         depth_levels,
+        code,
         backward,
     )
 
-    to_south, to_north, heat = call(
+    back_cross, back_inner, heat = call(
         functools.partial(split_kernel, lats),
         "split",
         [VMEM, ANY],
@@ -427,21 +504,24 @@
         (VMEM, VMEM, VMEM),
     )(back, done)
     heat = lax.all_to_all(heat, "lat", 0, 0, tiled=True)
-    back_north = lax.ppermute(to_south, "lat", south_pairs)
-    back_south = lax.ppermute(to_north, "lat", north_pairs)
+    back_cross = lax.ppermute(back_cross, "lat", cross_pairs)
+    back_inner = lax.ppermute(back_inner, "lat", inner_pairs)
 
     points = float(48 * 128 * lats * lons)
-    top = pl.BlockSpec((4, 1, 16, 384), lambda i: (0, 0, 0, 0))
     ocean_flux, new_tracers = call(
         functools.partial(finish_kernel, points),
         "finish",
-        [SMEM, SMEM, VMEM, VMEM, VMEM, VMEM, VMEM, top],
+        [SMEM, SMEM, VMEM, VMEM, VMEM, VMEM, VMEM, VMEM, ANY],
         (shape((48, 8, 128), BF16), shape((4, 8, 16, 384), F32)),
-        (VMEM, top),
-        [pltpu.VMEM((384, 128), F32)],
-        grid=(1,),
-        input_output_aliases={7: 1},
-    )(code, land_mask, back, back_north, back_south, heat, depth_levels, step.reshape(4, 8, 16, 384))
+        (ANY, ANY),
+        [
+            pltpu.VMEM((48, 8, 128), BF16),
+            pltpu.VMEM((4, 16, 384), F32),
+            pltpu.VMEM((384, 128), F32),
+            pltpu.SemaphoreType.DMA((2,)),
+        ],
+        input_output_aliases={8: 1},
+    )(done, land_mask, back, back_cross, back_inner, heat, depth_levels, top, step.reshape(4, 8, 16, 384))
     return (new_tracers, ocean_flux)
 
 

time: 82.8 us -> 77.9 us (0.941)
  starting transfers between devices: 49.3 us -> 46.2 us
  waiting for transfers between devices: 18.5 us -> 17.4 us
    all_to_all x1, starting transfers between devices: 10.4 us -> 6.7 us  [shards(): heat = lax.all_to_all(heat, 'lat', 0, 0, tiled=True)]
    ppermute x4, waiting for transfers between devices: 8.75 us -> 7.64 us  [the longest x1 2.91 us: shards(): inner = lax.ppermute(inner, 'lat', inner_pairs)]
  transfers between devices with their start and end apart: 7 -> 7, of which waited for: 5 -> 7; matrix products, arithmetic and copies ran while one was open for 0% -> 0% of each run, Pallas kernels for 4% -> 5%
where the time goes in v3:
time: 77.9 us; the launch traced here: 77 us
  starting transfers between devices  46.2 us (59%)
  waiting for transfers between devices  17.4 us (22%)
  Pallas kernels  11 us (14%)
  local copies, waits for them, and re-layouts  1.38 us (2%)
  between operations  0.81 us (1%)
    all_to_all x2, starting transfers between devices, turn(): return lax.all_to_all(values, 'lon', 0, 0, tiled=True).reshape(flat)  20 us
    ppermute x1, starting transfers between devices, shards(): cross = lax.ppermute(cross, 'lat', cross_pairs)  9.14 us
    all_to_all x2, waiting for transfers between devices, turn(): return lax.all_to_all(values, 'lon', 0, 0, tiled=True).reshape(flat)  9.07 us
    all_to_all x1, starting transfers between devices, shards(): heat = lax.all_to_all(heat, 'lat', 0, 0, tiled=True)  6.7 us
    ppermute x1, starting transfers between devices, shards(): back_cross = lax.ppermute(back_cross, 'lat', cross_pairs)  6.55 us
    pallas_call x1, Pallas kernels, shards(): call(functools.partial(stencil_kernel, lats), 'stencil', [SMEM] + [VMEM]...  3.68 us
    ppermute x1, waiting for transfers between devices, shards(): inner = lax.ppermute(inner, 'lat', inner_pairs)  2.91 us
    ppermute x1, waiting for transfers between devices, shards(): back_inner = lax.ppermute(back_inner, 'lat', inner_pairs)  2.83 us
  transfers between devices with their start and end apart: 7, of which 7 were waited for; matrix products, arithmetic and copies ran while one was open for 0% of the time, Pallas kernels for 5%

profile of v3, /device:TPU:1, one launch (start us, length us, event | category | flops | bytes accessed | tf_op | source)
XLA Modules:
  0.0 77.0 jit_solution(6357488989838138627)
XLA Ops:
  0.6 0.0 copy-start
  0.6 2.3 %pack.1 = (bf16[160,8,128]{2,1,0:T(8,128)(2,1)}, s32[48]{0:T(128)}) custom-call(s32[48]{0:T(128)} %dest_hbm.1, s32[48]{0:T(128)} %land_ref.5, bf16[48,8,128]{2,1,0:T(8,128)(2,1)} %state_hbm.1, f32[32,16,384]{2,1,0:T(8,128)} %bitcast.6, f32[8,16,384]{2,1,0:T(8,128)} %east_ref.1, f32[8,16,384]{2,1,0:T(8,128)} %kappa_ref.3, s32[16,384]{1,0:T(8,128)} %depth_ref.5), custom_call_target="tpu_custom_call" | custom-call | tf_op jit(solution)/shard_map/pack/pallas_call | solution.py:421
  3.0 0.0 copy-start.1
  3.0 0.0 copy-start.3
  3.0 0.0 copy-start.4
  3.0 14.0 %all-to-all-start = ((bf16[8,20,8,128]{3,2,1,0:T(8,128)(2,1)}), bf16[8,20,8,128]{3,2,1,0:T(8,128)(2,1)S(1)}, u32[]{:S(2)}, u32[]{:S(2)}) async-start(bf16[8,20,8,128]{3,2,1,0:T(8,128)(2,1)} %bitcast.15), calls=%async_computation | async-start | bytes 655360 | tf_op jit(solution)/shard_map/all_to_all | solution.py:417
  17.0 0.0 copy-start.13
  17.0 0.7 copy-done.12
  17.7 0.0 copy-done.13
  17.7 0.2 convert_reduce_fusion
  17.8 0.0 copy-start.9
  17.9 6.3 %all-to-all-done = bf16[8,20,8,128]{3,2,1,0:T(8,128)(2,1)S(1)} async-done(((bf16[8,20,8,128]{3,2,1,0:T(8,128)(2,1)}), bf16[8,20,8,128]{3,2,1,0:T(8,128)(2,1)S(1)}, u32[]{:S(2)}, u32[]{:S(2)}) %all-to-all-start) | async-done | bytes 327712 | tf_op jit(solution)/shard_map/all_to_all | solution.py:417
  24.1 0.0 copy-done
  24.1 0.0 copy-done.1
  24.1 0.0 copy-done.3
  24.1 0.0 copy-done.4
  24.2 0.0 copy-done.9
  24.2 0.0 copy-start.6
  24.2 0.0 copy-start.7
  24.2 0.0 copy-start.8
  24.2 0.7 rows.1
  24.9 0.0 copy-start.10
  24.9 9.1 %collective-permute-start = (bf16[69,8,128]{2,1,0:T(8,128)(2,1)S(1)}, bf16[69,8,128]{2,1,0:T(8,128)(2,1)S(1)}, u32[]{:S(2)}, u32[]{:S(2)}) collective-permute-start(bf16[69,8,128]{2,1,0:T(8,128)(2,1)S(1)} %get-tuple-element.15), channel_id=1, source_target_pairs={{0,760},{760,0},{16,8},{8,16},{32,24},{24,32},{48,40},{40,48},{64,... | collective-permute-start | bytes 423944 | tf_op jit(solution)/shard_map/ppermute | solution.py:463
  34.1 1.9 %collective-permute-start.1 = (bf16[69,8,128]{2,1,0:T(8,128)(2,1)S(1)}, bf16[69,8,128]{2,1,0:T(8,128)(2,1)S(1)}, u32[]{:S(2)}, u32[]{:S(2)}) collective-permute-start(bf16[69,8,128]{2,1,0:T(8,128)(2,1)S(1)} %get-tuple-element.16), channel_id=1, source_target_pairs={{0,8},{8,0},{16,24},{24,16},{32,40},{40,32},{48,56},{56,48},{64,72... | collective-permute-start | bytes 423944 | tf_op jit(solution)/shard_map/ppermute | solution.py:464
  36.0 1.0 %collective-permute-done.cross_ref.cross_halo_ref = bf16[69,8,128]{2,1,0:T(8,128)(2,1)S(1)} collective-permute-done((bf16[69,8,128]{2,1,0:T(8,128)(2,1)S(1)}, bf16[69,8,128]{2,1,0:T(8,128)(2,1)S(1)}, u32[]{:S(2)}, u32[]{:S(2)}) %collective-permute-start) | collective-permute-done | bytes 141344 | tf_op jit(solution)/shard_map/ppermute | solution.py:463
  37.0 2.9 %collective-permute-done.1.inner_ref.inner_halo_ref = bf16[69,8,128]{2,1,0:T(8,128)(2,1)S(1)} collective-permute-done((bf16[69,8,128]{2,1,0:T(8,128)(2,1)S(1)}, bf16[69,8,128]{2,1,0:T(8,128)(2,1)S(1)}, u32[]{:S(2)}, u32[]{:S(2)}) %collective-permute-start.1) | collective-permute-done | bytes 141344 | tf_op jit(solution)/shard_map/ppermute | solution.py:464
  39.9 0.0 copy-done.6
  39.9 0.0 copy-done.7
  39.9 0.0 copy-done.8
  39.9 0.0 copy-done.10
  39.9 2.0 %couple.1.after_ref = bf16[160,8,128]{2,1,0:T(8,128)(2,1)} custom-call(s32[48]{0:T(128)S(1)} %fusion.2.place_ref, bf16[160,8,128]{2,1,0:T(8,128)(2,1)S(1)} %bitcast.10, bf16[69,8,128]{2,1,0:T(8,128)(2,1)S(1)} %collective-permute-done.cross_ref.cross_halo_ref, bf16[69,8,128]{2,1,0:T(8,128)(2,1)S(1)} %collective-permute-done.1.inner_ref.inner_halo_ref, ...), custom_call_target="tpu_custom_call" | custom-call | tf_op jit(solution)/shard_map/couple/pallas_call | solution.py:466
  41.9 0.0 copy-start.2
  41.9 0.0 copy-start.5
  41.9 6.0 %all-to-all-start.1 = ((bf16[8,20,8,128]{3,2,1,0:T(8,128)(2,1)}), bf16[8,20,8,128]{3,2,1,0:T(8,128)(2,1)S(1)}, u32[]{:S(2)}, u32[]{:S(2)}) async-start(bf16[8,20,8,128]{3,2,1,0:T(8,128)(2,1)} %bitcast.3), calls=%async_computation.1 | async-start | bytes 655360 | tf_op jit(solution)/shard_map/all_to_all | solution.py:417
  47.9 0.0 copy-start.11
  47.9 0.0 copy-done.2
  47.9 0.0 copy-done.5
  47.9 0.6 copy-done.11
  48.6 3.7 %stencil.1 = (f32[32,16,384]{2,1,0:T(8,128)}, f32[4,16,384]{2,1,0:T(8,128)S(1)}, s32[48]{0:T(128)S(1)}) custom-call(s32[48]{0:T(128)S(1)} %copy-done.9, bf16[160,8,128]{2,1,0:T(8,128)(2,1)S(1)} %bitcast.11, bf16[69,8,128]{2,1,0:T(8,128)(2,1)S(1)} %collective-permute-done.cross_ref.cross_halo_ref, ...), custom_call_target="tpu_custom_call" | custom-call | flops 8000000 | bytes 3000000 | tf_op jit(solution)/shard_map/stencil/pallas_call | solution.py:476
  52.3 2.8 %all-to-all-done.1 = bf16[8,20,8,128]{3,2,1,0:T(8,128)(2,1)S(1)} async-done(((bf16[8,20,8,128]{3,2,1,0:T(8,128)(2,1)}), bf16[8,20,8,128]{3,2,1,0:T(8,128)(2,1)S(1)}, u32[]{:S(2)}, u32[]{:S(2)}) %all-to-all-start.1) | async-done | bytes 327712 | tf_op jit(solution)/shard_map/all_to_all | solution.py:417
  55.1 0.7 split.1
  55.7 6.7 %all-to-all-start.2 = ((f32[96,1,128]{2,1,0:T(1,128)}), f32[96,1,128]{2,1,0:T(1,128)S(1)}, u32[]{:S(2)}, u32[]{:S(2)}) async-start(f32[96,1,128]{2,1,0:T(1,128)} %get-tuple-element.21), calls=%async_computation.2 | async-start | bytes 98304 | tf_op jit(solution)/shard_map/all_to_all | solution.py:506
  62.4 6.6 %collective-permute-start.2 = (bf16[48,8,128]{2,1,0:T(8,128)(2,1)S(1)}, bf16[48,8,128]{2,1,0:T(8,128)(2,1)S(1)}, u32[]{:S(2)}, u32[]{:S(2)}) collective-permute-start(bf16[48,8,128]{2,1,0:T(8,128)(2,1)S(1)} %get-tuple-element.19), channel_id=1, source_target_pairs={{0,760},{760,0},{16,8},{8,16},{32,24},{24,32},{48,40},{40,48},{64,... | collective-permute-start | bytes 294920 | tf_op jit(solution)/shard_map/ppermute | solution.py:507
  69.0 1.9 %collective-permute-start.3 = (bf16[48,8,128]{2,1,0:T(8,128)(2,1)S(1)}, bf16[48,8,128]{2,1,0:T(8,128)(2,1)S(1)}, u32[]{:S(2)}, u32[]{:S(2)}) collective-permute-start(bf16[48,8,128]{2,1,0:T(8,128)(2,1)S(1)} %get-tuple-element.20), channel_id=1, source_target_pairs={{0,8},{8,0},{16,24},{24,16},{32,40},{40,32},{48,56},{56,48},{64,72... | collective-permute-start | bytes 294920 | tf_op jit(solution)/shard_map/ppermute | solution.py:508
  70.9 0.9 %collective-permute-done.2.cross_ref = bf16[48,8,128]{2,1,0:T(8,128)(2,1)S(1)} collective-permute-done((bf16[48,8,128]{2,1,0:T(8,128)(2,1)S(1)}, bf16[48,8,128]{2,1,0:T(8,128)(2,1)S(1)}, u32[]{:S(2)}, u32[]{:S(2)}) %collective-permute-start.2) | collective-permute-done | bytes 98336 | tf_op jit(solution)/shard_map/ppermute | solution.py:507
  71.9 2.8 %collective-permute-done.3.inner_ref = bf16[48,8,128]{2,1,0:T(8,128)(2,1)S(1)} collective-permute-done((bf16[48,8,128]{2,1,0:T(8,128)(2,1)S(1)}, bf16[48,8,128]{2,1,0:T(8,128)(2,1)S(1)}, u32[]{:S(2)}, u32[]{:S(2)}) %collective-permute-start.3) | collective-permute-done | bytes 98336 | tf_op jit(solution)/shard_map/ppermute | solution.py:508
  74.7 0.7 all-to-all-done.2.heat_ref
  75.3 1.6 %finish.1 = (bf16[48,8,128]{2,1,0:T(8,128)(2,1)}, f32[4,8,16,384]{3,2,1,0:T(8,128)}) custom-call(s32[48]{0:T(128)S(1)} %get-tuple-element.18.done_ref.code_ref, s32[48]{0:T(128)S(1)} %copy-done.9, bf16[160,8,128]{2,1,0:T(8,128)(2,1)S(1)} %bitcast.13, bf16[48,8,128]{2,1,0:T(8,128)(2,1)S(1)} %collective-permute-done.2.cross_ref, ...), custom_call_target="tpu_custom_call", output_to_operand_aliasing={{1}: (8, {})} | custom-call | tf_op jit(solution)/shard_map/finish/pallas_call | solution.py:511
  (2 shorter events, 0.0 us)
Async XLA Ops:
  0.6 23.5 %copy-start = (f32[4,8,16,384]{3,2,1,0:T(8,128)S(1)}, f32[4,8,16,384]{3,2,1,0:T(8,128)}, u32[]{:S(2)}) copy-start(f32[4,8,16,384]{3,2,1,0:T(8,128)} %param.16) | copy-start | bytes 2359300
  3.0 21.2 %copy-start.1 = (f32[8,16,384]{2,1,0:T(8,128)S(1)}, f32[8,16,384]{2,1,0:T(8,128)}, u32[]{:S(2)}) copy-start(f32[8,16,384]{2,1,0:T(8,128)} %kappa_ref.3) | copy-start | bytes 589828
  3.0 21.2 %copy-start.3 = (f32[8,16,384]{2,1,0:T(8,128)S(1)}, f32[8,16,384]{2,1,0:T(8,128)}, u32[]{:S(2)}) copy-start(f32[8,16,384]{2,1,0:T(8,128)} %north_ref.3) | copy-start | bytes 589828
  3.0 21.2 %copy-start.4 = (s32[16,384]{1,0:T(8,128)S(1)}, s32[16,384]{1,0:T(8,128)}, u32[]{:S(2)}) copy-start(s32[16,384]{1,0:T(8,128)} %depth_ref.5) | copy-start | bytes 73732
  3.0 21.1 %all-to-all-start = ((bf16[8,20,8,128]{3,2,1,0:T(8,128)(2,1)}), bf16[8,20,8,128]{3,2,1,0:T(8,128)(2,1)S(1)}, u32[]{:S(2)}, u32[]{:S(2)}) async-start(bf16[8,20,8,128]{3,2,1,0:T(8,128)(2,1)} %bitcast.15), calls=%async_computation | async-start | bytes 655360 | tf_op jit(solution)/shard_map/all_to_all | solution.py:417
  17.0 0.7 copy-start.12
  17.0 0.7 copy-start.13
  17.8 6.3 %copy-start.9 = (s32[48]{0:T(128)S(1)}, s32[48]{0:T(128)}, u32[]{:S(2)}) copy-start(s32[48]{0:T(128)} %land_ref.5) | copy-start | bytes 580
  24.2 15.7 %copy-start.6 = (f32[48,8,128]{2,1,0:T(8,128)S(1)}, f32[48,8,128]{2,1,0:T(8,128)}, u32[]{:S(2)}) copy-start(f32[48,8,128]{2,1,0:T(8,128)} %atm_ref.1) | copy-start | bytes 589828
  24.2 15.7 %copy-start.7 = (f32[48,128]{1,0:T(8,128)S(1)}, f32[48,128]{1,0:T(8,128)}, u32[]{:S(2)}) copy-start(f32[48,128]{1,0:T(8,128)} %coef_ref.1) | copy-start | bytes 73732
  24.2 15.7 %copy-start.8 = (f32[48,128]{1,0:T(8,128)S(1)}, f32[48,128]{1,0:T(8,128)}, u32[]{:S(2)}) copy-start(f32[48,128]{1,0:T(8,128)} %sun_ref.1) | copy-start | bytes 73732
  24.9 15.0 %copy-start.10 = (f32[8,8]{1,0:T(8,128)S(1)}, f32[8,8]{1,0:T(8,128)}, u32[]{:S(2)}) copy-start(f32[8,8]{1,0:T(8,128)} %mixing_ref.1) | copy-start | bytes 772
  24.9 12.1 %collective-permute-start = (bf16[69,8,128]{2,1,0:T(8,128)(2,1)S(1)}, bf16[69,8,128]{2,1,0:T(8,128)(2,1)S(1)}, u32[]{:S(2)}, u32[]{:S(2)}) collective-permute-start(bf16[69,8,128]{2,1,0:T(8,128)(2,1)S(1)} %get-tuple-element.15), channel_id=1, source_target_pairs={{0,760},{760,0},{16,8},{8,16},{32,24},{24,32},{48,40},{40,48},{64,... | collective-permute-start | bytes 423944 | tf_op jit(solution)/shard_map/ppermute | solution.py:463
  34.1 5.8 %collective-permute-start.1 = (bf16[69,8,128]{2,1,0:T(8,128)(2,1)S(1)}, bf16[69,8,128]{2,1,0:T(8,128)(2,1)S(1)}, u32[]{:S(2)}, u32[]{:S(2)}) collective-permute-start(bf16[69,8,128]{2,1,0:T(8,128)(2,1)S(1)} %get-tuple-element.16), channel_id=1, source_target_pairs={{0,8},{8,0},{16,24},{24,16},{32,40},{40,32},{48,56},{56,48},{64,72... | collective-permute-start | bytes 423944 | tf_op jit(solution)/shard_map/ppermute | solution.py:464
  41.9 6.0 %copy-start.2 = (f32[8,16,384]{2,1,0:T(8,128)S(1)}, f32[8,16,384]{2,1,0:T(8,128)}, u32[]{:S(2)}) copy-start(f32[8,16,384]{2,1,0:T(8,128)} %east_ref.1) | copy-start | bytes 589828
  41.9 6.0 %copy-start.5 = (f32[8,16,384]{2,1,0:T(8,128)S(1)}, f32[8,16,384]{2,1,0:T(8,128)}, u32[]{:S(2)}) copy-start(f32[8,16,384]{2,1,0:T(8,128)} %cross_ref.1) | copy-start | bytes 589828
  41.9 13.2 %all-to-all-start.1 = ((bf16[8,20,8,128]{3,2,1,0:T(8,128)(2,1)}), bf16[8,20,8,128]{3,2,1,0:T(8,128)(2,1)S(1)}, u32[]{:S(2)}, u32[]{:S(2)}) async-start(bf16[8,20,8,128]{3,2,1,0:T(8,128)(2,1)} %bitcast.3), calls=%async_computation.1 | async-start | bytes 655360 | tf_op jit(solution)/shard_map/all_to_all | solution.py:417
  47.9 0.7 copy-start.11
  55.7 19.6 %all-to-all-start.2 = ((f32[96,1,128]{2,1,0:T(1,128)}), f32[96,1,128]{2,1,0:T(1,128)S(1)}, u32[]{:S(2)}, u32[]{:S(2)}) async-start(f32[96,1,128]{2,1,0:T(1,128)} %get-tuple-element.21), calls=%async_computation.2 | async-start | bytes 98304 | tf_op jit(solution)/shard_map/all_to_all | solution.py:506
  62.4 9.4 %collective-permute-start.2 = (bf16[48,8,128]{2,1,0:T(8,128)(2,1)S(1)}, bf16[48,8,128]{2,1,0:T(8,128)(2,1)S(1)}, u32[]{:S(2)}, u32[]{:S(2)}) collective-permute-start(bf16[48,8,128]{2,1,0:T(8,128)(2,1)S(1)} %get-tuple-element.19), channel_id=1, source_target_pairs={{0,760},{760,0},{16,8},{8,16},{32,24},{24,32},{48,40},{40,48},{64,... | collective-permute-start | bytes 294920 | tf_op jit(solution)/shard_map/ppermute | solution.py:507
  69.0 5.7 %collective-permute-start.3 = (bf16[48,8,128]{2,1,0:T(8,128)(2,1)S(1)}, bf16[48,8,128]{2,1,0:T(8,128)(2,1)S(1)}, u32[]{:S(2)}, u32[]{:S(2)}) collective-permute-start(bf16[48,8,128]{2,1,0:T(8,128)(2,1)S(1)} %get-tuple-element.20), channel_id=1, source_target_pairs={{0,8},{8,0},{16,24},{24,16},{32,40},{40,32},{48,56},{56,48},{64,72... | collective-permute-start | bytes 294920 | tf_op jit(solution)/shard_map/ppermute | solution.py:508

commit v4 on v3

--- a/solution.py
+++ b/solution.py
@@ -144,7 +144,7 @@
 
 
 def couple_kernel(place_ref, came_ref, cross_ref, inner_ref, atm_ref, coef_ref, sun_ref, mixing_ref,
-                  out_ref, got_ref):
+                  back_cross_ref, back_inner_ref, back_own_ref, heat_ref, got_ref, out_ref):
     odd = lax.rem(lax.axis_index("lat"), 2)
     cross_off = jnp.where(odd == 1, 0, 2)
     total = jnp.zeros((8, 128), F32)
@@ -181,30 +181,30 @@
         flux = coef * mixed
         flux = flux + jnp.where(first, coef * sun_ref[q : q + 1, :], 0.0)
         rounded = flux.astype(BF16)
-        out_ref[slon * SLOTS + off * PAIR + rank] = rounded
+        way = jnp.where(off == 1, 2, jnp.where(off == cross_off, 0, 1))
+        out_ref[way * 48 + slon * PAIR + rank] = rounded
         heat = heat + jnp.where(wet, rounded.astype(F32), 0.0)
+    for i, ref in enumerate((back_cross_ref, back_inner_ref, back_own_ref)):
+        ref[...] = out_ref[48 * i : 48 * i + 48]
+    heat_ref[...] = jnp.broadcast_to(heat[0:1][None], heat_ref.shape)
+
+
+def merge_kernel(cross_ref, inner_ref, own_ref, heat_ref, out_ref):
+    odd = lax.rem(lax.axis_index("lat"), 2)
+    cross_at = jnp.where(odd == 1, 12, 0)
+    inner_at = 12 - cross_at
     subs = iota((8, 128), 0)
-    row = jnp.broadcast_to(heat[0:1], (8, 128))
+    row = jnp.broadcast_to(jnp.sum(heat_ref[...], axis=0), (8, 128))
     one = row.astype(BF16).astype(F32)
     two = (row - one).astype(BF16).astype(F32)
     three = row - one - two
     parts = jnp.where(subs == 0, one, jnp.where(subs == 1, two, jnp.where(subs == 2, three, 0.0)))
     for s in range(8):
+        for k in range(PAIR):
+            out_ref[s * SLOTS + cross_at + k] = cross_ref[s * PAIR + k]
+            out_ref[s * SLOTS + inner_at + k] = inner_ref[s * PAIR + k]
+            out_ref[s * SLOTS + PAIR + k] = own_ref[s * PAIR + k]
         out_ref[s * SLOTS + 18] = parts.astype(BF16)
-
-
-def split_kernel(lats, back_ref, done_ref, cross_ref, inner_ref, heat_ref):
-    odd = lax.rem(lax.axis_index("lat"), 2)
-    cross_at = jnp.where(odd == 1, 0, 12)
-    inner_at = 12 - cross_at
-    heat = jnp.zeros((8, 128), F32)
-    for s in range(8):
-        heat = heat + back_ref[s * SLOTS + 18].astype(F32)
-        for k in range(PAIR):
-            cross_ref[s * PAIR + k] = back_ref[s * SLOTS + cross_at + k]
-            inner_ref[s * PAIR + k] = back_ref[s * SLOTS + inner_at + k]
-    row = jnp.sum(heat, axis=0, keepdims=True)
-    heat_ref[...] = jnp.broadcast_to(row[None], (lats, 1, 128))
 
 
 def stencil_kernel(lats, land_ref, came_ref, cross_halo_ref, inner_halo_ref, tracer_ref, east_ref, north_ref,
@@ -331,26 +331,23 @@
         done_ref[t] = code_ref[t]
 
 
-def finish_kernel(points, code_ref, land_ref, back_ref, cross_ref, inner_ref, heat_ref, depth_ref,
-                  top_ref, step_hbm, flux_hbm, out_hbm, flux_ref, sum_ref, wide_ref, sems):
-    odd = lax.rem(lax.axis_index("lat"), 2)
-    cross_off = jnp.where(odd == 1, 2, 0)
+def finish_kernel(points, code_ref, land_ref, back_ref, depth_ref, top_ref, step_hbm, flux_hbm, out_hbm,
+                  flux_ref, sum_ref, wide_ref, sems):
     for t in range(48):
         code = code_ref[t]
         rank = lax.bitwise_and(code, 7)
         dlon = lax.bitwise_and(lax.shift_right_logical(code, 3), 7)
         off = lax.shift_right_logical(code, 6)
-        at = dlon * PAIR + rank
-        own = back_ref[dlon * SLOTS + PAIR + rank].astype(F32)
-        cross = cross_ref[at].astype(F32)
-        inner = inner_ref[at].astype(F32)
-        value = jnp.where(off == 1, own, jnp.where(off == cross_off, cross, inner))
+        value = back_ref[dlon * SLOTS + off * PAIR + rank].astype(F32)
         value = jnp.where(land_ref[t] > 0, value, 0.0)
         flux_ref[t] = value.astype(BF16)
         wide_ref[8 * t : 8 * t + 8, :] = value
     flux_copy = pltpu.make_async_copy(flux_ref, flux_hbm, sems.at[0])
     flux_copy.start()
-    heat = jnp.sum(jnp.sum(heat_ref[...], axis=0), axis=1, keepdims=True)
+    heat = jnp.zeros((8, 128), F32)
+    for i in range(8):
+        heat = heat + back_ref[i * SLOTS + 18].astype(F32)
+    heat = jnp.sum(jnp.sum(heat, axis=0, keepdims=True), axis=1, keepdims=True)
     correction = heat / points
     for j in range(3):
         cols = slice(128 * j, 128 * j + 128)
@@ -463,14 +460,21 @@
     cross = lax.ppermute(cross, "lat", cross_pairs)
     inner = lax.ppermute(inner, "lat", inner_pairs)
 
-    backward = call(
+    tiles_shape = shape((48, 8, 128), BF16)
+    back_cross, back_inner, back_own, heat = call(
         couple_kernel,
         "couple",
         [SMEM] + [VMEM] * 7,
-        shape(flat, BF16),
-        VMEM,
-        [pltpu.VMEM((48, 8, 128), F32)],
+        (tiles_shape, tiles_shape, tiles_shape, shape((lats, 1, 128), F32)),
+        (VMEM, VMEM, VMEM, VMEM),
+        [pltpu.VMEM((48, 8, 128), F32), pltpu.VMEM((144, 8, 128), BF16)],
     )(place, came, cross, inner, atm_state, exchange_coef, sunlight, mixing)
+    heat = lax.all_to_all(heat, "lat", 0, 0, tiled=True)
+    back_cross = lax.ppermute(back_cross, "lat", cross_pairs)
+    back_inner = lax.ppermute(back_inner, "lat", inner_pairs)
+    backward = call(merge_kernel, "merge", [VMEM] * 4, shape(flat, BF16), VMEM)(
+        back_cross, back_inner, back_own, heat
+    )
     back = turn(backward)
 
     step, top, done = call(
@@ -496,23 +500,12 @@
         backward,
     )
 
-    back_cross, back_inner, heat = call(
-        functools.partial(split_kernel, lats),
-        "split",
-        [VMEM, ANY],
-        (shape((48, 8, 128), BF16), shape((48, 8, 128), BF16), shape((lats, 1, 128), F32)),
-        (VMEM, VMEM, VMEM),
-    )(back, done)
-    heat = lax.all_to_all(heat, "lat", 0, 0, tiled=True)
-    back_cross = lax.ppermute(back_cross, "lat", cross_pairs)
-    back_inner = lax.ppermute(back_inner, "lat", inner_pairs)
-
     points = float(48 * 128 * lats * lons)
     ocean_flux, new_tracers = call(
         functools.partial(finish_kernel, points),
         "finish",
-        [SMEM, SMEM, VMEM, VMEM, VMEM, VMEM, VMEM, VMEM, ANY],
-        (shape((48, 8, 128), BF16), shape((4, 8, 16, 384), F32)),
+        [SMEM, SMEM, VMEM, VMEM, VMEM, ANY],
+        (tiles_shape, shape((4, 8, 16, 384), F32)),
         (ANY, ANY),
         [
             pltpu.VMEM((48, 8, 128), BF16),
@@ -520,8 +513,8 @@
             pltpu.VMEM((384, 128), F32),
             pltpu.SemaphoreType.DMA((2,)),
         ],
-        input_output_aliases={8: 1},
-    )(done, land_mask, back, back_cross, back_inner, heat, depth_levels, top, step.reshape(4, 8, 16, 384))
+        input_output_aliases={5: 1},
+    )(done, land_mask, back, depth_levels, top, step.reshape(4, 8, 16, 384))
     return (new_tracers, ocean_flux)
 
 

time: 77.9 us -> 78.8 us (1.012)
  starting transfers between devices: 46.2 us -> 47.7 us
    all_to_all x2, starting transfers between devices: 20 us -> 21.2 us  [turn(): return lax.all_to_all(values, 'lon', 0, 0, tiled=True).reshape(flat)]
where the time goes in v4:
time: 78.8 us; the launch traced here: 78.3 us
  starting transfers between devices  47.7 us (61%)
  waiting for transfers between devices  17.5 us (22%)
  Pallas kernels  10.8 us (14%)
  local copies, waits for them, and re-layouts  1.29 us (2%)
  between operations  0.81 us (1%)
    all_to_all x2, starting transfers between devices, turn(): return lax.all_to_all(values, 'lon', 0, 0, tiled=True).reshape(flat)  21.2 us
    all_to_all x2, waiting for transfers between devices, turn(): return lax.all_to_all(values, 'lon', 0, 0, tiled=True).reshape(flat)  9.19 us
    ppermute x1, starting transfers between devices, shards(): cross = lax.ppermute(cross, 'lat', cross_pairs)  9.14 us
    all_to_all x1, starting transfers between devices, shards(): heat = lax.all_to_all(heat, 'lat', 0, 0, tiled=True)  6.88 us
    ppermute x1, starting transfers between devices, shards(): back_cross = lax.ppermute(back_cross, 'lat', cross_pairs)  6.55 us
    pallas_call x1, Pallas kernels, shards(): call(functools.partial(stencil_kernel, lats), 'stencil', [SMEM] + [VMEM]...  3.65 us
    ppermute x1, waiting for transfers between devices, shards(): back_inner = lax.ppermute(back_inner, 'lat', inner_pairs)  2.96 us
    ppermute x1, waiting for transfers between devices, shards(): inner = lax.ppermute(inner, 'lat', inner_pairs)  2.91 us
  transfers between devices with their start and end apart: 7, of which 7 were waited for; matrix products, arithmetic and copies ran while one was open for 0% of the time, Pallas kernels for 5%

profile of v4, /device:TPU:1, one launch (start us, length us, event | category | flops | bytes accessed | tf_op | source)
XLA Modules:
  0.0 78.3 jit_solution(17148002208030832151)
XLA Ops:
  0.6 0.0 copy-start
  0.6 2.3 %pack.1 = (bf16[160,8,128]{2,1,0:T(8,128)(2,1)}, s32[48]{0:T(128)}) custom-call(s32[48]{0:T(128)} %dest_hbm.1, s32[48]{0:T(128)} %land_ref.5, bf16[48,8,128]{2,1,0:T(8,128)(2,1)} %state_hbm.1, f32[32,16,384]{2,1,0:T(8,128)} %bitcast.6, f32[8,16,384]{2,1,0:T(8,128)} %east_ref.1, f32[8,16,384]{2,1,0:T(8,128)} %kappa_ref.3, s32[16,384]{1,0:T(8,128)} %depth_ref.5), custom_call_target="tpu_custom_call" | custom-call | tf_op jit(solution)/shard_map/pack/pallas_call | solution.py:418
  3.0 0.0 copy-start.1
  3.0 0.0 copy-start.3
  3.0 0.0 copy-start.4
  3.0 14.0 %all-to-all-start = ((bf16[8,20,8,128]{3,2,1,0:T(8,128)(2,1)}), bf16[8,20,8,128]{3,2,1,0:T(8,128)(2,1)S(1)}, u32[]{:S(2)}, u32[]{:S(2)}) async-start(bf16[8,20,8,128]{3,2,1,0:T(8,128)(2,1)} %bitcast.14), calls=%async_computation | async-start | bytes 655360 | tf_op jit(solution)/shard_map/all_to_all | solution.py:414
  17.0 0.0 copy-start.13
  17.0 0.7 copy-done.12
  17.7 0.0 copy-done.13
  17.7 0.2 convert_reduce_fusion
  17.8 0.0 copy-start.9
  17.9 6.3 %all-to-all-done = bf16[8,20,8,128]{3,2,1,0:T(8,128)(2,1)S(1)} async-done(((bf16[8,20,8,128]{3,2,1,0:T(8,128)(2,1)}), bf16[8,20,8,128]{3,2,1,0:T(8,128)(2,1)S(1)}, u32[]{:S(2)}, u32[]{:S(2)}) %all-to-all-start) | async-done | bytes 327712 | tf_op jit(solution)/shard_map/all_to_all | solution.py:414
  24.1 0.0 copy-done
  24.1 0.0 copy-done.1
  24.1 0.0 copy-done.3
  24.1 0.0 copy-done.4
  24.2 0.0 copy-done.9
  24.2 0.0 copy-start.6
  24.2 0.0 copy-start.7
  24.2 0.0 copy-start.8
  24.2 0.7 rows.1
  24.9 0.0 copy-start.10
  24.9 9.1 %collective-permute-start = (bf16[69,8,128]{2,1,0:T(8,128)(2,1)S(1)}, bf16[69,8,128]{2,1,0:T(8,128)(2,1)S(1)}, u32[]{:S(2)}, u32[]{:S(2)}) collective-permute-start(bf16[69,8,128]{2,1,0:T(8,128)(2,1)S(1)} %get-tuple-element.16), channel_id=1, source_target_pairs={{0,760},{760,0},{16,8},{8,16},{32,24},{24,32},{48,40},{40,48},{64,... | collective-permute-start | bytes 423944 | tf_op jit(solution)/shard_map/ppermute | solution.py:460
  34.1 1.9 %collective-permute-start.1 = (bf16[69,8,128]{2,1,0:T(8,128)(2,1)S(1)}, bf16[69,8,128]{2,1,0:T(8,128)(2,1)S(1)}, u32[]{:S(2)}, u32[]{:S(2)}) collective-permute-start(bf16[69,8,128]{2,1,0:T(8,128)(2,1)S(1)} %get-tuple-element.17), channel_id=1, source_target_pairs={{0,8},{8,0},{16,24},{24,16},{32,40},{40,32},{48,56},{56,48},{64,72... | collective-permute-start | bytes 423944 | tf_op jit(solution)/shard_map/ppermute | solution.py:461
  36.0 1.0 %collective-permute-done.cross_ref.cross_halo_ref = bf16[69,8,128]{2,1,0:T(8,128)(2,1)S(1)} collective-permute-done((bf16[69,8,128]{2,1,0:T(8,128)(2,1)S(1)}, bf16[69,8,128]{2,1,0:T(8,128)(2,1)S(1)}, u32[]{:S(2)}, u32[]{:S(2)}) %collective-permute-start) | collective-permute-done | bytes 141344 | tf_op jit(solution)/shard_map/ppermute | solution.py:460
  37.0 2.9 %collective-permute-done.1.inner_ref.inner_halo_ref = bf16[69,8,128]{2,1,0:T(8,128)(2,1)S(1)} collective-permute-done((bf16[69,8,128]{2,1,0:T(8,128)(2,1)S(1)}, bf16[69,8,128]{2,1,0:T(8,128)(2,1)S(1)}, u32[]{:S(2)}, u32[]{:S(2)}) %collective-permute-start.1) | collective-permute-done | bytes 141344 | tf_op jit(solution)/shard_map/ppermute | solution.py:461
  39.9 0.0 copy-done.6
  39.9 0.0 copy-done.7
  39.9 0.0 copy-done.8
  39.9 0.0 copy-done.10
  39.9 1.9 %couple.1 = (bf16[48,8,128]{2,1,0:T(8,128)(2,1)S(1)}, bf16[48,8,128]{2,1,0:T(8,128)(2,1)S(1)}, bf16[48,8,128]{2,1,0:T(8,128)(2,1)S(1)}, f32[96,1,128]{2,1,0:T(1,128)}) custom-call(s32[48]{0:T(128)S(1)} %fusion.2.place_ref, bf16[160,8,128]{2,1,0:T(8,128)(2,1)S(1)} %bitcast.10, bf16[69,8,128]{2,1,0:T(8,128)(2,1)S(1)} %collective-permute-done.cross_ref.cross_halo_ref, ...), custom_call_target="tpu_custom_call" | custom-call | tf_op jit(solution)/shard_map/couple/pallas_call | solution.py:464
  41.8 6.9 %all-to-all-start.1 = ((f32[96,1,128]{2,1,0:T(1,128)}), f32[96,1,128]{2,1,0:T(1,128)S(1)}, u32[]{:S(2)}, u32[]{:S(2)}) async-start(f32[96,1,128]{2,1,0:T(1,128)} %get-tuple-element.22), calls=%async_computation.1 | async-start | bytes 98304 | tf_op jit(solution)/shard_map/all_to_all | solution.py:472
  48.7 6.6 %collective-permute-start.2 = (bf16[48,8,128]{2,1,0:T(8,128)(2,1)S(1)}, bf16[48,8,128]{2,1,0:T(8,128)(2,1)S(1)}, u32[]{:S(2)}, u32[]{:S(2)}) collective-permute-start(bf16[48,8,128]{2,1,0:T(8,128)(2,1)S(1)} %get-tuple-element.19), channel_id=1, source_target_pairs={{0,760},{760,0},{16,8},{8,16},{32,24},{24,32},{48,40},{40,48},{64,... | collective-permute-start | bytes 294920 | tf_op jit(solution)/shard_map/ppermute | solution.py:473
  55.2 1.9 %collective-permute-start.3 = (bf16[48,8,128]{2,1,0:T(8,128)(2,1)S(1)}, bf16[48,8,128]{2,1,0:T(8,128)(2,1)S(1)}, u32[]{:S(2)}, u32[]{:S(2)}) collective-permute-start(bf16[48,8,128]{2,1,0:T(8,128)(2,1)S(1)} %get-tuple-element.20), channel_id=1, source_target_pairs={{0,8},{8,0},{16,24},{24,16},{32,40},{40,32},{48,56},{56,48},{64,72... | collective-permute-start | bytes 294920 | tf_op jit(solution)/shard_map/ppermute | solution.py:474
  57.2 0.8 %collective-permute-done.2.cross_ref = bf16[48,8,128]{2,1,0:T(8,128)(2,1)S(1)} collective-permute-done((bf16[48,8,128]{2,1,0:T(8,128)(2,1)S(1)}, bf16[48,8,128]{2,1,0:T(8,128)(2,1)S(1)}, u32[]{:S(2)}, u32[]{:S(2)}) %collective-permute-start.2) | collective-permute-done | bytes 98336 | tf_op jit(solution)/shard_map/ppermute | solution.py:473
  58.0 3.0 %collective-permute-done.3.inner_ref = bf16[48,8,128]{2,1,0:T(8,128)(2,1)S(1)} collective-permute-done((bf16[48,8,128]{2,1,0:T(8,128)(2,1)S(1)}, bf16[48,8,128]{2,1,0:T(8,128)(2,1)S(1)}, u32[]{:S(2)}, u32[]{:S(2)}) %collective-permute-start.3) | collective-permute-done | bytes 98336 | tf_op jit(solution)/shard_map/ppermute | solution.py:474
  61.0 0.6 all-to-all-done.1.heat_ref
  61.6 0.9 %merge.1.after_ref = bf16[160,8,128]{2,1,0:T(8,128)(2,1)} custom-call(bf16[48,8,128]{2,1,0:T(8,128)(2,1)S(1)} %collective-permute-done.2.cross_ref, bf16[48,8,128]{2,1,0:T(8,128)(2,1)S(1)} %collective-permute-done.3.inner_ref, bf16[48,8,128]{2,1,0:T(8,128)(2,1)S(1)} %get-tuple-element.21.own_ref, f32[96,1,128]{2,1,0:T(1,128)S(1)} %all-to-all-done.1.heat_ref), custom_call_target="tpu_custom_call" | custom-call | tf_op jit(solution)/shard_map/merge/pallas_call | solution.py:475
  62.5 0.0 copy-start.2
  62.5 0.0 copy-start.5
  62.5 7.3 %all-to-all-start.2 = ((bf16[8,20,8,128]{3,2,1,0:T(8,128)(2,1)}), bf16[8,20,8,128]{3,2,1,0:T(8,128)(2,1)S(1)}, u32[]{:S(2)}, u32[]{:S(2)}) async-start(bf16[8,20,8,128]{3,2,1,0:T(8,128)(2,1)} %bitcast.3), calls=%async_computation.2 | async-start | bytes 655360 | tf_op jit(solution)/shard_map/all_to_all | solution.py:414
  69.7 0.0 copy-start.11
  69.7 0.0 copy-done.2
  69.7 0.0 copy-done.5
  69.7 0.6 copy-done.11
  70.3 3.6 %stencil.1 = (f32[32,16,384]{2,1,0:T(8,128)}, f32[4,16,384]{2,1,0:T(8,128)S(1)}, s32[48]{0:T(128)S(1)}) custom-call(s32[48]{0:T(128)S(1)} %copy-done.9, bf16[160,8,128]{2,1,0:T(8,128)(2,1)S(1)} %bitcast.11, bf16[69,8,128]{2,1,0:T(8,128)(2,1)S(1)} %collective-permute-done.cross_ref.cross_halo_ref, ...), custom_call_target="tpu_custom_call" | custom-call | flops 8000000 | bytes 3000000 | tf_op jit(solution)/shard_map/stencil/pallas_call | solution.py:480
  73.9 2.9 %all-to-all-done.2 = bf16[8,20,8,128]{3,2,1,0:T(8,128)(2,1)S(1)} async-done(((bf16[8,20,8,128]{3,2,1,0:T(8,128)(2,1)}), bf16[8,20,8,128]{3,2,1,0:T(8,128)(2,1)S(1)}, u32[]{:S(2)}, u32[]{:S(2)}) %all-to-all-start.2) | async-done | bytes 327712 | tf_op jit(solution)/shard_map/all_to_all | solution.py:414
  76.9 1.4 %finish.1 = (bf16[48,8,128]{2,1,0:T(8,128)(2,1)}, f32[4,8,16,384]{3,2,1,0:T(8,128)}) custom-call(s32[48]{0:T(128)S(1)} %get-tuple-element.23.code_ref, s32[48]{0:T(128)S(1)} %copy-done.9, bf16[160,8,128]{2,1,0:T(8,128)(2,1)S(1)} %bitcast.12, s32[16,384]{1,0:T(8,128)S(1)} %copy-done.4, ...), custom_call_target="tpu_custom_call", output_to_operand_aliasing={{1}: (5, {})} | custom-call | tf_op jit(solution)/shard_map/finish/pallas_call | solution.py:504
  (2 shorter events, 0.0 us)
Async XLA Ops:
  0.6 23.5 %copy-start = (f32[4,8,16,384]{3,2,1,0:T(8,128)S(1)}, f32[4,8,16,384]{3,2,1,0:T(8,128)}, u32[]{:S(2)}) copy-start(f32[4,8,16,384]{3,2,1,0:T(8,128)} %param.16) | copy-start | bytes 2359300
  3.0 21.2 %copy-start.1 = (f32[8,16,384]{2,1,0:T(8,128)S(1)}, f32[8,16,384]{2,1,0:T(8,128)}, u32[]{:S(2)}) copy-start(f32[8,16,384]{2,1,0:T(8,128)} %kappa_ref.3) | copy-start | bytes 589828
  3.0 21.2 %copy-start.3 = (f32[8,16,384]{2,1,0:T(8,128)S(1)}, f32[8,16,384]{2,1,0:T(8,128)}, u32[]{:S(2)}) copy-start(f32[8,16,384]{2,1,0:T(8,128)} %north_ref.3) | copy-start | bytes 589828
  3.0 21.2 %copy-start.4 = (s32[16,384]{1,0:T(8,128)S(1)}, s32[16,384]{1,0:T(8,128)}, u32[]{:S(2)}) copy-start(s32[16,384]{1,0:T(8,128)} %depth_ref.5) | copy-start | bytes 73732
  3.0 21.1 %all-to-all-start = ((bf16[8,20,8,128]{3,2,1,0:T(8,128)(2,1)}), bf16[8,20,8,128]{3,2,1,0:T(8,128)(2,1)S(1)}, u32[]{:S(2)}, u32[]{:S(2)}) async-start(bf16[8,20,8,128]{3,2,1,0:T(8,128)(2,1)} %bitcast.14), calls=%async_computation | async-start | bytes 655360 | tf_op jit(solution)/shard_map/all_to_all | solution.py:414
  17.0 0.7 copy-start.12
  17.0 0.7 copy-start.13
  17.8 6.3 %copy-start.9 = (s32[48]{0:T(128)S(1)}, s32[48]{0:T(128)}, u32[]{:S(2)}) copy-start(s32[48]{0:T(128)} %land_ref.5) | copy-start | bytes 580
  24.2 15.7 %copy-start.6 = (f32[48,8,128]{2,1,0:T(8,128)S(1)}, f32[48,8,128]{2,1,0:T(8,128)}, u32[]{:S(2)}) copy-start(f32[48,8,128]{2,1,0:T(8,128)} %atm_ref.1) | copy-start | bytes 589828
  24.2 15.7 %copy-start.7 = (f32[48,128]{1,0:T(8,128)S(1)}, f32[48,128]{1,0:T(8,128)}, u32[]{:S(2)}) copy-start(f32[48,128]{1,0:T(8,128)} %coef_ref.1) | copy-start | bytes 73732
  24.2 15.7 %copy-start.8 = (f32[48,128]{1,0:T(8,128)S(1)}, f32[48,128]{1,0:T(8,128)}, u32[]{:S(2)}) copy-start(f32[48,128]{1,0:T(8,128)} %sun_ref.1) | copy-start | bytes 73732
  24.9 15.0 %copy-start.10 = (f32[8,8]{1,0:T(8,128)S(1)}, f32[8,8]{1,0:T(8,128)}, u32[]{:S(2)}) copy-start(f32[8,8]{1,0:T(8,128)} %mixing_ref.1) | copy-start | bytes 772
  24.9 12.1 %collective-permute-start = (bf16[69,8,128]{2,1,0:T(8,128)(2,1)S(1)}, bf16[69,8,128]{2,1,0:T(8,128)(2,1)S(1)}, u32[]{:S(2)}, u32[]{:S(2)}) collective-permute-start(bf16[69,8,128]{2,1,0:T(8,128)(2,1)S(1)} %get-tuple-element.16), channel_id=1, source_target_pairs={{0,760},{760,0},{16,8},{8,16},{32,24},{24,32},{48,40},{40,48},{64,... | collective-permute-start | bytes 423944 | tf_op jit(solution)/shard_map/ppermute | solution.py:460
  34.1 5.8 %collective-permute-start.1 = (bf16[69,8,128]{2,1,0:T(8,128)(2,1)S(1)}, bf16[69,8,128]{2,1,0:T(8,128)(2,1)S(1)}, u32[]{:S(2)}, u32[]{:S(2)}) collective-permute-start(bf16[69,8,128]{2,1,0:T(8,128)(2,1)S(1)} %get-tuple-element.17), channel_id=1, source_target_pairs={{0,8},{8,0},{16,24},{24,16},{32,40},{40,32},{48,56},{56,48},{64,72... | collective-permute-start | bytes 423944 | tf_op jit(solution)/shard_map/ppermute | solution.py:461
  41.8 19.8 %all-to-all-start.1 = ((f32[96,1,128]{2,1,0:T(1,128)}), f32[96,1,128]{2,1,0:T(1,128)S(1)}, u32[]{:S(2)}, u32[]{:S(2)}) async-start(f32[96,1,128]{2,1,0:T(1,128)} %get-tuple-element.22), calls=%async_computation.1 | async-start | bytes 98304 | tf_op jit(solution)/shard_map/all_to_all | solution.py:472
  48.7 9.3 %collective-permute-start.2 = (bf16[48,8,128]{2,1,0:T(8,128)(2,1)S(1)}, bf16[48,8,128]{2,1,0:T(8,128)(2,1)S(1)}, u32[]{:S(2)}, u32[]{:S(2)}) collective-permute-start(bf16[48,8,128]{2,1,0:T(8,128)(2,1)S(1)} %get-tuple-element.19), channel_id=1, source_target_pairs={{0,760},{760,0},{16,8},{8,16},{32,24},{24,32},{48,40},{40,48},{64,... | collective-permute-start | bytes 294920 | tf_op jit(solution)/shard_map/ppermute | solution.py:473
  55.2 5.7 %collective-permute-start.3 = (bf16[48,8,128]{2,1,0:T(8,128)(2,1)S(1)}, bf16[48,8,128]{2,1,0:T(8,128)(2,1)S(1)}, u32[]{:S(2)}, u32[]{:S(2)}) collective-permute-start(bf16[48,8,128]{2,1,0:T(8,128)(2,1)S(1)} %get-tuple-element.20), channel_id=1, source_target_pairs={{0,8},{8,0},{16,24},{24,16},{32,40},{40,32},{48,56},{56,48},{64,72... | collective-permute-start | bytes 294920 | tf_op jit(solution)/shard_map/ppermute | solution.py:474
  62.5 7.3 %copy-start.2 = (f32[8,16,384]{2,1,0:T(8,128)S(1)}, f32[8,16,384]{2,1,0:T(8,128)}, u32[]{:S(2)}) copy-start(f32[8,16,384]{2,1,0:T(8,128)} %east_ref.1) | copy-start | bytes 589828
  62.5 7.3 %copy-start.5 = (f32[8,16,384]{2,1,0:T(8,128)S(1)}, f32[8,16,384]{2,1,0:T(8,128)}, u32[]{:S(2)}) copy-start(f32[8,16,384]{2,1,0:T(8,128)} %cross_ref.1) | copy-start | bytes 589828
  62.5 14.4 %all-to-all-start.2 = ((bf16[8,20,8,128]{3,2,1,0:T(8,128)(2,1)}), bf16[8,20,8,128]{3,2,1,0:T(8,128)(2,1)S(1)}, u32[]{:S(2)}, u32[]{:S(2)}) async-start(bf16[8,20,8,128]{3,2,1,0:T(8,128)(2,1)} %bitcast.3), calls=%async_computation.2 | async-start | bytes 655360 | tf_op jit(solution)/shard_map/all_to_all | solution.py:414
  69.7 0.6 copy-start.11

commit v5 on v3

--- a/solution.py
+++ b/solution.py
@@ -332,7 +332,7 @@
 
 
 def finish_kernel(points, code_ref, land_ref, back_ref, cross_ref, inner_ref, heat_ref, depth_ref,
-                  top_ref, step_hbm, flux_hbm, out_hbm, flux_ref, sum_ref, wide_ref, sems):
+                  top_ref, step_hbm, flux_ref, out_ref, wide_ref):
     odd = lax.rem(lax.axis_index("lat"), 2)
     cross_off = jnp.where(odd == 1, 2, 0)
     for t in range(48):
@@ -348,8 +348,6 @@
         value = jnp.where(land_ref[t] > 0, value, 0.0)
         flux_ref[t] = value.astype(BF16)
         wide_ref[8 * t : 8 * t + 8, :] = value
-    flux_copy = pltpu.make_async_copy(flux_ref, flux_hbm, sems.at[0])
-    flux_copy.start()
     heat = jnp.sum(jnp.sum(heat_ref[...], axis=0), axis=1, keepdims=True)
     correction = heat / points
     for j in range(3):
@@ -360,11 +358,7 @@
             force = wide_ref[pl.ds(8 * j + t, 16, stride=24), :]
             if t == 0:
                 force = force - correction
-            sum_ref[t, :, cols] = top_ref[t, :, cols] + gain * force
-    top_copy = pltpu.make_async_copy(sum_ref, out_hbm.at[:, 0], sems.at[1])
-    top_copy.start()
-    flux_copy.wait()
-    top_copy.wait()
+            out_ref[t, 0, :, cols] = top_ref[t, :, cols] + gain * force
 
 
 def call(kernel, name, in_specs, out_shape, out_specs, scratch=(), limit=SMALL, **more):
@@ -513,13 +507,9 @@
         "finish",
         [SMEM, SMEM, VMEM, VMEM, VMEM, VMEM, VMEM, VMEM, ANY],
         (shape((48, 8, 128), BF16), shape((4, 8, 16, 384), F32)),
-        (ANY, ANY),
-        [
-            pltpu.VMEM((48, 8, 128), BF16),
-            pltpu.VMEM((4, 16, 384), F32),
-            pltpu.VMEM((384, 128), F32),
-            pltpu.SemaphoreType.DMA((2,)),
-        ],
+        (VMEM, pl.BlockSpec((4, 1, 16, 384), lambda i: (0, 0, 0, 0))),
+        [pltpu.VMEM((416, 128), F32)],
+        grid=(1,),
         input_output_aliases={8: 1},
     )(done, land_mask, back, back_cross, back_inner, heat, depth_levels, top, step.reshape(4, 8, 16, 384))
     return (new_tracers, ocean_flux)

time: 77.9 us -> 77.8 us (level)
  no operation moved by 1% of the time
where the time goes in v5:
time: 77.8 us; the launch traced here: 76.9 us
  starting transfers between devices  46.2 us (59%)
  waiting for transfers between devices  17.4 us (22%)
  Pallas kernels  10.9 us (14%)
  local copies, waits for them, and re-layouts  1.38 us (2%)
  between operations  0.81 us (1%)
    all_to_all x2, starting transfers between devices, turn(): return lax.all_to_all(values, 'lon', 0, 0, tiled=True).reshape(flat)  20 us
    ppermute x1, starting transfers between devices, shards(): cross = lax.ppermute(cross, 'lat', cross_pairs)  9.14 us
    all_to_all x2, waiting for transfers between devices, turn(): return lax.all_to_all(values, 'lon', 0, 0, tiled=True).reshape(flat)  9.07 us
    all_to_all x1, starting transfers between devices, shards(): heat = lax.all_to_all(heat, 'lat', 0, 0, tiled=True)  6.7 us
    ppermute x1, starting transfers between devices, shards(): back_cross = lax.ppermute(back_cross, 'lat', cross_pairs)  6.55 us
    pallas_call x1, Pallas kernels, shards(): call(functools.partial(stencil_kernel, lats), 'stencil', [SMEM] + [VMEM]...  3.68 us
    ppermute x1, waiting for transfers between devices, shards(): inner = lax.ppermute(inner, 'lat', inner_pairs)  2.91 us
    ppermute x1, waiting for transfers between devices, shards(): back_inner = lax.ppermute(back_inner, 'lat', inner_pairs)  2.83 us
  transfers between devices with their start and end apart: 7, of which 7 were waited for; matrix products, arithmetic and copies ran while one was open for 0% of the time, Pallas kernels for 5%

profile of v5, /device:TPU:1, one launch (start us, length us, event | category | flops | bytes accessed | tf_op | source)
XLA Modules:
  0.0 76.9 jit_solution(6423444784458020256)
XLA Ops:
  0.6 0.0 copy-start
  0.6 2.3 %pack.1 = (bf16[160,8,128]{2,1,0:T(8,128)(2,1)}, s32[48]{0:T(128)}) custom-call(s32[48]{0:T(128)} %dest_hbm.1, s32[48]{0:T(128)} %land_ref.5, bf16[48,8,128]{2,1,0:T(8,128)(2,1)} %state_hbm.1, f32[32,16,384]{2,1,0:T(8,128)} %bitcast.6, f32[8,16,384]{2,1,0:T(8,128)} %east_ref.1, f32[8,16,384]{2,1,0:T(8,128)} %kappa_ref.3, s32[16,384]{1,0:T(8,128)} %depth_ref.5), custom_call_target="tpu_custom_call" | custom-call | tf_op jit(solution)/shard_map/pack/pallas_call | solution.py:415
  3.0 0.0 copy-start.1
  3.0 0.0 copy-start.3
  3.0 0.0 copy-start.4
  3.0 14.0 %all-to-all-start = ((bf16[8,20,8,128]{3,2,1,0:T(8,128)(2,1)}), bf16[8,20,8,128]{3,2,1,0:T(8,128)(2,1)S(1)}, u32[]{:S(2)}, u32[]{:S(2)}) async-start(bf16[8,20,8,128]{3,2,1,0:T(8,128)(2,1)} %bitcast.15), calls=%async_computation | async-start | bytes 655360 | tf_op jit(solution)/shard_map/all_to_all | solution.py:411
  17.0 0.0 copy-start.12
  17.0 0.0 copy-start.13
  17.0 0.7 copy-done.12
  17.7 0.0 copy-done.13
  17.7 0.2 convert_reduce_fusion
  17.8 0.0 copy-start.9
  17.9 6.3 %all-to-all-done = bf16[8,20,8,128]{3,2,1,0:T(8,128)(2,1)S(1)} async-done(((bf16[8,20,8,128]{3,2,1,0:T(8,128)(2,1)}), bf16[8,20,8,128]{3,2,1,0:T(8,128)(2,1)S(1)}, u32[]{:S(2)}, u32[]{:S(2)}) %all-to-all-start) | async-done | bytes 327712 | tf_op jit(solution)/shard_map/all_to_all | solution.py:411
  24.1 0.0 copy-done
  24.1 0.0 copy-done.1
  24.1 0.0 copy-done.3
  24.1 0.0 copy-done.4
  24.2 0.0 copy-done.9
  24.2 0.0 copy-start.6
  24.2 0.0 copy-start.7
  24.2 0.0 copy-start.8
  24.2 0.7 rows.1
  24.9 0.0 copy-start.10
  24.9 9.1 %collective-permute-start = (bf16[69,8,128]{2,1,0:T(8,128)(2,1)S(1)}, bf16[69,8,128]{2,1,0:T(8,128)(2,1)S(1)}, u32[]{:S(2)}, u32[]{:S(2)}) collective-permute-start(bf16[69,8,128]{2,1,0:T(8,128)(2,1)S(1)} %get-tuple-element.15), channel_id=1, source_target_pairs={{0,760},{760,0},{16,8},{8,16},{32,24},{24,32},{48,40},{40,48},{64,... | collective-permute-start | bytes 423944 | tf_op jit(solution)/shard_map/ppermute | solution.py:457
  34.1 1.9 %collective-permute-start.1 = (bf16[69,8,128]{2,1,0:T(8,128)(2,1)S(1)}, bf16[69,8,128]{2,1,0:T(8,128)(2,1)S(1)}, u32[]{:S(2)}, u32[]{:S(2)}) collective-permute-start(bf16[69,8,128]{2,1,0:T(8,128)(2,1)S(1)} %get-tuple-element.16), channel_id=1, source_target_pairs={{0,8},{8,0},{16,24},{24,16},{32,40},{40,32},{48,56},{56,48},{64,72... | collective-permute-start | bytes 423944 | tf_op jit(solution)/shard_map/ppermute | solution.py:458
  36.0 1.0 %collective-permute-done.cross_ref.cross_halo_ref = bf16[69,8,128]{2,1,0:T(8,128)(2,1)S(1)} collective-permute-done((bf16[69,8,128]{2,1,0:T(8,128)(2,1)S(1)}, bf16[69,8,128]{2,1,0:T(8,128)(2,1)S(1)}, u32[]{:S(2)}, u32[]{:S(2)}) %collective-permute-start) | collective-permute-done | bytes 141344 | tf_op jit(solution)/shard_map/ppermute | solution.py:457
  37.0 2.9 %collective-permute-done.1.inner_ref.inner_halo_ref = bf16[69,8,128]{2,1,0:T(8,128)(2,1)S(1)} collective-permute-done((bf16[69,8,128]{2,1,0:T(8,128)(2,1)S(1)}, bf16[69,8,128]{2,1,0:T(8,128)(2,1)S(1)}, u32[]{:S(2)}, u32[]{:S(2)}) %collective-permute-start.1) | collective-permute-done | bytes 141344 | tf_op jit(solution)/shard_map/ppermute | solution.py:458
  39.9 0.0 copy-done.6
  39.9 0.0 copy-done.7
  39.9 0.0 copy-done.8
  39.9 0.0 copy-done.10
  39.9 2.0 %couple.1.after_ref = bf16[160,8,128]{2,1,0:T(8,128)(2,1)} custom-call(s32[48]{0:T(128)S(1)} %fusion.2.place_ref, bf16[160,8,128]{2,1,0:T(8,128)(2,1)S(1)} %bitcast.10, bf16[69,8,128]{2,1,0:T(8,128)(2,1)S(1)} %collective-permute-done.cross_ref.cross_halo_ref, bf16[69,8,128]{2,1,0:T(8,128)(2,1)S(1)} %collective-permute-done.1.inner_ref.inner_halo_ref, ...), custom_call_target="tpu_custom_call" | custom-call | tf_op jit(solution)/shard_map/couple/pallas_call | solution.py:460
  41.9 0.0 copy-start.5
  41.9 6.0 %all-to-all-start.1 = ((bf16[8,20,8,128]{3,2,1,0:T(8,128)(2,1)}), bf16[8,20,8,128]{3,2,1,0:T(8,128)(2,1)S(1)}, u32[]{:S(2)}, u32[]{:S(2)}) async-start(bf16[8,20,8,128]{3,2,1,0:T(8,128)(2,1)} %bitcast.3), calls=%async_computation.1 | async-start | bytes 655360 | tf_op jit(solution)/shard_map/all_to_all | solution.py:411
  47.9 0.0 copy-start.11
  47.9 0.0 copy-done.2
  47.9 0.0 copy-done.5
  47.9 0.6 copy-done.11
  48.6 3.7 %stencil.1 = (f32[32,16,384]{2,1,0:T(8,128)}, f32[4,16,384]{2,1,0:T(8,128)S(1)}, s32[48]{0:T(128)S(1)}) custom-call(s32[48]{0:T(128)S(1)} %copy-done.9, bf16[160,8,128]{2,1,0:T(8,128)(2,1)S(1)} %bitcast.11, bf16[69,8,128]{2,1,0:T(8,128)(2,1)S(1)} %collective-permute-done.cross_ref.cross_halo_ref, ...), custom_call_target="tpu_custom_call" | custom-call | flops 8000000 | bytes 3000000 | tf_op jit(solution)/shard_map/stencil/pallas_call | solution.py:470
  52.3 2.8 %all-to-all-done.1 = bf16[8,20,8,128]{3,2,1,0:T(8,128)(2,1)S(1)} async-done(((bf16[8,20,8,128]{3,2,1,0:T(8,128)(2,1)}), bf16[8,20,8,128]{3,2,1,0:T(8,128)(2,1)S(1)}, u32[]{:S(2)}, u32[]{:S(2)}) %all-to-all-start.1) | async-done | bytes 327712 | tf_op jit(solution)/shard_map/all_to_all | solution.py:411
  55.1 0.7 split.1
  55.7 6.7 %all-to-all-start.2 = ((f32[96,1,128]{2,1,0:T(1,128)}), f32[96,1,128]{2,1,0:T(1,128)S(1)}, u32[]{:S(2)}, u32[]{:S(2)}) async-start(f32[96,1,128]{2,1,0:T(1,128)} %get-tuple-element.21), calls=%async_computation.2 | async-start | bytes 98304 | tf_op jit(solution)/shard_map/all_to_all | solution.py:500
  62.4 6.6 %collective-permute-start.2 = (bf16[48,8,128]{2,1,0:T(8,128)(2,1)S(1)}, bf16[48,8,128]{2,1,0:T(8,128)(2,1)S(1)}, u32[]{:S(2)}, u32[]{:S(2)}) collective-permute-start(bf16[48,8,128]{2,1,0:T(8,128)(2,1)S(1)} %get-tuple-element.19), channel_id=1, source_target_pairs={{0,760},{760,0},{16,8},{8,16},{32,24},{24,32},{48,40},{40,48},{64,... | collective-permute-start | bytes 294920 | tf_op jit(solution)/shard_map/ppermute | solution.py:501
  69.0 1.9 %collective-permute-start.3 = (bf16[48,8,128]{2,1,0:T(8,128)(2,1)S(1)}, bf16[48,8,128]{2,1,0:T(8,128)(2,1)S(1)}, u32[]{:S(2)}, u32[]{:S(2)}) collective-permute-start(bf16[48,8,128]{2,1,0:T(8,128)(2,1)S(1)} %get-tuple-element.20), channel_id=1, source_target_pairs={{0,8},{8,0},{16,24},{24,16},{32,40},{40,32},{48,56},{56,48},{64,72... | collective-permute-start | bytes 294920 | tf_op jit(solution)/shard_map/ppermute | solution.py:502
  70.9 0.9 %collective-permute-done.2.cross_ref = bf16[48,8,128]{2,1,0:T(8,128)(2,1)S(1)} collective-permute-done((bf16[48,8,128]{2,1,0:T(8,128)(2,1)S(1)}, bf16[48,8,128]{2,1,0:T(8,128)(2,1)S(1)}, u32[]{:S(2)}, u32[]{:S(2)}) %collective-permute-start.2) | collective-permute-done | bytes 98336 | tf_op jit(solution)/shard_map/ppermute | solution.py:501
  71.9 2.8 %collective-permute-done.3.inner_ref = bf16[48,8,128]{2,1,0:T(8,128)(2,1)S(1)} collective-permute-done((bf16[48,8,128]{2,1,0:T(8,128)(2,1)S(1)}, bf16[48,8,128]{2,1,0:T(8,128)(2,1)S(1)}, u32[]{:S(2)}, u32[]{:S(2)}) %collective-permute-start.3) | collective-permute-done | bytes 98336 | tf_op jit(solution)/shard_map/ppermute | solution.py:502
  74.7 0.7 all-to-all-done.2.heat_ref
  75.3 1.6 %finish.1 = (bf16[48,8,128]{2,1,0:T(8,128)(2,1)}, f32[4,8,16,384]{3,2,1,0:T(8,128)}) custom-call(s32[48]{0:T(128)S(1)} %get-tuple-element.18.done_ref.code_ref, s32[48]{0:T(128)S(1)} %copy-done.9, bf16[160,8,128]{2,1,0:T(8,128)(2,1)S(1)} %bitcast.13, bf16[48,8,128]{2,1,0:T(8,128)(2,1)S(1)} %collective-permute-done.2.cross_ref, ...), custom_call_target="tpu_custom_call", output_to_operand_aliasing={{1}: (8, {})} | custom-call | tf_op jit(solution)/shard_map/finish/pallas_call | solution.py:505
  (2 shorter events, 0.0 us)
Async XLA Ops:
  0.6 23.5 %copy-start = (f32[4,8,16,384]{3,2,1,0:T(8,128)S(1)}, f32[4,8,16,384]{3,2,1,0:T(8,128)}, u32[]{:S(2)}) copy-start(f32[4,8,16,384]{3,2,1,0:T(8,128)} %param.16) | copy-start | bytes 2359300
  3.0 21.2 %copy-start.1 = (f32[8,16,384]{2,1,0:T(8,128)S(1)}, f32[8,16,384]{2,1,0:T(8,128)}, u32[]{:S(2)}) copy-start(f32[8,16,384]{2,1,0:T(8,128)} %kappa_ref.3) | copy-start | bytes 589828
  3.0 21.2 %copy-start.3 = (f32[8,16,384]{2,1,0:T(8,128)S(1)}, f32[8,16,384]{2,1,0:T(8,128)}, u32[]{:S(2)}) copy-start(f32[8,16,384]{2,1,0:T(8,128)} %north_ref.3) | copy-start | bytes 589828
  3.0 21.2 %copy-start.4 = (s32[16,384]{1,0:T(8,128)S(1)}, s32[16,384]{1,0:T(8,128)}, u32[]{:S(2)}) copy-start(s32[16,384]{1,0:T(8,128)} %depth_ref.5) | copy-start | bytes 73732
  3.0 21.1 %all-to-all-start = ((bf16[8,20,8,128]{3,2,1,0:T(8,128)(2,1)}), bf16[8,20,8,128]{3,2,1,0:T(8,128)(2,1)S(1)}, u32[]{:S(2)}, u32[]{:S(2)}) async-start(bf16[8,20,8,128]{3,2,1,0:T(8,128)(2,1)} %bitcast.15), calls=%async_computation | async-start | bytes 655360 | tf_op jit(solution)/shard_map/all_to_all | solution.py:411
  17.0 0.7 copy-start.12
  17.0 0.7 copy-start.13
  17.8 6.3 %copy-start.9 = (s32[48]{0:T(128)S(1)}, s32[48]{0:T(128)}, u32[]{:S(2)}) copy-start(s32[48]{0:T(128)} %land_ref.5) | copy-start | bytes 580
  24.2 15.7 %copy-start.6 = (f32[48,8,128]{2,1,0:T(8,128)S(1)}, f32[48,8,128]{2,1,0:T(8,128)}, u32[]{:S(2)}) copy-start(f32[48,8,128]{2,1,0:T(8,128)} %atm_ref.1) | copy-start | bytes 589828
  24.2 15.7 %copy-start.7 = (f32[48,128]{1,0:T(8,128)S(1)}, f32[48,128]{1,0:T(8,128)}, u32[]{:S(2)}) copy-start(f32[48,128]{1,0:T(8,128)} %coef_ref.1) | copy-start | bytes 73732
  24.2 15.7 %copy-start.8 = (f32[48,128]{1,0:T(8,128)S(1)}, f32[48,128]{1,0:T(8,128)}, u32[]{:S(2)}) copy-start(f32[48,128]{1,0:T(8,128)} %sun_ref.1) | copy-start | bytes 73732
  24.9 15.0 %copy-start.10 = (f32[8,8]{1,0:T(8,128)S(1)}, f32[8,8]{1,0:T(8,128)}, u32[]{:S(2)}) copy-start(f32[8,8]{1,0:T(8,128)} %mixing_ref.1) | copy-start | bytes 772
  24.9 12.1 %collective-permute-start = (bf16[69,8,128]{2,1,0:T(8,128)(2,1)S(1)}, bf16[69,8,128]{2,1,0:T(8,128)(2,1)S(1)}, u32[]{:S(2)}, u32[]{:S(2)}) collective-permute-start(bf16[69,8,128]{2,1,0:T(8,128)(2,1)S(1)} %get-tuple-element.15), channel_id=1, source_target_pairs={{0,760},{760,0},{16,8},{8,16},{32,24},{24,32},{48,40},{40,48},{64,... | collective-permute-start | bytes 423944 | tf_op jit(solution)/shard_map/ppermute | solution.py:457
  34.1 5.8 %collective-permute-start.1 = (bf16[69,8,128]{2,1,0:T(8,128)(2,1)S(1)}, bf16[69,8,128]{2,1,0:T(8,128)(2,1)S(1)}, u32[]{:S(2)}, u32[]{:S(2)}) collective-permute-start(bf16[69,8,128]{2,1,0:T(8,128)(2,1)S(1)} %get-tuple-element.16), channel_id=1, source_target_pairs={{0,8},{8,0},{16,24},{24,16},{32,40},{40,32},{48,56},{56,48},{64,72... | collective-permute-start | bytes 423944 | tf_op jit(solution)/shard_map/ppermute | solution.py:458
  41.9 6.0 %copy-start.2 = (f32[8,16,384]{2,1,0:T(8,128)S(1)}, f32[8,16,384]{2,1,0:T(8,128)}, u32[]{:S(2)}) copy-start(f32[8,16,384]{2,1,0:T(8,128)} %east_ref.1) | copy-start | bytes 589828
  41.9 6.0 %copy-start.5 = (f32[8,16,384]{2,1,0:T(8,128)S(1)}, f32[8,16,384]{2,1,0:T(8,128)}, u32[]{:S(2)}) copy-start(f32[8,16,384]{2,1,0:T(8,128)} %cross_ref.1) | copy-start | bytes 589828
  41.9 13.2 %all-to-all-start.1 = ((bf16[8,20,8,128]{3,2,1,0:T(8,128)(2,1)}), bf16[8,20,8,128]{3,2,1,0:T(8,128)(2,1)S(1)}, u32[]{:S(2)}, u32[]{:S(2)}) async-start(bf16[8,20,8,128]{3,2,1,0:T(8,128)(2,1)} %bitcast.3), calls=%async_computation.1 | async-start | bytes 655360 | tf_op jit(solution)/shard_map/all_to_all | solution.py:411
  47.9 0.7 copy-start.11
  55.7 19.6 %all-to-all-start.2 = ((f32[96,1,128]{2,1,0:T(1,128)}), f32[96,1,128]{2,1,0:T(1,128)S(1)}, u32[]{:S(2)}, u32[]{:S(2)}) async-start(f32[96,1,128]{2,1,0:T(1,128)} %get-tuple-element.21), calls=%async_computation.2 | async-start | bytes 98304 | tf_op jit(solution)/shard_map/all_to_all | solution.py:500
  62.4 9.4 %collective-permute-start.2 = (bf16[48,8,128]{2,1,0:T(8,128)(2,1)S(1)}, bf16[48,8,128]{2,1,0:T(8,128)(2,1)S(1)}, u32[]{:S(2)}, u32[]{:S(2)}) collective-permute-start(bf16[48,8,128]{2,1,0:T(8,128)(2,1)S(1)} %get-tuple-element.19), channel_id=1, source_target_pairs={{0,760},{760,0},{16,8},{8,16},{32,24},{24,32},{48,40},{40,48},{64,... | collective-permute-start | bytes 294920 | tf_op jit(solution)/shard_map/ppermute | solution.py:501
  69.0 5.7 %collective-permute-start.3 = (bf16[48,8,128]{2,1,0:T(8,128)(2,1)S(1)}, bf16[48,8,128]{2,1,0:T(8,128)(2,1)S(1)}, u32[]{:S(2)}, u32[]{:S(2)}) collective-permute-start(bf16[48,8,128]{2,1,0:T(8,128)(2,1)S(1)} %get-tuple-element.20), channel_id=1, source_target_pairs={{0,8},{8,0},{16,24},{24,16},{32,40},{40,32},{48,56},{56,48},{64,72... | collective-permute-start | bytes 294920 | tf_op jit(solution)/shard_map/ppermute | solution.py:502

commit v6 on v5

--- a/solution.py
+++ b/solution.py
@@ -10,7 +10,7 @@
 F32 = jnp.float32
 BF16 = jnp.bfloat16
 PAIR = 6
-SLOTS = 20
+SLOTS = 19
 LAND = 2.0**100
 LAND_TEST = 2.0**90
 VMEM = pl.BlockSpec(memory_space=pltpu.VMEM)
@@ -91,8 +91,8 @@
         bottom = block_of(depth_ref, block)[...].astype(F32) * tile_column(land_ref, block)
         packed = jnp.where(lanes == 48, bottom[:, lane : lane + 1], packed)
         target = lax.rem(lon + shift, lons)
-        out_ref[target * SLOTS + 18] = packed[:8].astype(BF16)
-        out_ref[target * SLOTS + 19] = packed[8:].astype(BF16)
+        halo = jnp.where(lanes[:8] < 64, packed[:8], pltpu.roll(packed[8:], 64, 1))
+        out_ref[target * SLOTS + 18] = halo.astype(BF16)
 
 
 def by_parity(body, cross, inner):
@@ -121,12 +121,10 @@
         for s in range(8):
             for k in range(PAIR):
                 out_ref[s * PAIR + k] = came_ref[s * SLOTS + first + k]
-        half, sub = (19, 7) if row else (18, 0)
-        corners = (
-            came_ref[west * SLOTS + half].astype(F32)[sub : sub + 1],
-            None,
-            came_ref[east * SLOTS + half].astype(F32)[sub : sub + 1],
-        )
+        corners = [None] * 3
+        for j, side in ((0, west), (2, east)):
+            halo = came_ref[side * SLOTS + 18].astype(F32)
+            corners[j] = pltpu.roll(halo, 64, 1)[7:8] if row else halo[0:1]
         for j in range(3):
             cols = slice(128 * j, 128 * j + 128)
             for k in range(4):
@@ -223,9 +221,8 @@
     lane8, sub8 = iota((8, 128), 1), iota((8, 128), 0)
 
     def columns_of(side):
-        return jnp.concatenate(
-            [came_ref[side * SLOTS + 18].astype(F32), came_ref[side * SLOTS + 19].astype(F32)], axis=0
-        )
+        halo = came_ref[side * SLOTS + 18].astype(F32)
+        return jnp.concatenate([halo, pltpu.roll(halo, 64, 1)], axis=0)
 
     def from_west(v, column):
         return jnp.where(at_west, column, pltpu.roll(v, 1, 1))

time: 77.8 us -> 77.5 us (level)
  no operation moved by 1% of the time
where the time goes in v6:
time: 77.5 us; the launch traced here: 76.6 us
  starting transfers between devices  46.2 us (60%)
  waiting for transfers between devices  17 us (22%)
  Pallas kernels  11 us (14%)
  local copies, waits for them, and re-layouts  1.38 us (2%)
  between operations  0.81 us (1%)
    all_to_all x2, starting transfers between devices, turn(): return lax.all_to_all(values, 'lon', 0, 0, tiled=True).reshape(flat)  20 us
    ppermute x1, starting transfers between devices, shards(): cross = lax.ppermute(cross, 'lat', cross_pairs)  9.15 us
    all_to_all x2, waiting for transfers between devices, turn(): return lax.all_to_all(values, 'lon', 0, 0, tiled=True).reshape(flat)  8.72 us
    all_to_all x1, starting transfers between devices, shards(): heat = lax.all_to_all(heat, 'lat', 0, 0, tiled=True)  6.7 us
    ppermute x1, starting transfers between devices, shards(): back_cross = lax.ppermute(back_cross, 'lat', cross_pairs)  6.55 us
    pallas_call x1, Pallas kernels, shards(): call(functools.partial(stencil_kernel, lats), 'stencil', [SMEM] + [VMEM]...  3.73 us
    ppermute x1, waiting for transfers between devices, shards(): inner = lax.ppermute(inner, 'lat', inner_pairs)  2.89 us
    ppermute x1, waiting for transfers between devices, shards(): back_inner = lax.ppermute(back_inner, 'lat', inner_pairs)  2.83 us
  transfers between devices with their start and end apart: 7, of which 7 were waited for; matrix products, arithmetic and copies ran while one was open for 0% of the time, Pallas kernels for 5%

profile of v6, /device:TPU:1, one launch (start us, length us, event | category | flops | bytes accessed | tf_op | source)
XLA Modules:
  0.0 76.6 jit_solution(9095159867853058599)
XLA Ops:
  0.6 0.0 copy-start
  0.6 2.4 %pack.1 = (bf16[152,8,128]{2,1,0:T(8,128)(2,1)}, s32[48]{0:T(128)}) custom-call(s32[48]{0:T(128)} %dest_hbm.1, s32[48]{0:T(128)} %land_ref.5, bf16[48,8,128]{2,1,0:T(8,128)(2,1)} %state_hbm.1, f32[32,16,384]{2,1,0:T(8,128)} %bitcast.6, f32[8,16,384]{2,1,0:T(8,128)} %east_ref.1, f32[8,16,384]{2,1,0:T(8,128)} %kappa_ref.3, s32[16,384]{1,0:T(8,128)} %depth_ref.5), custom_call_target="tpu_custom_call" | custom-call | tf_op jit(solution)/shard_map/pack/pallas_call | solution.py:412
  3.0 0.0 copy-start.1
  3.0 0.0 copy-start.3
  3.0 0.0 copy-start.4
  3.1 14.0 %all-to-all-start = ((bf16[8,19,8,128]{3,2,1,0:T(8,128)(2,1)}), bf16[8,19,8,128]{3,2,1,0:T(8,128)(2,1)S(1)}, u32[]{:S(2)}, u32[]{:S(2)}) async-start(bf16[8,19,8,128]{3,2,1,0:T(8,128)(2,1)} %bitcast.15), calls=%async_computation | async-start | bytes 622592 | tf_op jit(solution)/shard_map/all_to_all | solution.py:408
  17.0 0.0 copy-start.12
  17.0 0.0 copy-start.13
  17.1 0.7 copy-done.12
  17.7 0.0 copy-done.13
  17.7 0.2 convert_reduce_fusion
  17.9 0.0 copy-start.9
  17.9 6.1 %all-to-all-done = bf16[8,19,8,128]{3,2,1,0:T(8,128)(2,1)S(1)} async-done(((bf16[8,19,8,128]{3,2,1,0:T(8,128)(2,1)}), bf16[8,19,8,128]{3,2,1,0:T(8,128)(2,1)S(1)}, u32[]{:S(2)}, u32[]{:S(2)}) %all-to-all-start) | async-done | bytes 311328 | tf_op jit(solution)/shard_map/all_to_all | solution.py:408
  24.0 0.0 copy-done
  24.0 0.0 copy-done.1
  24.0 0.0 copy-done.3
  24.0 0.0 copy-done.4
  24.1 0.0 copy-done.9
  24.1 0.0 copy-start.6
  24.1 0.0 copy-start.7
  24.1 0.0 copy-start.8
  24.1 0.7 rows.1
  24.8 0.0 copy-start.10
  24.8 9.1 %collective-permute-start = (bf16[69,8,128]{2,1,0:T(8,128)(2,1)S(1)}, bf16[69,8,128]{2,1,0:T(8,128)(2,1)S(1)}, u32[]{:S(2)}, u32[]{:S(2)}) collective-permute-start(bf16[69,8,128]{2,1,0:T(8,128)(2,1)S(1)} %get-tuple-element.15), channel_id=1, source_target_pairs={{0,760},{760,0},{16,8},{8,16},{32,24},{24,32},{48,40},{40,48},{64,... | collective-permute-start | bytes 423944 | tf_op jit(solution)/shard_map/ppermute | solution.py:454
  34.0 1.9 %collective-permute-start.1 = (bf16[69,8,128]{2,1,0:T(8,128)(2,1)S(1)}, bf16[69,8,128]{2,1,0:T(8,128)(2,1)S(1)}, u32[]{:S(2)}, u32[]{:S(2)}) collective-permute-start(bf16[69,8,128]{2,1,0:T(8,128)(2,1)S(1)} %get-tuple-element.16), channel_id=1, source_target_pairs={{0,8},{8,0},{16,24},{24,16},{32,40},{40,32},{48,56},{56,48},{64,72... | collective-permute-start | bytes 423944 | tf_op jit(solution)/shard_map/ppermute | solution.py:455
  35.9 1.0 %collective-permute-done.cross_ref.cross_halo_ref = bf16[69,8,128]{2,1,0:T(8,128)(2,1)S(1)} collective-permute-done((bf16[69,8,128]{2,1,0:T(8,128)(2,1)S(1)}, bf16[69,8,128]{2,1,0:T(8,128)(2,1)S(1)}, u32[]{:S(2)}, u32[]{:S(2)}) %collective-permute-start) | collective-permute-done | bytes 141344 | tf_op jit(solution)/shard_map/ppermute | solution.py:454
  36.9 2.9 %collective-permute-done.1.inner_ref.inner_halo_ref = bf16[69,8,128]{2,1,0:T(8,128)(2,1)S(1)} collective-permute-done((bf16[69,8,128]{2,1,0:T(8,128)(2,1)S(1)}, bf16[69,8,128]{2,1,0:T(8,128)(2,1)S(1)}, u32[]{:S(2)}, u32[]{:S(2)}) %collective-permute-start.1) | collective-permute-done | bytes 141344 | tf_op jit(solution)/shard_map/ppermute | solution.py:455
  39.8 0.0 copy-done.6
  39.8 0.0 copy-done.7
  39.8 0.0 copy-done.8
  39.8 0.0 copy-done.10
  39.8 2.0 %couple.1.after_ref = bf16[152,8,128]{2,1,0:T(8,128)(2,1)} custom-call(s32[48]{0:T(128)S(1)} %fusion.2.place_ref, bf16[152,8,128]{2,1,0:T(8,128)(2,1)S(1)} %bitcast.10, bf16[69,8,128]{2,1,0:T(8,128)(2,1)S(1)} %collective-permute-done.cross_ref.cross_halo_ref, bf16[69,8,128]{2,1,0:T(8,128)(2,1)S(1)} %collective-permute-done.1.inner_ref.inner_halo_ref, ...), custom_call_target="tpu_custom_call" | custom-call | tf_op jit(solution)/shard_map/couple/pallas_call | solution.py:457
  41.8 0.0 copy-start.2
  41.8 0.0 copy-start.5
  41.8 6.0 %all-to-all-start.1 = ((bf16[8,19,8,128]{3,2,1,0:T(8,128)(2,1)}), bf16[8,19,8,128]{3,2,1,0:T(8,128)(2,1)S(1)}, u32[]{:S(2)}, u32[]{:S(2)}) async-start(bf16[8,19,8,128]{3,2,1,0:T(8,128)(2,1)} %bitcast.3), calls=%async_computation.1 | async-start | bytes 622592 | tf_op jit(solution)/shard_map/all_to_all | solution.py:408
  47.8 0.0 copy-done.2
  47.8 0.0 copy-done.5
  47.8 0.6 copy-done.11
  48.4 3.7 %stencil.1 = (f32[32,16,384]{2,1,0:T(8,128)}, f32[4,16,384]{2,1,0:T(8,128)S(1)}, s32[48]{0:T(128)S(1)}) custom-call(s32[48]{0:T(128)S(1)} %copy-done.9, bf16[152,8,128]{2,1,0:T(8,128)(2,1)S(1)} %bitcast.11, bf16[69,8,128]{2,1,0:T(8,128)(2,1)S(1)} %collective-permute-done.cross_ref.cross_halo_ref, ...), custom_call_target="tpu_custom_call" | custom-call | flops 8000000 | bytes 3000000 | tf_op jit(solution)/shard_map/stencil/pallas_call | solution.py:467
  52.2 2.6 %all-to-all-done.1 = bf16[8,19,8,128]{3,2,1,0:T(8,128)(2,1)S(1)} async-done(((bf16[8,19,8,128]{3,2,1,0:T(8,128)(2,1)}), bf16[8,19,8,128]{3,2,1,0:T(8,128)(2,1)S(1)}, u32[]{:S(2)}, u32[]{:S(2)}) %all-to-all-start.1) | async-done | bytes 311328 | tf_op jit(solution)/shard_map/all_to_all | solution.py:408
  54.8 0.7 split.1
  55.4 6.7 %all-to-all-start.2 = ((f32[96,1,128]{2,1,0:T(1,128)}), f32[96,1,128]{2,1,0:T(1,128)S(1)}, u32[]{:S(2)}, u32[]{:S(2)}) async-start(f32[96,1,128]{2,1,0:T(1,128)} %get-tuple-element.21), calls=%async_computation.2 | async-start | bytes 98304 | tf_op jit(solution)/shard_map/all_to_all | solution.py:497
  62.1 6.6 %collective-permute-start.2 = (bf16[48,8,128]{2,1,0:T(8,128)(2,1)S(1)}, bf16[48,8,128]{2,1,0:T(8,128)(2,1)S(1)}, u32[]{:S(2)}, u32[]{:S(2)}) collective-permute-start(bf16[48,8,128]{2,1,0:T(8,128)(2,1)S(1)} %get-tuple-element.19), channel_id=1, source_target_pairs={{0,760},{760,0},{16,8},{8,16},{32,24},{24,32},{48,40},{40,48},{64,... | collective-permute-start | bytes 294920 | tf_op jit(solution)/shard_map/ppermute | solution.py:498
  68.7 1.9 %collective-permute-start.3 = (bf16[48,8,128]{2,1,0:T(8,128)(2,1)S(1)}, bf16[48,8,128]{2,1,0:T(8,128)(2,1)S(1)}, u32[]{:S(2)}, u32[]{:S(2)}) collective-permute-start(bf16[48,8,128]{2,1,0:T(8,128)(2,1)S(1)} %get-tuple-element.20), channel_id=1, source_target_pairs={{0,8},{8,0},{16,24},{24,16},{32,40},{40,32},{48,56},{56,48},{64,72... | collective-permute-start | bytes 294920 | tf_op jit(solution)/shard_map/ppermute | solution.py:499
  70.6 0.9 %collective-permute-done.2.cross_ref = bf16[48,8,128]{2,1,0:T(8,128)(2,1)S(1)} collective-permute-done((bf16[48,8,128]{2,1,0:T(8,128)(2,1)S(1)}, bf16[48,8,128]{2,1,0:T(8,128)(2,1)S(1)}, u32[]{:S(2)}, u32[]{:S(2)}) %collective-permute-start.2) | collective-permute-done | bytes 98336 | tf_op jit(solution)/shard_map/ppermute | solution.py:498
  71.6 2.8 %collective-permute-done.3.inner_ref = bf16[48,8,128]{2,1,0:T(8,128)(2,1)S(1)} collective-permute-done((bf16[48,8,128]{2,1,0:T(8,128)(2,1)S(1)}, bf16[48,8,128]{2,1,0:T(8,128)(2,1)S(1)}, u32[]{:S(2)}, u32[]{:S(2)}) %collective-permute-start.3) | collective-permute-done | bytes 98336 | tf_op jit(solution)/shard_map/ppermute | solution.py:499
  74.4 0.7 all-to-all-done.2.heat_ref
  75.0 1.6 %finish.1 = (bf16[48,8,128]{2,1,0:T(8,128)(2,1)}, f32[4,8,16,384]{3,2,1,0:T(8,128)}) custom-call(s32[48]{0:T(128)S(1)} %get-tuple-element.18.done_ref.code_ref, s32[48]{0:T(128)S(1)} %copy-done.9, bf16[152,8,128]{2,1,0:T(8,128)(2,1)S(1)} %bitcast.13, bf16[48,8,128]{2,1,0:T(8,128)(2,1)S(1)} %collective-permute-done.2.cross_ref, ...), custom_call_target="tpu_custom_call", output_to_operand_aliasing={{1}: (8, {})} | custom-call | tf_op jit(solution)/shard_map/finish/pallas_call | solution.py:502
  (2 shorter events, 0.0 us)
Async XLA Ops:
  0.6 23.4 %copy-start = (f32[4,8,16,384]{3,2,1,0:T(8,128)S(1)}, f32[4,8,16,384]{3,2,1,0:T(8,128)}, u32[]{:S(2)}) copy-start(f32[4,8,16,384]{3,2,1,0:T(8,128)} %param.16) | copy-start | bytes 2359300
  3.0 21.0 %copy-start.1 = (f32[8,16,384]{2,1,0:T(8,128)S(1)}, f32[8,16,384]{2,1,0:T(8,128)}, u32[]{:S(2)}) copy-start(f32[8,16,384]{2,1,0:T(8,128)} %kappa_ref.3) | copy-start | bytes 589828
  3.0 21.0 %copy-start.3 = (f32[8,16,384]{2,1,0:T(8,128)S(1)}, f32[8,16,384]{2,1,0:T(8,128)}, u32[]{:S(2)}) copy-start(f32[8,16,384]{2,1,0:T(8,128)} %north_ref.3) | copy-start | bytes 589828
  3.0 21.0 %copy-start.4 = (s32[16,384]{1,0:T(8,128)S(1)}, s32[16,384]{1,0:T(8,128)}, u32[]{:S(2)}) copy-start(s32[16,384]{1,0:T(8,128)} %depth_ref.5) | copy-start | bytes 73732
  3.1 21.0 %all-to-all-start = ((bf16[8,19,8,128]{3,2,1,0:T(8,128)(2,1)}), bf16[8,19,8,128]{3,2,1,0:T(8,128)(2,1)S(1)}, u32[]{:S(2)}, u32[]{:S(2)}) async-start(bf16[8,19,8,128]{3,2,1,0:T(8,128)(2,1)} %bitcast.15), calls=%async_computation | async-start | bytes 622592 | tf_op jit(solution)/shard_map/all_to_all | solution.py:408
  17.0 0.7 copy-start.12
  17.0 0.7 copy-start.13
  17.9 6.2 %copy-start.9 = (s32[48]{0:T(128)S(1)}, s32[48]{0:T(128)}, u32[]{:S(2)}) copy-start(s32[48]{0:T(128)} %land_ref.5) | copy-start | bytes 580
  24.1 15.7 %copy-start.6 = (f32[48,8,128]{2,1,0:T(8,128)S(1)}, f32[48,8,128]{2,1,0:T(8,128)}, u32[]{:S(2)}) copy-start(f32[48,8,128]{2,1,0:T(8,128)} %atm_ref.1) | copy-start | bytes 589828
  24.1 15.7 %copy-start.7 = (f32[48,128]{1,0:T(8,128)S(1)}, f32[48,128]{1,0:T(8,128)}, u32[]{:S(2)}) copy-start(f32[48,128]{1,0:T(8,128)} %coef_ref.1) | copy-start | bytes 73732
  24.1 15.7 %copy-start.8 = (f32[48,128]{1,0:T(8,128)S(1)}, f32[48,128]{1,0:T(8,128)}, u32[]{:S(2)}) copy-start(f32[48,128]{1,0:T(8,128)} %sun_ref.1) | copy-start | bytes 73732
  24.8 15.0 %copy-start.10 = (f32[8,8]{1,0:T(8,128)S(1)}, f32[8,8]{1,0:T(8,128)}, u32[]{:S(2)}) copy-start(f32[8,8]{1,0:T(8,128)} %mixing_ref.1) | copy-start | bytes 772
  24.8 12.1 %collective-permute-start = (bf16[69,8,128]{2,1,0:T(8,128)(2,1)S(1)}, bf16[69,8,128]{2,1,0:T(8,128)(2,1)S(1)}, u32[]{:S(2)}, u32[]{:S(2)}) collective-permute-start(bf16[69,8,128]{2,1,0:T(8,128)(2,1)S(1)} %get-tuple-element.15), channel_id=1, source_target_pairs={{0,760},{760,0},{16,8},{8,16},{32,24},{24,32},{48,40},{40,48},{64,... | collective-permute-start | bytes 423944 | tf_op jit(solution)/shard_map/ppermute | solution.py:454
  34.0 5.8 %collective-permute-start.1 = (bf16[69,8,128]{2,1,0:T(8,128)(2,1)S(1)}, bf16[69,8,128]{2,1,0:T(8,128)(2,1)S(1)}, u32[]{:S(2)}, u32[]{:S(2)}) collective-permute-start(bf16[69,8,128]{2,1,0:T(8,128)(2,1)S(1)} %get-tuple-element.16), channel_id=1, source_target_pairs={{0,8},{8,0},{16,24},{24,16},{32,40},{40,32},{48,56},{56,48},{64,72... | collective-permute-start | bytes 423944 | tf_op jit(solution)/shard_map/ppermute | solution.py:455
  41.8 6.0 %copy-start.2 = (f32[8,16,384]{2,1,0:T(8,128)S(1)}, f32[8,16,384]{2,1,0:T(8,128)}, u32[]{:S(2)}) copy-start(f32[8,16,384]{2,1,0:T(8,128)} %east_ref.1) | copy-start | bytes 589828
  41.8 6.0 %copy-start.5 = (f32[8,16,384]{2,1,0:T(8,128)S(1)}, f32[8,16,384]{2,1,0:T(8,128)}, u32[]{:S(2)}) copy-start(f32[8,16,384]{2,1,0:T(8,128)} %cross_ref.1) | copy-start | bytes 589828
  41.8 13.0 %all-to-all-start.1 = ((bf16[8,19,8,128]{3,2,1,0:T(8,128)(2,1)}), bf16[8,19,8,128]{3,2,1,0:T(8,128)(2,1)S(1)}, u32[]{:S(2)}, u32[]{:S(2)}) async-start(bf16[8,19,8,128]{3,2,1,0:T(8,128)(2,1)} %bitcast.3), calls=%async_computation.1 | async-start | bytes 622592 | tf_op jit(solution)/shard_map/all_to_all | solution.py:408
  47.8 0.7 copy-start.11
  55.4 19.6 %all-to-all-start.2 = ((f32[96,1,128]{2,1,0:T(1,128)}), f32[96,1,128]{2,1,0:T(1,128)S(1)}, u32[]{:S(2)}, u32[]{:S(2)}) async-start(f32[96,1,128]{2,1,0:T(1,128)} %get-tuple-element.21), calls=%async_computation.2 | async-start | bytes 98304 | tf_op jit(solution)/shard_map/all_to_all | solution.py:497
  62.1 9.4 %collective-permute-start.2 = (bf16[48,8,128]{2,1,0:T(8,128)(2,1)S(1)}, bf16[48,8,128]{2,1,0:T(8,128)(2,1)S(1)}, u32[]{:S(2)}, u32[]{:S(2)}) collective-permute-start(bf16[48,8,128]{2,1,0:T(8,128)(2,1)S(1)} %get-tuple-element.19), channel_id=1, source_target_pairs={{0,760},{760,0},{16,8},{8,16},{32,24},{24,32},{48,40},{40,48},{64,... | collective-permute-start | bytes 294920 | tf_op jit(solution)/shard_map/ppermute | solution.py:498
  68.7 5.7 %collective-permute-start.3 = (bf16[48,8,128]{2,1,0:T(8,128)(2,1)S(1)}, bf16[48,8,128]{2,1,0:T(8,128)(2,1)S(1)}, u32[]{:S(2)}, u32[]{:S(2)}) collective-permute-start(bf16[48,8,128]{2,1,0:T(8,128)(2,1)S(1)} %get-tuple-element.20), channel_id=1, source_target_pairs={{0,8},{8,0},{16,24},{24,16},{32,40},{40,32},{48,56},{56,48},{64,72... | collective-permute-start | bytes 294920 | tf_op jit(solution)/shard_map/ppermute | solution.py:499

commit v7 on v5

--- a/solution.py
+++ b/solution.py
@@ -143,7 +143,7 @@
             out_ref[48 + 18 + j] = last.astype(BF16)
 
 
-def couple_kernel(place_ref, came_ref, cross_ref, inner_ref, atm_ref, coef_ref, sun_ref, mixing_ref,
+def couple_kernel(place_ref, came_ref, inner_ref, cross_ref, atm_ref, coef_ref, sun_ref, mixing_ref,
                   out_ref, got_ref):
     odd = lax.rem(lax.axis_index("lat"), 2)
     cross_off = jnp.where(odd == 1, 0, 2)
@@ -207,7 +207,7 @@
     heat_ref[...] = jnp.broadcast_to(row[None], (lats, 1, 128))
 
 
-def stencil_kernel(lats, land_ref, came_ref, cross_halo_ref, inner_halo_ref, tracer_ref, east_ref, north_ref,
+def stencil_kernel(lats, land_ref, came_ref, inner_halo_ref, cross_halo_ref, tracer_ref, east_ref, north_ref,
                    kappa_ref, cross_ref, depth_ref, code_ref, after_ref, out_ref, top_ref, done_ref, rows_ref,
                    diag_ref, bottom_ref):
     lat = lax.axis_index("lat")
@@ -454,8 +454,8 @@
         diffusivity,
         depth_levels,
     )
+    inner = lax.ppermute(inner, "lat", inner_pairs)
     cross = lax.ppermute(cross, "lat", cross_pairs)
-    inner = lax.ppermute(inner, "lat", inner_pairs)
 
     backward = call(
         couple_kernel,
@@ -464,7 +464,7 @@
         shape(flat, BF16),
         VMEM,
         [pltpu.VMEM((48, 8, 128), F32)],
-    )(place, came, cross, inner, atm_state, exchange_coef, sunlight, mixing)
+    )(place, came, inner, cross, atm_state, exchange_coef, sunlight, mixing)
     back = turn(backward)
 
     step, top, done = call(
@@ -478,8 +478,8 @@
     )(
         land_mask,
         came,
+        inner,
         cross,
-        inner,
         tracers_l,
         east_velocity,
         north_velocity,

time: 77.8 us -> 79.5 us (1.022)
  starting transfers between devices: 46.2 us -> 49.4 us
  waiting for transfers between devices: 17.4 us -> 15.9 us
    ppermute x1, waiting for transfers between devices: 2.91 us -> 0.01 us  [shards(): inner = lax.ppermute(inner, 'lat', inner_pairs)]
    all_to_all x1, starting transfers between devices: 6.7 us -> 9.11 us  [shards(): heat = lax.all_to_all(heat, 'lat', 0, 0, tiled=True)]
    ppermute x1, waiting for transfers between devices: 0.96 us -> 2.42 us  [shards(): cross = lax.ppermute(cross, 'lat', cross_pairs)]
    ppermute x1, starting transfers between devices: 9.14 us -> 10.2 us  [shards(): cross = lax.ppermute(cross, 'lat', cross_pairs)]
  transfers between devices with their start and end apart: 7 -> 7, of which waited for: 7 -> 6; matrix products, arithmetic and copies ran while one was open for 0% -> 0% of each run, Pallas kernels for 5% -> 5%
where the time goes in v7:
time: 79.5 us; the launch traced here: 78.7 us
  starting transfers between devices  49.4 us (62%)
  waiting for transfers between devices  15.9 us (20%)
  Pallas kernels  10.9 us (14%)
  local copies, waits for them, and re-layouts  1.38 us (2%)
  between operations  0.82 us (1%)
    all_to_all x2, starting transfers between devices, turn(): return lax.all_to_all(values, 'lon', 0, 0, tiled=True).reshape(flat)  19.7 us
    ppermute x1, starting transfers between devices, shards(): cross = lax.ppermute(cross, 'lat', cross_pairs)  10.2 us
    all_to_all x1, starting transfers between devices, shards(): heat = lax.all_to_all(heat, 'lat', 0, 0, tiled=True)  9.11 us
    all_to_all x2, waiting for transfers between devices, turn(): return lax.all_to_all(values, 'lon', 0, 0, tiled=True).reshape(flat)  9.07 us
    ppermute x1, starting transfers between devices, shards(): back_cross = lax.ppermute(back_cross, 'lat', cross_pairs)  6.55 us
    pallas_call x1, Pallas kernels, shards(): call(functools.partial(stencil_kernel, lats), 'stencil', [SMEM] + [VMEM]...  3.68 us
    ppermute x1, waiting for transfers between devices, shards(): back_inner = lax.ppermute(back_inner, 'lat', inner_pairs)  2.83 us
    ppermute x1, waiting for transfers between devices, shards(): cross = lax.ppermute(cross, 'lat', cross_pairs)  2.42 us
  transfers between devices with their start and end apart: 7, of which 6 were waited for; matrix products, arithmetic and copies ran while one was open for 0% of the time, Pallas kernels for 5%

profile of v7, /device:TPU:1, one launch (start us, length us, event | category | flops | bytes accessed | tf_op | source)
XLA Modules:
  0.0 78.7 jit_solution(15794744314948961081)
XLA Ops:
  0.6 0.0 copy-start
  0.6 2.3 %pack.1 = (bf16[160,8,128]{2,1,0:T(8,128)(2,1)}, s32[48]{0:T(128)}) custom-call(s32[48]{0:T(128)} %dest_hbm.1, s32[48]{0:T(128)} %land_ref.5, bf16[48,8,128]{2,1,0:T(8,128)(2,1)} %state_hbm.1, f32[32,16,384]{2,1,0:T(8,128)} %bitcast.6, f32[8,16,384]{2,1,0:T(8,128)} %east_ref.1, f32[8,16,384]{2,1,0:T(8,128)} %kappa_ref.3, s32[16,384]{1,0:T(8,128)} %depth_ref.5), custom_call_target="tpu_custom_call" | custom-call | tf_op jit(solution)/shard_map/pack/pallas_call | solution.py:415
  3.0 0.0 copy-start.1
  3.0 0.0 copy-start.3
  3.0 0.0 copy-start.4
  3.0 14.0 %all-to-all-start = ((bf16[8,20,8,128]{3,2,1,0:T(8,128)(2,1)}), bf16[8,20,8,128]{3,2,1,0:T(8,128)(2,1)S(1)}, u32[]{:S(2)}, u32[]{:S(2)}) async-start(bf16[8,20,8,128]{3,2,1,0:T(8,128)(2,1)} %bitcast.15), calls=%async_computation | async-start | bytes 655360 | tf_op jit(solution)/shard_map/all_to_all | solution.py:411
  17.0 0.0 copy-start.13
  17.0 0.7 copy-done.12
  17.7 0.0 copy-done.13
  17.7 0.2 convert_reduce_fusion
  17.8 0.0 copy-start.9
  17.9 6.3 %all-to-all-done = bf16[8,20,8,128]{3,2,1,0:T(8,128)(2,1)S(1)} async-done(((bf16[8,20,8,128]{3,2,1,0:T(8,128)(2,1)}), bf16[8,20,8,128]{3,2,1,0:T(8,128)(2,1)S(1)}, u32[]{:S(2)}, u32[]{:S(2)}) %all-to-all-start) | async-done | bytes 327712 | tf_op jit(solution)/shard_map/all_to_all | solution.py:411
  24.1 0.0 copy-done
  24.1 0.0 copy-done.1
  24.1 0.0 copy-done.3
  24.1 0.0 copy-done.4
  24.2 0.0 copy-done.9
  24.2 0.0 copy-start.6
  24.2 0.0 copy-start.7
  24.2 0.0 copy-start.8
  24.2 0.7 rows.1
  24.9 0.0 copy-start.10
  24.9 1.9 %collective-permute-start = (bf16[69,8,128]{2,1,0:T(8,128)(2,1)S(1)}, bf16[69,8,128]{2,1,0:T(8,128)(2,1)S(1)}, u32[]{:S(2)}, u32[]{:S(2)}) collective-permute-start(bf16[69,8,128]{2,1,0:T(8,128)(2,1)S(1)} %get-tuple-element.15), channel_id=1, source_target_pairs={{0,8},{8,0},{16,24},{24,16},{32,40},{40,32},{48,56},{56,48},{64,72... | collective-permute-start | bytes 423944 | tf_op jit(solution)/shard_map/ppermute | solution.py:457
  26.8 10.2 %collective-permute-start.1 = (bf16[69,8,128]{2,1,0:T(8,128)(2,1)S(1)}, bf16[69,8,128]{2,1,0:T(8,128)(2,1)S(1)}, u32[]{:S(2)}, u32[]{:S(2)}) collective-permute-start(bf16[69,8,128]{2,1,0:T(8,128)(2,1)S(1)} %get-tuple-element.16), channel_id=1, source_target_pairs={{0,760},{760,0},{16,8},{8,16},{32,24},{24,32},{48,40},{40,48},{64,... | collective-permute-start | bytes 423944 | tf_op jit(solution)/shard_map/ppermute | solution.py:458
  37.1 0.0 collective-permute-done.inner_ref.inner_halo_ref
  37.1 2.4 %collective-permute-done.1.cross_ref.cross_halo_ref = bf16[69,8,128]{2,1,0:T(8,128)(2,1)S(1)} collective-permute-done((bf16[69,8,128]{2,1,0:T(8,128)(2,1)S(1)}, bf16[69,8,128]{2,1,0:T(8,128)(2,1)S(1)}, u32[]{:S(2)}, u32[]{:S(2)}) %collective-permute-start.1) | collective-permute-done | bytes 141344 | tf_op jit(solution)/shard_map/ppermute | solution.py:458
  39.5 0.0 copy-done.6
  39.5 0.0 copy-done.7
  39.5 0.0 copy-done.8
  39.5 0.0 copy-done.10
  39.5 2.0 %couple.1.after_ref = bf16[160,8,128]{2,1,0:T(8,128)(2,1)} custom-call(s32[48]{0:T(128)S(1)} %fusion.2.place_ref, bf16[160,8,128]{2,1,0:T(8,128)(2,1)S(1)} %bitcast.10, bf16[69,8,128]{2,1,0:T(8,128)(2,1)S(1)} %collective-permute-done.inner_ref.inner_halo_ref, bf16[69,8,128]{2,1,0:T(8,128)(2,1)S(1)} %collective-permute-done.1.cross_ref.cross_halo_ref, ...), custom_call_target="tpu_custom_call" | custom-call | tf_op jit(solution)/shard_map/couple/pallas_call | solution.py:460
  41.5 0.0 copy-start.2
  41.5 0.0 copy-start.5
  41.5 5.7 %all-to-all-start.1 = ((bf16[8,20,8,128]{3,2,1,0:T(8,128)(2,1)}), bf16[8,20,8,128]{3,2,1,0:T(8,128)(2,1)S(1)}, u32[]{:S(2)}, u32[]{:S(2)}) async-start(bf16[8,20,8,128]{3,2,1,0:T(8,128)(2,1)} %bitcast.3), calls=%async_computation.1 | async-start | bytes 655360 | tf_op jit(solution)/shard_map/all_to_all | solution.py:411
  47.3 0.0 copy-start.11
  47.3 0.0 copy-done.2
  47.3 0.0 copy-done.5
  47.3 0.6 copy-done.11
  47.9 3.7 %stencil.1 = (f32[32,16,384]{2,1,0:T(8,128)}, f32[4,16,384]{2,1,0:T(8,128)S(1)}, s32[48]{0:T(128)S(1)}) custom-call(s32[48]{0:T(128)S(1)} %copy-done.9, bf16[160,8,128]{2,1,0:T(8,128)(2,1)S(1)} %bitcast.11, bf16[69,8,128]{2,1,0:T(8,128)(2,1)S(1)} %collective-permute-done.inner_ref.inner_halo_ref, ...), custom_call_target="tpu_custom_call" | custom-call | flops 8000000 | bytes 3000000 | tf_op jit(solution)/shard_map/stencil/pallas_call | solution.py:470
  51.6 2.8 %all-to-all-done.1 = bf16[8,20,8,128]{3,2,1,0:T(8,128)(2,1)S(1)} async-done(((bf16[8,20,8,128]{3,2,1,0:T(8,128)(2,1)}), bf16[8,20,8,128]{3,2,1,0:T(8,128)(2,1)S(1)}, u32[]{:S(2)}, u32[]{:S(2)}) %all-to-all-start.1) | async-done | bytes 327712 | tf_op jit(solution)/shard_map/all_to_all | solution.py:411
  54.4 0.7 split.1
  55.1 9.1 %all-to-all-start.2 = ((f32[96,1,128]{2,1,0:T(1,128)}), f32[96,1,128]{2,1,0:T(1,128)S(1)}, u32[]{:S(2)}, u32[]{:S(2)}) async-start(f32[96,1,128]{2,1,0:T(1,128)} %get-tuple-element.21), calls=%async_computation.2 | async-start | bytes 98304 | tf_op jit(solution)/shard_map/all_to_all | solution.py:500
  64.2 6.6 %collective-permute-start.2 = (bf16[48,8,128]{2,1,0:T(8,128)(2,1)S(1)}, bf16[48,8,128]{2,1,0:T(8,128)(2,1)S(1)}, u32[]{:S(2)}, u32[]{:S(2)}) collective-permute-start(bf16[48,8,128]{2,1,0:T(8,128)(2,1)S(1)} %get-tuple-element.19), channel_id=1, source_target_pairs={{0,760},{760,0},{16,8},{8,16},{32,24},{24,32},{48,40},{40,48},{64,... | collective-permute-start | bytes 294920 | tf_op jit(solution)/shard_map/ppermute | solution.py:501
  70.7 1.9 %collective-permute-start.3 = (bf16[48,8,128]{2,1,0:T(8,128)(2,1)S(1)}, bf16[48,8,128]{2,1,0:T(8,128)(2,1)S(1)}, u32[]{:S(2)}, u32[]{:S(2)}) collective-permute-start(bf16[48,8,128]{2,1,0:T(8,128)(2,1)S(1)} %get-tuple-element.20), channel_id=1, source_target_pairs={{0,8},{8,0},{16,24},{24,16},{32,40},{40,32},{48,56},{56,48},{64,72... | collective-permute-start | bytes 294920 | tf_op jit(solution)/shard_map/ppermute | solution.py:502
  72.7 0.9 %collective-permute-done.2.cross_ref = bf16[48,8,128]{2,1,0:T(8,128)(2,1)S(1)} collective-permute-done((bf16[48,8,128]{2,1,0:T(8,128)(2,1)S(1)}, bf16[48,8,128]{2,1,0:T(8,128)(2,1)S(1)}, u32[]{:S(2)}, u32[]{:S(2)}) %collective-permute-start.2) | collective-permute-done | bytes 98336 | tf_op jit(solution)/shard_map/ppermute | solution.py:501
  73.6 2.8 %collective-permute-done.3.inner_ref = bf16[48,8,128]{2,1,0:T(8,128)(2,1)S(1)} collective-permute-done((bf16[48,8,128]{2,1,0:T(8,128)(2,1)S(1)}, bf16[48,8,128]{2,1,0:T(8,128)(2,1)S(1)}, u32[]{:S(2)}, u32[]{:S(2)}) %collective-permute-start.3) | collective-permute-done | bytes 98336 | tf_op jit(solution)/shard_map/ppermute | solution.py:502
  76.4 0.7 all-to-all-done.2.heat_ref
  77.1 1.6 %finish.1 = (bf16[48,8,128]{2,1,0:T(8,128)(2,1)}, f32[4,8,16,384]{3,2,1,0:T(8,128)}) custom-call(s32[48]{0:T(128)S(1)} %get-tuple-element.18.done_ref.code_ref, s32[48]{0:T(128)S(1)} %copy-done.9, bf16[160,8,128]{2,1,0:T(8,128)(2,1)S(1)} %bitcast.13, bf16[48,8,128]{2,1,0:T(8,128)(2,1)S(1)} %collective-permute-done.2.cross_ref, ...), custom_call_target="tpu_custom_call", output_to_operand_aliasing={{1}: (8, {})} | custom-call | tf_op jit(solution)/shard_map/finish/pallas_call | solution.py:505
  (2 shorter events, 0.0 us)
Async XLA Ops:
  0.6 23.5 %copy-start = (f32[4,8,16,384]{3,2,1,0:T(8,128)S(1)}, f32[4,8,16,384]{3,2,1,0:T(8,128)}, u32[]{:S(2)}) copy-start(f32[4,8,16,384]{3,2,1,0:T(8,128)} %param.16) | copy-start | bytes 2359300
  3.0 21.2 %copy-start.1 = (f32[8,16,384]{2,1,0:T(8,128)S(1)}, f32[8,16,384]{2,1,0:T(8,128)}, u32[]{:S(2)}) copy-start(f32[8,16,384]{2,1,0:T(8,128)} %kappa_ref.3) | copy-start | bytes 589828
  3.0 21.2 %copy-start.3 = (f32[8,16,384]{2,1,0:T(8,128)S(1)}, f32[8,16,384]{2,1,0:T(8,128)}, u32[]{:S(2)}) copy-start(f32[8,16,384]{2,1,0:T(8,128)} %north_ref.3) | copy-start | bytes 589828
  3.0 21.2 %copy-start.4 = (s32[16,384]{1,0:T(8,128)S(1)}, s32[16,384]{1,0:T(8,128)}, u32[]{:S(2)}) copy-start(s32[16,384]{1,0:T(8,128)} %depth_ref.5) | copy-start | bytes 73732
  3.0 21.1 %all-to-all-start = ((bf16[8,20,8,128]{3,2,1,0:T(8,128)(2,1)}), bf16[8,20,8,128]{3,2,1,0:T(8,128)(2,1)S(1)}, u32[]{:S(2)}, u32[]{:S(2)}) async-start(bf16[8,20,8,128]{3,2,1,0:T(8,128)(2,1)} %bitcast.15), calls=%async_computation | async-start | bytes 655360 | tf_op jit(solution)/shard_map/all_to_all | solution.py:411
  17.0 0.7 copy-start.12
  17.0 0.7 copy-start.13
  17.8 6.3 %copy-start.9 = (s32[48]{0:T(128)S(1)}, s32[48]{0:T(128)}, u32[]{:S(2)}) copy-start(s32[48]{0:T(128)} %land_ref.5) | copy-start | bytes 580
  24.2 15.3 %copy-start.6 = (f32[48,8,128]{2,1,0:T(8,128)S(1)}, f32[48,8,128]{2,1,0:T(8,128)}, u32[]{:S(2)}) copy-start(f32[48,8,128]{2,1,0:T(8,128)} %atm_ref.1) | copy-start | bytes 589828
  24.2 15.3 %copy-start.7 = (f32[48,128]{1,0:T(8,128)S(1)}, f32[48,128]{1,0:T(8,128)}, u32[]{:S(2)}) copy-start(f32[48,128]{1,0:T(8,128)} %coef_ref.1) | copy-start | bytes 73732
  24.2 15.3 %copy-start.8 = (f32[48,128]{1,0:T(8,128)S(1)}, f32[48,128]{1,0:T(8,128)}, u32[]{:S(2)}) copy-start(f32[48,128]{1,0:T(8,128)} %sun_ref.1) | copy-start | bytes 73732
  24.9 14.6 %copy-start.10 = (f32[8,8]{1,0:T(8,128)S(1)}, f32[8,8]{1,0:T(8,128)}, u32[]{:S(2)}) copy-start(f32[8,8]{1,0:T(8,128)} %mixing_ref.1) | copy-start | bytes 772
  24.9 12.2 %collective-permute-start = (bf16[69,8,128]{2,1,0:T(8,128)(2,1)S(1)}, bf16[69,8,128]{2,1,0:T(8,128)(2,1)S(1)}, u32[]{:S(2)}, u32[]{:S(2)}) collective-permute-start(bf16[69,8,128]{2,1,0:T(8,128)(2,1)S(1)} %get-tuple-element.15), channel_id=1, source_target_pairs={{0,8},{8,0},{16,24},{24,16},{32,40},{40,32},{48,56},{56,48},{64,72... | collective-permute-start | bytes 423944 | tf_op jit(solution)/shard_map/ppermute | solution.py:457
  26.8 12.7 %collective-permute-start.1 = (bf16[69,8,128]{2,1,0:T(8,128)(2,1)S(1)}, bf16[69,8,128]{2,1,0:T(8,128)(2,1)S(1)}, u32[]{:S(2)}, u32[]{:S(2)}) collective-permute-start(bf16[69,8,128]{2,1,0:T(8,128)(2,1)S(1)} %get-tuple-element.16), channel_id=1, source_target_pairs={{0,760},{760,0},{16,8},{8,16},{32,24},{24,32},{48,40},{40,48},{64,... | collective-permute-start | bytes 423944 | tf_op jit(solution)/shard_map/ppermute | solution.py:458
  41.5 5.8 %copy-start.2 = (f32[8,16,384]{2,1,0:T(8,128)S(1)}, f32[8,16,384]{2,1,0:T(8,128)}, u32[]{:S(2)}) copy-start(f32[8,16,384]{2,1,0:T(8,128)} %east_ref.1) | copy-start | bytes 589828
  41.5 5.8 %copy-start.5 = (f32[8,16,384]{2,1,0:T(8,128)S(1)}, f32[8,16,384]{2,1,0:T(8,128)}, u32[]{:S(2)}) copy-start(f32[8,16,384]{2,1,0:T(8,128)} %cross_ref.1) | copy-start | bytes 589828
  41.5 12.9 %all-to-all-start.1 = ((bf16[8,20,8,128]{3,2,1,0:T(8,128)(2,1)}), bf16[8,20,8,128]{3,2,1,0:T(8,128)(2,1)S(1)}, u32[]{:S(2)}, u32[]{:S(2)}) async-start(bf16[8,20,8,128]{3,2,1,0:T(8,128)(2,1)} %bitcast.3), calls=%async_computation.1 | async-start | bytes 655360 | tf_op jit(solution)/shard_map/all_to_all | solution.py:411
  47.3 0.7 copy-start.11
  55.1 22.0 %all-to-all-start.2 = ((f32[96,1,128]{2,1,0:T(1,128)}), f32[96,1,128]{2,1,0:T(1,128)S(1)}, u32[]{:S(2)}, u32[]{:S(2)}) async-start(f32[96,1,128]{2,1,0:T(1,128)} %get-tuple-element.21), calls=%async_computation.2 | async-start | bytes 98304 | tf_op jit(solution)/shard_map/all_to_all | solution.py:500
  64.2 9.4 %collective-permute-start.2 = (bf16[48,8,128]{2,1,0:T(8,128)(2,1)S(1)}, bf16[48,8,128]{2,1,0:T(8,128)(2,1)S(1)}, u32[]{:S(2)}, u32[]{:S(2)}) collective-permute-start(bf16[48,8,128]{2,1,0:T(8,128)(2,1)S(1)} %get-tuple-element.19), channel_id=1, source_target_pairs={{0,760},{760,0},{16,8},{8,16},{32,24},{24,32},{48,40},{40,48},{64,... | collective-permute-start | bytes 294920 | tf_op jit(solution)/shard_map/ppermute | solution.py:501
  70.7 5.7 %collective-permute-start.3 = (bf16[48,8,128]{2,1,0:T(8,128)(2,1)S(1)}, bf16[48,8,128]{2,1,0:T(8,128)(2,1)S(1)}, u32[]{:S(2)}, u32[]{:S(2)}) collective-permute-start(bf16[48,8,128]{2,1,0:T(8,128)(2,1)S(1)} %get-tuple-element.20), channel_id=1, source_target_pairs={{0,8},{8,0},{16,24},{24,16},{32,40},{40,32},{48,56},{56,48},{64,72... | collective-permute-start | bytes 294920 | tf_op jit(solution)/shard_map/ppermute | solution.py:502

commit v8 on v5

--- a/solution.py
+++ b/solution.py
@@ -208,7 +208,8 @@
 
 
 def stencil_kernel(lats, land_ref, came_ref, cross_halo_ref, inner_halo_ref, tracer_ref, east_ref, north_ref,
-                   kappa_ref, cross_ref, depth_ref, code_ref, after_ref, out_ref, top_ref, done_ref, rows_ref,
+                   kappa_ref, cross_ref, depth_ref, code_ref, after_ref, out_ref, top_ref, gain_ref, done_ref,
+                   rows_ref,
                    diag_ref, bottom_ref):
     lat = lax.axis_index("lat")
     lon = lax.axis_index("lon")
@@ -327,11 +328,12 @@
     lax.fori_loop(0, 8, level_step, 0)
     for t in range(4):
         top_ref[t] = out_ref[8 * t]
+    gain_ref[...] = jnp.where(bottom > 0.0, 0.5, 0.0)
     for t in range(48):
-        done_ref[t] = code_ref[t]
-
-
-def finish_kernel(points, code_ref, land_ref, back_ref, cross_ref, inner_ref, heat_ref, depth_ref,
+        done_ref[t] = code_ref[t] + 256 * land_ref[t]
+
+
+def finish_kernel(points, code_ref, back_ref, cross_ref, inner_ref, heat_ref, gain_ref,
                   top_ref, step_hbm, flux_ref, out_ref, wide_ref):
     odd = lax.rem(lax.axis_index("lat"), 2)
     cross_off = jnp.where(odd == 1, 2, 0)
@@ -339,21 +341,20 @@
         code = code_ref[t]
         rank = lax.bitwise_and(code, 7)
         dlon = lax.bitwise_and(lax.shift_right_logical(code, 3), 7)
-        off = lax.shift_right_logical(code, 6)
+        off = lax.bitwise_and(lax.shift_right_logical(code, 6), 3)
         at = dlon * PAIR + rank
         own = back_ref[dlon * SLOTS + PAIR + rank].astype(F32)
         cross = cross_ref[at].astype(F32)
         inner = inner_ref[at].astype(F32)
         value = jnp.where(off == 1, own, jnp.where(off == cross_off, cross, inner))
-        value = jnp.where(land_ref[t] > 0, value, 0.0)
+        value = jnp.where(code >= 256, value, 0.0)
         flux_ref[t] = value.astype(BF16)
         wide_ref[8 * t : 8 * t + 8, :] = value
     heat = jnp.sum(jnp.sum(heat_ref[...], axis=0), axis=1, keepdims=True)
     correction = heat / points
     for j in range(3):
         cols = slice(128 * j, 128 * j + 128)
-        wet = depth_ref[:, cols].astype(F32) * tile_column(land_ref, j)
-        gain = jnp.where(wet > 0.0, 0.5, 0.0)
+        gain = gain_ref[:, cols]
         for t in range(4):
             force = wide_ref[pl.ds(8 * j + t, 16, stride=24), :]
             if t == 0:
@@ -467,12 +468,12 @@
     )(place, came, cross, inner, atm_state, exchange_coef, sunlight, mixing)
     back = turn(backward)
 
-    step, top, done = call(
+    step, top, gain, done = call(
         functools.partial(stencil_kernel, lats),
         "stencil",
         [SMEM] + [VMEM] * 9 + [SMEM, ANY],
-        (shape((32, 16, 384), F32), shape((4, 16, 384), F32), shape((48,), jnp.int32)),
-        (VMEM, VMEM, SMEM),
+        (shape((32, 16, 384), F32), shape((4, 16, 384), F32), shape((16, 384), F32), shape((48,), jnp.int32)),
+        (VMEM, VMEM, VMEM, SMEM),
         [pltpu.VMEM((2, 56, 384), F32), pltpu.VMEM((2, 32, 384), F32), pltpu.VMEM((5, 16, 384), F32)],
         cost_estimate=pl.CostEstimate(flops=8000000, bytes_accessed=3000000, transcendentals=0),
     )(
@@ -505,13 +506,13 @@
     ocean_flux, new_tracers = call(
         functools.partial(finish_kernel, points),
         "finish",
-        [SMEM, SMEM, VMEM, VMEM, VMEM, VMEM, VMEM, VMEM, ANY],
+        [SMEM, VMEM, VMEM, VMEM, VMEM, VMEM, VMEM, ANY],
         (shape((48, 8, 128), BF16), shape((4, 8, 16, 384), F32)),
         (VMEM, pl.BlockSpec((4, 1, 16, 384), lambda i: (0, 0, 0, 0))),
         [pltpu.VMEM((416, 128), F32)],
         grid=(1,),
-        input_output_aliases={8: 1},
-    )(done, land_mask, back, back_cross, back_inner, heat, depth_levels, top, step.reshape(4, 8, 16, 384))
+        input_output_aliases={7: 1},
+    )(done, back, back_cross, back_inner, heat, gain, top, step.reshape(4, 8, 16, 384))
     return (new_tracers, ocean_flux)
 
 

time: 77.8 us -> 77.8 us (level)
  no operation moved by 1% of the time
where the time goes in v8:
time: 77.8 us; the launch traced here: 76.9 us
  starting transfers between devices  46.3 us (60%)
  waiting for transfers between devices  17.4 us (22%)
  Pallas kernels  10.9 us (14%)
  local copies, waits for them, and re-layouts  1.38 us (2%)
  between operations  0.81 us (1%)
    all_to_all x2, starting transfers between devices, turn(): return lax.all_to_all(values, 'lon', 0, 0, tiled=True).reshape(flat)  20 us
    ppermute x1, starting transfers between devices, shards(): cross = lax.ppermute(cross, 'lat', cross_pairs)  9.14 us
    all_to_all x2, waiting for transfers between devices, turn(): return lax.all_to_all(values, 'lon', 0, 0, tiled=True).reshape(flat)  9.1 us
    all_to_all x1, starting transfers between devices, shards(): heat = lax.all_to_all(heat, 'lat', 0, 0, tiled=True)  6.7 us
    ppermute x1, starting transfers between devices, shards(): back_cross = lax.ppermute(back_cross, 'lat', cross_pairs)  6.55 us
    pallas_call x1, Pallas kernels, shards(): call(functools.partial(stencil_kernel, lats), 'stencil', [SMEM] + [VMEM]...  3.65 us
    ppermute x1, waiting for transfers between devices, shards(): inner = lax.ppermute(inner, 'lat', inner_pairs)  2.91 us
    ppermute x1, waiting for transfers between devices, shards(): back_inner = lax.ppermute(back_inner, 'lat', inner_pairs)  2.83 us
  transfers between devices with their start and end apart: 7, of which 7 were waited for; matrix products, arithmetic and copies ran while one was open for 0% of the time, Pallas kernels for 5%

profile of v8, /device:TPU:1, one launch (start us, length us, event | category | flops | bytes accessed | tf_op | source)
XLA Modules:
  0.0 76.9 jit_solution(8707423698911875691)
XLA Ops:
  0.6 0.0 copy-start
  0.6 2.3 %pack.1 = (bf16[160,8,128]{2,1,0:T(8,128)(2,1)}, s32[48]{0:T(128)}) custom-call(s32[48]{0:T(128)} %dest_hbm.1, s32[48]{0:T(128)} %land_ref.3, bf16[48,8,128]{2,1,0:T(8,128)(2,1)} %state_hbm.1, f32[32,16,384]{2,1,0:T(8,128)} %bitcast.6, f32[8,16,384]{2,1,0:T(8,128)} %east_ref.1, f32[8,16,384]{2,1,0:T(8,128)} %kappa_ref.3, s32[16,384]{1,0:T(8,128)} %depth_ref.3), custom_call_target="tpu_custom_call" | custom-call | tf_op jit(solution)/shard_map/pack/pallas_call | solution.py:416
  3.0 0.0 copy-start.1
  3.0 0.0 copy-start.3
  3.0 0.0 copy-start.4
  3.0 14.0 %all-to-all-start = ((bf16[8,20,8,128]{3,2,1,0:T(8,128)(2,1)}), bf16[8,20,8,128]{3,2,1,0:T(8,128)(2,1)S(1)}, u32[]{:S(2)}, u32[]{:S(2)}) async-start(bf16[8,20,8,128]{3,2,1,0:T(8,128)(2,1)} %bitcast.15), calls=%async_computation | async-start | bytes 655360 | tf_op jit(solution)/shard_map/all_to_all | solution.py:412
  17.0 0.0 copy-start.12
  17.0 0.0 copy-start.13
  17.0 0.7 copy-done.12
  17.7 0.0 copy-done.13
  17.7 0.2 convert_reduce_fusion
  17.8 0.0 copy-start.9
  17.9 6.3 %all-to-all-done = bf16[8,20,8,128]{3,2,1,0:T(8,128)(2,1)S(1)} async-done(((bf16[8,20,8,128]{3,2,1,0:T(8,128)(2,1)}), bf16[8,20,8,128]{3,2,1,0:T(8,128)(2,1)S(1)}, u32[]{:S(2)}, u32[]{:S(2)}) %all-to-all-start) | async-done | bytes 327712 | tf_op jit(solution)/shard_map/all_to_all | solution.py:412
  24.1 0.0 copy-done
  24.1 0.0 copy-done.1
  24.1 0.0 copy-done.3
  24.1 0.0 copy-done.4
  24.2 0.0 copy-done.9
  24.2 0.0 copy-start.6
  24.2 0.0 copy-start.7
  24.2 0.0 copy-start.8
  24.2 0.7 rows.1
  24.9 0.0 copy-start.10
  24.9 9.1 %collective-permute-start = (bf16[69,8,128]{2,1,0:T(8,128)(2,1)S(1)}, bf16[69,8,128]{2,1,0:T(8,128)(2,1)S(1)}, u32[]{:S(2)}, u32[]{:S(2)}) collective-permute-start(bf16[69,8,128]{2,1,0:T(8,128)(2,1)S(1)} %get-tuple-element.16), channel_id=1, source_target_pairs={{0,760},{760,0},{16,8},{8,16},{32,24},{24,32},{48,40},{40,48},{64,... | collective-permute-start | bytes 423944 | tf_op jit(solution)/shard_map/ppermute | solution.py:458
  34.1 1.9 %collective-permute-start.1 = (bf16[69,8,128]{2,1,0:T(8,128)(2,1)S(1)}, bf16[69,8,128]{2,1,0:T(8,128)(2,1)S(1)}, u32[]{:S(2)}, u32[]{:S(2)}) collective-permute-start(bf16[69,8,128]{2,1,0:T(8,128)(2,1)S(1)} %get-tuple-element.17), channel_id=1, source_target_pairs={{0,8},{8,0},{16,24},{24,16},{32,40},{40,32},{48,56},{56,48},{64,72... | collective-permute-start | bytes 423944 | tf_op jit(solution)/shard_map/ppermute | solution.py:459
  36.0 1.0 %collective-permute-done.cross_ref.cross_halo_ref = bf16[69,8,128]{2,1,0:T(8,128)(2,1)S(1)} collective-permute-done((bf16[69,8,128]{2,1,0:T(8,128)(2,1)S(1)}, bf16[69,8,128]{2,1,0:T(8,128)(2,1)S(1)}, u32[]{:S(2)}, u32[]{:S(2)}) %collective-permute-start) | collective-permute-done | bytes 141344 | tf_op jit(solution)/shard_map/ppermute | solution.py:458
  37.0 2.9 %collective-permute-done.1.inner_ref.inner_halo_ref = bf16[69,8,128]{2,1,0:T(8,128)(2,1)S(1)} collective-permute-done((bf16[69,8,128]{2,1,0:T(8,128)(2,1)S(1)}, bf16[69,8,128]{2,1,0:T(8,128)(2,1)S(1)}, u32[]{:S(2)}, u32[]{:S(2)}) %collective-permute-start.1) | collective-permute-done | bytes 141344 | tf_op jit(solution)/shard_map/ppermute | solution.py:459
  39.9 0.0 copy-done.6
  39.9 0.0 copy-done.7
  39.9 0.0 copy-done.8
  39.9 0.0 copy-done.10
  39.9 2.0 %couple.1.after_ref = bf16[160,8,128]{2,1,0:T(8,128)(2,1)} custom-call(s32[48]{0:T(128)S(1)} %fusion.2.place_ref, bf16[160,8,128]{2,1,0:T(8,128)(2,1)S(1)} %bitcast.10, bf16[69,8,128]{2,1,0:T(8,128)(2,1)S(1)} %collective-permute-done.cross_ref.cross_halo_ref, bf16[69,8,128]{2,1,0:T(8,128)(2,1)S(1)} %collective-permute-done.1.inner_ref.inner_halo_ref, ...), custom_call_target="tpu_custom_call" | custom-call | tf_op jit(solution)/shard_map/couple/pallas_call | solution.py:461
  41.9 0.0 copy-start.5
  41.9 6.0 %all-to-all-start.1 = ((bf16[8,20,8,128]{3,2,1,0:T(8,128)(2,1)}), bf16[8,20,8,128]{3,2,1,0:T(8,128)(2,1)S(1)}, u32[]{:S(2)}, u32[]{:S(2)}) async-start(bf16[8,20,8,128]{3,2,1,0:T(8,128)(2,1)} %bitcast.3), calls=%async_computation.1 | async-start | bytes 655360 | tf_op jit(solution)/shard_map/all_to_all | solution.py:412
  47.9 0.0 copy-start.11
  47.9 0.0 copy-done.2
  47.9 0.0 copy-done.5
  47.9 0.6 copy-done.11
  48.6 3.7 %stencil.1 = (f32[32,16,384]{2,1,0:T(8,128)}, f32[4,16,384]{2,1,0:T(8,128)S(1)}, f32[16,384]{1,0:T(8,128)S(1)}, s32[48]{0:T(128)S(1)}) custom-call(s32[48]{0:T(128)S(1)} %copy-done.9, bf16[160,8,128]{2,1,0:T(8,128)(2,1)S(1)} %bitcast.11, bf16[69,8,128]{2,1,0:T(8,128)(2,1)S(1)} %collective-permute-done.cross_ref.cross_halo_ref, ...), custom_call_target="tpu_custom_call" | custom-call | flops 8000000 | bytes 3000000 | tf_op jit(solution)/shard_map/stencil/pallas_call | solution.py:471
  52.2 2.8 %all-to-all-done.1 = bf16[8,20,8,128]{3,2,1,0:T(8,128)(2,1)S(1)} async-done(((bf16[8,20,8,128]{3,2,1,0:T(8,128)(2,1)}), bf16[8,20,8,128]{3,2,1,0:T(8,128)(2,1)S(1)}, u32[]{:S(2)}, u32[]{:S(2)}) %all-to-all-start.1) | async-done | bytes 327712 | tf_op jit(solution)/shard_map/all_to_all | solution.py:412
  55.1 0.7 split.1
  55.7 6.7 %all-to-all-start.2 = ((f32[96,1,128]{2,1,0:T(1,128)}), f32[96,1,128]{2,1,0:T(1,128)S(1)}, u32[]{:S(2)}, u32[]{:S(2)}) async-start(f32[96,1,128]{2,1,0:T(1,128)} %get-tuple-element.22), calls=%async_computation.2 | async-start | bytes 98304 | tf_op jit(solution)/shard_map/all_to_all | solution.py:501
  62.4 6.6 %collective-permute-start.2 = (bf16[48,8,128]{2,1,0:T(8,128)(2,1)S(1)}, bf16[48,8,128]{2,1,0:T(8,128)(2,1)S(1)}, u32[]{:S(2)}, u32[]{:S(2)}) collective-permute-start(bf16[48,8,128]{2,1,0:T(8,128)(2,1)S(1)} %get-tuple-element.20), channel_id=1, source_target_pairs={{0,760},{760,0},{16,8},{8,16},{32,24},{24,32},{48,40},{40,48},{64,... | collective-permute-start | bytes 294920 | tf_op jit(solution)/shard_map/ppermute | solution.py:502
  69.0 1.9 %collective-permute-start.3 = (bf16[48,8,128]{2,1,0:T(8,128)(2,1)S(1)}, bf16[48,8,128]{2,1,0:T(8,128)(2,1)S(1)}, u32[]{:S(2)}, u32[]{:S(2)}) collective-permute-start(bf16[48,8,128]{2,1,0:T(8,128)(2,1)S(1)} %get-tuple-element.21), channel_id=1, source_target_pairs={{0,8},{8,0},{16,24},{24,16},{32,40},{40,32},{48,56},{56,48},{64,72... | collective-permute-start | bytes 294920 | tf_op jit(solution)/shard_map/ppermute | solution.py:503
  70.9 0.9 %collective-permute-done.2.cross_ref = bf16[48,8,128]{2,1,0:T(8,128)(2,1)S(1)} collective-permute-done((bf16[48,8,128]{2,1,0:T(8,128)(2,1)S(1)}, bf16[48,8,128]{2,1,0:T(8,128)(2,1)S(1)}, u32[]{:S(2)}, u32[]{:S(2)}) %collective-permute-start.2) | collective-permute-done | bytes 98336 | tf_op jit(solution)/shard_map/ppermute | solution.py:502
  71.9 2.8 %collective-permute-done.3.inner_ref = bf16[48,8,128]{2,1,0:T(8,128)(2,1)S(1)} collective-permute-done((bf16[48,8,128]{2,1,0:T(8,128)(2,1)S(1)}, bf16[48,8,128]{2,1,0:T(8,128)(2,1)S(1)}, u32[]{:S(2)}, u32[]{:S(2)}) %collective-permute-start.3) | collective-permute-done | bytes 98336 | tf_op jit(solution)/shard_map/ppermute | solution.py:503
  74.7 0.7 all-to-all-done.2.heat_ref
  75.3 1.5 %finish.1 = (bf16[48,8,128]{2,1,0:T(8,128)(2,1)}, f32[4,8,16,384]{3,2,1,0:T(8,128)}) custom-call(s32[48]{0:T(128)S(1)} %get-tuple-element.19.done_ref.code_ref, bf16[160,8,128]{2,1,0:T(8,128)(2,1)S(1)} %bitcast.13, bf16[48,8,128]{2,1,0:T(8,128)(2,1)S(1)} %collective-permute-done.2.cross_ref, ...), custom_call_target="tpu_custom_call", output_to_operand_aliasing={{1}: (7, {})} | custom-call | tf_op jit(solution)/shard_map/finish/pallas_call | solution.py:506
  (2 shorter events, 0.0 us)
Async XLA Ops:
  0.6 23.5 %copy-start = (f32[4,8,16,384]{3,2,1,0:T(8,128)S(1)}, f32[4,8,16,384]{3,2,1,0:T(8,128)}, u32[]{:S(2)}) copy-start(f32[4,8,16,384]{3,2,1,0:T(8,128)} %param.16) | copy-start | bytes 2359300
  3.0 21.2 %copy-start.1 = (f32[8,16,384]{2,1,0:T(8,128)S(1)}, f32[8,16,384]{2,1,0:T(8,128)}, u32[]{:S(2)}) copy-start(f32[8,16,384]{2,1,0:T(8,128)} %kappa_ref.3) | copy-start | bytes 589828
  3.0 21.2 %copy-start.3 = (f32[8,16,384]{2,1,0:T(8,128)S(1)}, f32[8,16,384]{2,1,0:T(8,128)}, u32[]{:S(2)}) copy-start(f32[8,16,384]{2,1,0:T(8,128)} %north_ref.3) | copy-start | bytes 589828
  3.0 21.2 %copy-start.4 = (s32[16,384]{1,0:T(8,128)S(1)}, s32[16,384]{1,0:T(8,128)}, u32[]{:S(2)}) copy-start(s32[16,384]{1,0:T(8,128)} %depth_ref.3) | copy-start | bytes 73732
  3.0 21.1 %all-to-all-start = ((bf16[8,20,8,128]{3,2,1,0:T(8,128)(2,1)}), bf16[8,20,8,128]{3,2,1,0:T(8,128)(2,1)S(1)}, u32[]{:S(2)}, u32[]{:S(2)}) async-start(bf16[8,20,8,128]{3,2,1,0:T(8,128)(2,1)} %bitcast.15), calls=%async_computation | async-start | bytes 655360 | tf_op jit(solution)/shard_map/all_to_all | solution.py:412
  17.0 0.7 copy-start.12
  17.0 0.7 copy-start.13
  17.8 6.3 %copy-start.9 = (s32[48]{0:T(128)S(1)}, s32[48]{0:T(128)}, u32[]{:S(2)}) copy-start(s32[48]{0:T(128)} %land_ref.3) | copy-start | bytes 580
  24.2 15.7 %copy-start.6 = (f32[48,8,128]{2,1,0:T(8,128)S(1)}, f32[48,8,128]{2,1,0:T(8,128)}, u32[]{:S(2)}) copy-start(f32[48,8,128]{2,1,0:T(8,128)} %atm_ref.1) | copy-start | bytes 589828
  24.2 15.7 %copy-start.7 = (f32[48,128]{1,0:T(8,128)S(1)}, f32[48,128]{1,0:T(8,128)}, u32[]{:S(2)}) copy-start(f32[48,128]{1,0:T(8,128)} %coef_ref.1) | copy-start | bytes 73732
  24.2 15.7 %copy-start.8 = (f32[48,128]{1,0:T(8,128)S(1)}, f32[48,128]{1,0:T(8,128)}, u32[]{:S(2)}) copy-start(f32[48,128]{1,0:T(8,128)} %sun_ref.1) | copy-start | bytes 73732
  24.9 15.0 %copy-start.10 = (f32[8,8]{1,0:T(8,128)S(1)}, f32[8,8]{1,0:T(8,128)}, u32[]{:S(2)}) copy-start(f32[8,8]{1,0:T(8,128)} %mixing_ref.1) | copy-start | bytes 772
  24.9 12.1 %collective-permute-start = (bf16[69,8,128]{2,1,0:T(8,128)(2,1)S(1)}, bf16[69,8,128]{2,1,0:T(8,128)(2,1)S(1)}, u32[]{:S(2)}, u32[]{:S(2)}) collective-permute-start(bf16[69,8,128]{2,1,0:T(8,128)(2,1)S(1)} %get-tuple-element.16), channel_id=1, source_target_pairs={{0,760},{760,0},{16,8},{8,16},{32,24},{24,32},{48,40},{40,48},{64,... | collective-permute-start | bytes 423944 | tf_op jit(solution)/shard_map/ppermute | solution.py:458
  34.1 5.8 %collective-permute-start.1 = (bf16[69,8,128]{2,1,0:T(8,128)(2,1)S(1)}, bf16[69,8,128]{2,1,0:T(8,128)(2,1)S(1)}, u32[]{:S(2)}, u32[]{:S(2)}) collective-permute-start(bf16[69,8,128]{2,1,0:T(8,128)(2,1)S(1)} %get-tuple-element.17), channel_id=1, source_target_pairs={{0,8},{8,0},{16,24},{24,16},{32,40},{40,32},{48,56},{56,48},{64,72... | collective-permute-start | bytes 423944 | tf_op jit(solution)/shard_map/ppermute | solution.py:459
  41.9 6.0 %copy-start.2 = (f32[8,16,384]{2,1,0:T(8,128)S(1)}, f32[8,16,384]{2,1,0:T(8,128)}, u32[]{:S(2)}) copy-start(f32[8,16,384]{2,1,0:T(8,128)} %east_ref.1) | copy-start | bytes 589828
  41.9 6.0 %copy-start.5 = (f32[8,16,384]{2,1,0:T(8,128)S(1)}, f32[8,16,384]{2,1,0:T(8,128)}, u32[]{:S(2)}) copy-start(f32[8,16,384]{2,1,0:T(8,128)} %cross_ref.1) | copy-start | bytes 589828
  41.9 13.2 %all-to-all-start.1 = ((bf16[8,20,8,128]{3,2,1,0:T(8,128)(2,1)}), bf16[8,20,8,128]{3,2,1,0:T(8,128)(2,1)S(1)}, u32[]{:S(2)}, u32[]{:S(2)}) async-start(bf16[8,20,8,128]{3,2,1,0:T(8,128)(2,1)} %bitcast.3), calls=%async_computation.1 | async-start | bytes 655360 | tf_op jit(solution)/shard_map/all_to_all | solution.py:412
  47.9 0.7 copy-start.11
  55.7 19.6 %all-to-all-start.2 = ((f32[96,1,128]{2,1,0:T(1,128)}), f32[96,1,128]{2,1,0:T(1,128)S(1)}, u32[]{:S(2)}, u32[]{:S(2)}) async-start(f32[96,1,128]{2,1,0:T(1,128)} %get-tuple-element.22), calls=%async_computation.2 | async-start | bytes 98304 | tf_op jit(solution)/shard_map/all_to_all | solution.py:501
  62.4 9.4 %collective-permute-start.2 = (bf16[48,8,128]{2,1,0:T(8,128)(2,1)S(1)}, bf16[48,8,128]{2,1,0:T(8,128)(2,1)S(1)}, u32[]{:S(2)}, u32[]{:S(2)}) collective-permute-start(bf16[48,8,128]{2,1,0:T(8,128)(2,1)S(1)} %get-tuple-element.20), channel_id=1, source_target_pairs={{0,760},{760,0},{16,8},{8,16},{32,24},{24,32},{48,40},{40,48},{64,... | collective-permute-start | bytes 294920 | tf_op jit(solution)/shard_map/ppermute | solution.py:502
  69.0 5.7 %collective-permute-start.3 = (bf16[48,8,128]{2,1,0:T(8,128)(2,1)S(1)}, bf16[48,8,128]{2,1,0:T(8,128)(2,1)S(1)}, u32[]{:S(2)}, u32[]{:S(2)}) collective-permute-start(bf16[48,8,128]{2,1,0:T(8,128)(2,1)S(1)} %get-tuple-element.21), channel_id=1, source_target_pairs={{0,8},{8,0},{16,24},{24,16},{32,40},{40,32},{48,56},{56,48},{64,72... | collective-permute-start | bytes 294920 | tf_op jit(solution)/shard_map/ppermute | solution.py:503
